TPU v7x, 256 devices: a whole 4x4x8 slice. The times are simulated.
256 devices in a mesh: mpo: 4 (over y), tensor: 64 (over x, z, core).
Axes of the slice: x: 4, y: 4, z: 8, core: 2. Of those that a mesh axis runs over, the one named last changes fastest.
Arguments:
- wavefunction: float32 [4096, 128, 128], P('tensor'), may hold values from -6 to 6
- left_env: float32 [16, 64, 128, 128], P('mpo', 'tensor'), may hold values from -0.5 to 0.5
- right_env: float32 [16, 64, 128, 128], P('mpo', 'tensor'), may hold values from -0.5 to 0.5
- mpo_values: float32 [16, 16], P('mpo'), may hold values from -4 to 4
- mpo_pattern: int32 [16, 16], P('mpo'), may hold values 0 or 1
- physical: int32 [4096], P('tensor'), may hold values from 0 to 15
- right_sector: int32 [4096, 1], P('tensor'), may hold values from 0 to 63; in each aligned block of 64 rows (0 to 63, 64 to 127, ...) no two rows name the same one
- sector_size: int32 [64], P('tensor'), may hold values from 64 to 128, as said below
Outputs:
- product: float32 [4096, 128, 128], P('tensor', 'mpo')
Inputs may be any that keep to these rules, and one draw needn't show every extreme that they name: `right_sector`: among the 64 blocks of one left sector (aligned runs of blocks), no right sector appears more than 1 times. `sector_size`: some sector has exactly 128 live rows.
All inputs are finite; a program needn't handle non-finite values. No bound on the sum of `mpo_pattern` on one device may be relied on, other than what follows from the above.
Results may differ from a plain program's by a relative error of at most 0.0003.
Values sent between devices are 32-bit elements; how exact they have to be, the bound alone decides.
No kernel may reach another device: no remote copies, remote signals or barrier semaphores. Data moves between devices by JAX's collectives and lax.ppermute only.
A program may use at most 128 MiB of HBM per device.

v0:
```python
import jax
import jax.numpy as jnp
from jax import lax
from jax.sharding import PartitionSpec as P


def body(
    wavefunction, left_env, right_env, mpo_values, mpo_pattern, physical, right_sector, sector_size
):
    blocks, rows, _ = wavefunction.shape
    devices = lax.axis_size("tensor")
    quarters = lax.axis_size("mpo")
    capacity = (blocks + devices - 1) // devices
    all_sizes = lax.all_gather(sector_size, "tensor", axis=0, tiled=True)
    right_index = right_sector[:, 0]
    sectors = jnp.arange(all_sizes.shape[0], dtype=jnp.int32)
    right_rows = jnp.sum(
        jnp.where(right_index[:, None] == sectors[None, :], all_sizes[None, :], 0), axis=1
    )
    left_rows = sector_size[0]
    positions = jnp.arange(rows, dtype=jnp.int32)
    row_mask = (positions < left_rows).astype(jnp.float32)
    column_mask = (positions[None, :] < right_rows[:, None]).astype(jnp.float32)
    masked = wavefunction * row_mask[None, :, None] * column_mask[:, None, :]
    states = jnp.arange(mpo_values.shape[1], dtype=jnp.int32)
    one_hot = (physical[:, None] == states[None, :]).astype(jnp.float32)
    weights = mpo_values * mpo_pattern.astype(jnp.float32)
    coef = jnp.dot(weights, one_hot.T, precision=lax.Precision.HIGHEST)
    left_part = jnp.einsum("wab,kbc->kwac", left_env[:, 0], masked, precision=lax.Precision.HIGHEST)
    left_part = left_part * coef.T[:, :, None, None]
    right_own = right_env[:, 0]
    same_sector = right_index[:, None] == right_index[None, :]
    earlier = jnp.arange(blocks)[None, :] < jnp.arange(blocks)[:, None]
    slot_index = jnp.sum((same_sector & earlier).astype(jnp.int32), axis=1)
    outgoing = jnp.zeros((devices, capacity) + left_part.shape[1:], jnp.float32)
    outgoing = outgoing.at[right_index, slot_index].set(left_part)
    gathered = jnp.einsum(
        "smwac,wdc->smad",
        lax.all_to_all(outgoing, "tensor", split_axis=0, concat_axis=0, tiled=True),
        right_own,
        precision=lax.Precision.HIGHEST,
    )
    returned = lax.all_to_all(gathered, "tensor", split_axis=0, concat_axis=0, tiled=True)
    partial_sum = returned[right_index, slot_index]
    total = lax.psum_scatter(partial_sum, "mpo", scatter_dimension=1, tiled=True)
    share = rows // quarters
    own_rows = lax.axis_index("mpo") * share + jnp.arange(share, dtype=jnp.int32)
    own_mask = (own_rows < left_rows).astype(jnp.float32)
    return total * own_mask[None, :, None] * column_mask[:, None, :]


def solution(mesh):
    in_specs = (
        P("tensor", None, None),
        P("mpo", "tensor", None, None),
        P("mpo", "tensor", None, None),
        P("mpo", None),
        P("mpo", None),
        P("tensor"),
        P("tensor", None),
        P("tensor"),
    )
    out_specs = P("tensor", "mpo", None)
    return jax.shard_map(body, mesh=mesh, in_specs=in_specs, out_specs=out_specs, check_vma=False)
```

profile of v0, /device:TPU:1, one launch (start us, length us, event | category | flops | bytes accessed | tf_op | source)
XLA Modules:
  0.0 659.7 jit_solution(6247953395766872241)
XLA Ops:
  6.5 0.0 copy-start
  6.5 0.0 reduce-scatter.2.cloned.1.call-start
  7.3 1.3 dynamic-slice
  8.6 0.8 dynamic-update-slice
  9.4 20.7 %all-reduce = s32[64]{0:T(128)S(1)} all-reduce(s32[64]{0:T(128)S(1)} %dynamic-update-slice), channel_id=1, replica_groups=mesh['mpo'=4,'tensor'=64] {'tensor'}, use_global_device_ids=true, to_apply=%add | all-reduce | flops 64 | bytes 512
  30.1 0.9 select_reduce_fusion
  31.0 0.7 or_bitcast_fusion
  31.7 0.1 fusion.13
  31.8 0.9 fusion.14
  32.7 0.0 copy-done
  32.7 19.5 %multiply_bitcast_fusion = f32[64,4,128,128]{2,3,1,0:T(8,128)} fusion(f32[64,4]{1,0:T(8,128)S(1)} %fusion.14, f32[64,128,128]{2,1,0:T(8,128)} %param.8, f32[64,128]{1,0:T(8,128)S(1)} %fusion.13, f32[128]{0:T(128)S(1)} %compare_convert_fusion.1, f32[4,1,128,128]{3,2,1,0:T(8,128)S(1)} %copy-done), kind=kOutput, calls=%fused_computation.4 | convolution fusion | flops 6448742400 | bytes 21267968 | tf_op jit(solution)/shard_map/wab,kbc->kwac/dot_general | solution.py:29
  52.2 17.5 %copy.19 = f32[64,4,128,128]{3,2,1,0:T(8,128)} copy(f32[64,4,128,128]{2,3,1,0:T(8,128)} %multiply_bitcast_fusion) | data formatting | bytes 33554432 | tf_op jit(solution)/shard_map/mul | solution.py:30
  69.6 7.8 %broadcast.68 = f32[64,4,128,128]{3,2,1,0:T(8,128)} broadcast(f32[]{:T(128)} %constant.7.clone.1), dimensions={} | broadcast | bytes 16777220 | tf_op jit(solution)/shard_map/broadcast_in_dim | solution.py:35
  77.5 30.3 %scatter_fusion = f32[64,4,128,128]{3,2,1,0:T(8,128)} fusion(f32[64,4,128,128]{3,2,1,0:T(8,128)} %broadcast.68, s32[64]{0:T(128)S(1)} %get-tuple-element.8, f32[64,4,128,128]{3,2,1,0:T(8,128)} %copy.19), kind=kCustom, calls=%fused_computation.1 | custom fusion | bytes 50331904 | tf_op jit(solution)/shard_map/scatter | solution.py:36
  107.7 0.0 copy-start.2
  107.7 375.1 %all_to_all.10 = f32[64,1,4,128,128]{4,3,2,1,0:T(8,128)S(1)} all-to-all(f32[64,1,4,128,128]{4,3,2,1,0:T(8,128)} %bitcast.45), channel_id=1, replica_groups=mesh['mpo'=4,'tensor'=64] {'tensor'}, dimensions={0} | all-to-all | bytes 33554432 | tf_op jit(solution)/shard_map/all_to_all | solution.py:39
  482.8 0.0 copy-done.2
  482.8 0.0 copy-start.1
  482.8 14.6 %fusion.5 = f32[64,1,128,128]{3,2,1,0:T(8,128)S(1)} fusion(f32[64,1,4,128,128]{4,3,2,1,0:T(8,128)S(1)} %all_to_all.10, f32[4,1,128,128]{3,2,1,0:T(8,128)S(1)} %copy-done.2), kind=kOutput, calls=%fused_computation.8 | convolution fusion | flops 6442450944 | bytes 21233664 | tf_op jit(solution)/shard_map/smwac,wdc->smad/dot_general | solution.py:37
  497.3 101.9 %all_to_all.11 = f32[64,1,128,128]{3,2,1,0:T(8,128)} all-to-all(f32[64,1,128,128]{3,2,1,0:T(8,128)S(1)} %fusion.5), channel_id=1, replica_groups=mesh['mpo'=4,'tensor'=64] {'tensor'}, dimensions={0} | all-to-all | bytes 8388608 | tf_op jit(solution)/shard_map/all_to_all | solution.py:43
  599.3 4.9 gather_fusion
  604.2 0.0 reduce-scatter.2.cloned.1.call-update
  604.2 46.2 %reduce-scatter.2.cloned.1.call-done = f32[64,32,128]{2,1,0:T(8,128)} async-done(((f32[64,128,128]{2,1,0:T(8,128)}), f32[64,32,128]{2,1,0:T(8,128)}) %reduce-scatter.2.cloned.1.call-update) | async-done | bytes 1048592 | tf_op jit(solution)/shard_map/reduce_scatter | solution.py:45
  650.5 2.4 multiply_multiply_fusion
  652.9 0.0 copy-done.1
  (3 shorter events, 0.0 us)
Async XLA Ops:
  6.5 26.1 %copy-start = (f32[4,1,128,128]{3,2,1,0:T(8,128)S(1)}, f32[4,1,128,128]{3,2,1,0:T(8,128)}, u32[]{:S(2)}) copy-start(f32[4,1,128,128]{3,2,1,0:T(8,128)} %param.9) | copy-start | bytes 786436
  6.5 643.9 %reduce-scatter.2.cloned.1.call-start = ((), (), s32[]{:S(2)}) async-start(), calls=%async_computation.3 | async-start | bytes 5242880 | tf_op jit(solution)/shard_map/reduce_scatter | solution.py:45
  107.7 375.1 %copy-start.2 = (f32[4,1,128,128]{3,2,1,0:T(8,128)S(1)}, f32[4,1,128,128]{3,2,1,0:T(8,128)}, u32[]{:S(2)}) copy-start(f32[4,1,128,128]{3,2,1,0:T(8,128)} %param.10) | copy-start | bytes 786436
  482.8 170.1 %copy-start.1 = (f32[4,1,128,128]{3,2,1,0:T(8,128)S(1)}, f32[4,1,128,128]{3,2,1,0:T(8,128)}, u32[]{:S(2)}) copy-start(f32[4,1,128,128]{3,2,1,0:T(8,128)} %param.9) | copy-start | bytes 786436
Sparse Core Ops, SparseCore 0:
  604.3 46.0 reduce-scatter.1
where the time goes:
time: 660 us
  blocking collectives  498 us (75%)
  local copies, waits for them, and re-layouts  62.6 us (9%)
  waiting for transfers between devices  46.3 us (7%)
  matrix products  34.9 us (5%)
  between operations  14.2 us (2%)
    all_to_all x1, blocking collectives, body(): lax.all_to_all(outgoing, 'tensor', split_axis=0, concat_axis=0, tiled=True)  375 us
    all_to_all x1, blocking collectives, body(): lax.all_to_all(gathered, 'tensor', split_axis=0, concat_axis=0, tiled=True)  102 us
    reduce_scatter x1, waiting for transfers between devices, body(): lax.psum_scatter(partial_sum, 'mpo', scatter_dimension=1, tiled=True)  46.2 us
    scatter x1, local copies, waits for them, and re-layouts, body(): outgoing = outgoing.at[right_index, slot_index].set(left_part)  30.3 us
    unnamed x1, blocking collectives  20.7 us
    dot_general x1, matrix products, body(): jnp.einsum('wab,kbc->kwac', left_env[:, 0], masked, precision=lax.Precisi...  19.5 us
    mul x1, local copies, waits for them, and re-layouts, body(): left_part = left_part * coef.T[:, :, None, None]  17.5 us
    dot_general x1, matrix products, body(): jnp.einsum('smwac,wdc->smad', lax.all_to_all(outgoing, 'tensor', split_ax...  14.6 us
  transfers between devices with their start and end apart: 1, of which 1 were waited for; matrix products, arithmetic and copies ran while one was open for 0% of the time, Pallas kernels for 0%

commit v1 on v0

v1 whole, which is shorter than its diff:
```python
import functools

import jax
import jax.numpy as jnp
from jax import lax
from jax.experimental import pallas as pl
from jax.experimental.pallas import tpu as pltpu
from jax.sharding import Mesh
from jax.sharding import PartitionSpec as P

NX, NZ, NC, NM = 4, 8, 2, 4
N = 128
TENSOR = ("x", "z", "c")

SYM = dict(
    own=(0, 0), zf1=(0, -1), zb1=(0, 1), zf2=(0, -2), zb2=(0, 2), zf3=(0, -3), zb3=(0, 3), z4=(0, 4),
    xf1=(-1, 0), xb1=(1, 0), x2=(2, 0), df1=(-1, 4), db1=(1, 4), d2=(2, 4),
)
ROW = (-1, 1, 2)
SET_P, SET_Q = (-1, 1, -2), (2, -3, 3)
TRIPLE = dict(
    m1f=([(d, -1) for d in ROW], [(-1, d) for d in SET_P]),
    m1b=([(d, 1) for d in ROW], [(1, d) for d in SET_P]),
    m2f=([(d, -2) for d in ROW], [(-1, d) for d in SET_Q]),
    m2b=([(d, 2) for d in ROW], [(1, d) for d in SET_Q]),
    m3f=([(d, -3) for d in ROW], [(-2, d) for d in SET_P]),
    m3b=([(d, 3) for d in ROW], [(2, d) for d in SET_Q]),
)
BATCHES = (
    ("own", "zf1", "zb1", "xf1", "xb1", "x2", "zf2", "zb2", "m1f", "m1b"),
    ("zf3", "zb3", "z4", "m2f", "m2b", "df1", "db1", "d2"),
    ("m3f", "m3b"),
)


def slots_of(names):
    slots = []
    for name in names:
        slots += [(SYM[name], SYM[name])] if name in SYM else list(zip(*TRIPLE[name]))
    return slots


def width(name):
    return 1 if name in SYM else 3


def sector(pos, core, slot):
    (x0, z0), (x1, z1) = slot
    first = core == 0
    x = (pos[1] + jnp.where(first, x0 % NX, x1 % NX)) % NX
    z = (pos[2] + jnp.where(first, z0 % NZ, z1 % NZ)) % NZ
    return (x * NZ + z) * NC + core


def invert(meta, inverse):
    def step(k, carry):
        inverse[meta[k]] = k
        return carry

    lax.fori_loop(0, NX * NZ * NC, step, 0)


def gather_kernel(meta, pos, blocks, out, inverse, sems):
    invert(meta, inverse)
    other = 1 - pos[3]
    half = NX * NZ

    def copy(j):
        return pltpu.make_async_copy(blocks.at[inverse[j * NC + other]], out.at[j], sems.at[j])

    lax.fori_loop(0, half, lambda j, c: (copy(j).start(), c)[1], 0)
    lax.fori_loop(0, half, lambda j, c: (copy(j).wait(), c)[1], 0)


def split(value):
    high = value.astype(jnp.bfloat16)
    return high, (value - high.astype(jnp.float32)).astype(jnp.bfloat16)


def dot_nt(a, b):
    return lax.dot_general(a, b, (((1,), (1,)), ((), ())), preferred_element_type=jnp.float32)


def work_kernel(names, pos, meta_own, meta_sib, values, pattern, left_own, left_sib, blocks, blocks_sib, *rest):
    count = len(names)
    arrays, rest = rest[:count], rest[count:]
    send_own, keep_own, send_sib, keep_sib = rest[:4]
    inv_own, inv_sib, sectors, right, wave, lefts, total, sem_r, sem_a, sem_b = rest[4:]
    slots = slots_of(names)
    n = len(slots)

    at = 0
    copies = []
    for name, array in zip(names, arrays):
        if width(name) == 1:
            copies.append(pltpu.make_async_copy(array, right.at[at], sem_r.at[at]))
        else:
            copies += [pltpu.make_async_copy(array.at[t], right.at[at + t], sem_r.at[at + t]) for t in range(3)]
        at += width(name)
    for copy in copies:
        copy.start()

    invert(meta_own, inv_own)
    invert(meta_sib, inv_sib)
    core = pos[3]
    for i, slot in enumerate(slots):
        sectors[i] = sector(pos, core, slot)

    def own_copy(i):
        return pltpu.make_async_copy(blocks.at[inv_own[sectors[i]]], wave.at[i, 0], sem_a.at[i])

    def sib_copy(i):
        return pltpu.make_async_copy(blocks_sib.at[sectors[i] // NC], wave.at[i, 1], sem_b.at[i])

    def start(i, carry):
        own_copy(i).start()
        sib_copy(i).start()
        return carry

    lax.fori_loop(0, n, start, 0)
    for side, ref in enumerate((left_own, left_sib)):
        for w in range(NM):
            high, low = split(ref[w])
            lefts[side, w * N:(w + 1) * N, :N] = high
            lefts[side, w * N:(w + 1) * N, N:] = low

    m = pos[0]
    zero = jnp.zeros((N, N), jnp.bfloat16)

    def step(i, carry):
        pltpu.make_async_copy(right.at[i], right.at[i], sem_r.at[i]).wait()
        own_copy(i).wait()
        sib_copy(i).wait()
        parts = []
        for side, (meta, inverse) in enumerate(((meta_own, inv_own), (meta_sib, inv_sib))):
            high, low = split(wave[i, side])
            weights = jnp.concatenate(
                [jnp.concatenate([high, low], 1), jnp.concatenate([high, zero], 1)], 0)
            both = jnp.dot(lefts[side], weights, preferred_element_type=jnp.float32)
            both = both[:, :N] + both[:, N:]
            state = meta[NX * NZ * NC + inverse[sectors[i]]]
            coef = [values[w, state] * pattern[w, state].astype(jnp.float32) for w in range(NM)]
            parts.append([split(both[w * N:(w + 1) * N] * coef[w]) for w in range(NM)])
        acc = None
        for w in range(0, NM, 2):
            high = jnp.concatenate([jnp.concatenate([parts[s][w][0], parts[s][w + 1][0]], 1) for s in range(2)], 0)
            low = jnp.concatenate([jnp.concatenate([parts[s][w][1], parts[s][w + 1][1]], 1) for s in range(2)], 0)
            r0, r1 = split(right[i, w]), split(right[i, w + 1])
            r_high = jnp.concatenate([r0[0], r1[0]], 1)
            r_low = jnp.concatenate([r0[1], r1[1]], 1)
            big = dot_nt(high, jnp.concatenate([r_high, r_low], 0))
            small = dot_nt(low, r_high)
            now = big[:, :N] + big[:, N:] + small
            acc = now if acc is None else acc + now
        total[...] = acc
        share = N // NM
        for side, (send, keep, near, far) in enumerate(((send_own, keep_own, 1, 3), (send_sib, keep_sib, 3, 1))):
            def rows(q):
                return total[pl.ds(pl.multiple_of(side * N + q * share, share), share), :]

            send[0, i] = rows(m ^ near)
            send[1, i] = rows(m ^ 2)
            keep[0, i] = rows(m)
            keep[1, i] = rows(m ^ far)
        return carry

    lax.fori_loop(0, n, step, 0)


def final_kernel(pos, meta, *rest):
    out, inverse = rest[-2:]
    invert(meta, inverse)
    core = pos[3]
    for b, names in enumerate(BATCHES):
        own0, own1, sib0, sib1 = rest[4 * b:4 * b + 4]
        for i, slot in enumerate(slots_of(names)):
            out[inverse[sector(pos, core, slot)]] = own0[i] + own1[i]
            out[inverse[sector(pos, 1 - core, slot)]] = sib0[i] + sib1[i]


SMEM = pl.BlockSpec(memory_space=pltpu.SMEM)
VMEM = pl.BlockSpec(memory_space=pltpu.VMEM)
ANY = pl.BlockSpec(memory_space=pl.ANY)


def gather_blocks(meta, pos, blocks):
    half = NX * NZ
    return pl.pallas_call(
        gather_kernel,
        out_shape=jax.ShapeDtypeStruct((half, N, N), jnp.float32),
        in_specs=[SMEM, SMEM, ANY],
        out_specs=ANY,
        scratch_shapes=[pltpu.SMEM((NX * NZ * NC,), jnp.int32), pltpu.SemaphoreType.DMA((half,))],
        cost_estimate=pl.CostEstimate(flops=0, bytes_accessed=half * N * N * 8, transcendentals=0),
        name="gather_blocks",
    )(meta, pos, blocks)


def work(names, pos, meta_own, meta_sib, values, pattern, left_own, left_sib, blocks, blocks_sib, arrays):
    n = sum(width(name) for name in names)
    piece = jax.ShapeDtypeStruct((2, n, N // NM, N), jnp.float32)
    return pl.pallas_call(
        functools.partial(work_kernel, names),
        out_shape=(piece,) * 4,
        in_specs=[SMEM] * 5 + [VMEM] * 2 + [ANY] * (2 + len(arrays)),
        out_specs=(VMEM,) * 4,
        scratch_shapes=[
            pltpu.SMEM((NX * NZ * NC,), jnp.int32),
            pltpu.SMEM((NX * NZ * NC,), jnp.int32),
            pltpu.SMEM((n,), jnp.int32),
            pltpu.VMEM((n, NM, N, N), jnp.float32),
            pltpu.VMEM((n, 2, N, N), jnp.float32),
            pltpu.VMEM((2, NM * N, 2 * N), jnp.bfloat16),
            pltpu.VMEM((2 * N, N), jnp.float32),
            pltpu.SemaphoreType.DMA((n,)),
            pltpu.SemaphoreType.DMA((n,)),
            pltpu.SemaphoreType.DMA((n,)),
        ],
        compiler_params=pltpu.CompilerParams(vmem_limit_bytes=24 * 2**20),
        cost_estimate=pl.CostEstimate(flops=n * 3 * 16 * 2 * N**3, bytes_accessed=n * 10 * N * N * 4, transcendentals=0),
        name="work",
    )(pos, meta_own, meta_sib, values, pattern, left_own, left_sib, blocks, blocks_sib, *arrays)


def finish(pos, meta, pieces):
    return pl.pallas_call(
        final_kernel,
        out_shape=jax.ShapeDtypeStruct((NX * NZ * NC, N // NM, N), jnp.float32),
        in_specs=[SMEM, SMEM] + [VMEM] * len(pieces),
        out_specs=VMEM,
        scratch_shapes=[pltpu.SMEM((NX * NZ * NC,), jnp.int32)],
        compiler_params=pltpu.CompilerParams(vmem_limit_bytes=16 * 2**20),
        name="finish",
    )(pos, meta, *pieces)


def shift(array, axis, step):
    size = {"x": NX, "z": NZ, "c": NC}[axis]
    return lax.ppermute(array, axis, [(i, (i + step) % size) for i in range(size)])


def place(x, z, c):
    return ((x % NX) * NZ + z % NZ) * NC + c


def by_core(array, step):
    pairs = []
    for x in range(NX):
        for z in range(NZ):
            pairs.append((place(x, z, 0), place(x, z + step, 0)))
            pairs.append((place(x, z, 1), place(x + step, z, 1)))
    return lax.ppermute(array, TENSOR, pairs)


def z_far(array):
    pairs = []
    for x in range(NX):
        for z in range(NZ):
            pairs.append((place(x, z, 0), place(x, z + 1, 0)))
            pairs.append((place(x, z, 1), place(x, z - 1, 1)))
    return lax.ppermute(array, TENSOR, pairs)


def body(wavefunction, left_env, right_env, mpo_values, mpo_pattern, physical, right_sector, sector_size):
    m, x, z, c = (lax.axis_index(a) for a in ("m", "x", "z", "c"))
    first = c == 0
    pos = jnp.stack([m, x, z, c]).astype(jnp.int32)
    live = jnp.arange(N, dtype=jnp.int32) < sector_size[0]
    mask = live[:, None] & live[None, :]
    own = jnp.where(mask, right_env[:, 0], 0.0)
    left = jnp.where(mask, left_env[:, 0], 0.0)
    meta = jnp.concatenate([right_sector[:, 0], physical])
    meta_sib = shift(meta, "c", 1)
    left_sib = shift(left, "c", 1)
    blocks_sib = shift(gather_blocks(meta, pos, wavefunction), "c", 1)

    got = dict(own=own)
    got["zf1"], got["zb1"] = shift(own, "z", 1), shift(own, "z", -1)
    got["xf1"], got["xb1"] = shift(own, "x", 1), shift(own, "x", -1)
    got["zf2"], got["zb2"] = shift(got["zf1"], "z", 1), shift(got["zb1"], "z", -1)
    got["x2"] = shift(got["xf1"], "x", 1)
    row = jnp.stack([got["xf1"], got["xb1"], got["x2"]])
    set_p = jnp.stack([got["zf1"], got["zb1"], got["zf2"]])
    m1 = jnp.where(first, row, set_p)
    got["m1f"], got["m1b"] = by_core(m1, 1), by_core(m1, -1)
    got["zf3"], got["zb3"] = shift(got["zf2"], "z", 1), shift(got["zb2"], "z", -1)
    set_q = jnp.stack([got["zb2"], got["zf3"], got["zb3"]])
    got["m2f"] = by_core(jnp.where(first, got["m1f"], set_q), 1)
    got["m2b"] = by_core(jnp.where(first, got["m1b"], set_q), -1)
    got["z4"] = z_far(jnp.where(first, got["zf3"], got["zb3"]))
    got["df1"], got["db1"] = shift(got["z4"], "x", 1), shift(got["z4"], "x", -1)
    got["d2"] = shift(got["db1"], "x", -1)
    got["m3f"] = by_core(jnp.where(first, got["m2f"], got["m1f"]), 1)
    got["m3b"] = by_core(got["m2b"], -1)

    near = [(i, i ^ 1) for i in range(NM)]
    far = [(i, i ^ 3) for i in range(NM)]
    straight = [(i * NC + c, i * NC + 1 - c) for i in range(NM) for c in range(NC)]
    across = [(i * NC + c, (i ^ 1) * NC + 1 - c) for i in range(NM) for c in range(NC)]
    pieces = []
    for names in BATCHES:
        send_own, keep_own, send_sib, keep_sib = work(
            names, pos, meta, meta_sib, mpo_values, mpo_pattern, left, left_sib, wavefunction, blocks_sib,
            [got[name] for name in names])
        sum_own = keep_own + lax.ppermute(send_own, "m", near)
        sum_sib = keep_sib + lax.ppermute(send_sib, "m", far)
        pieces += [
            sum_own[0],
            lax.ppermute(sum_own[1], "m", far),
            lax.ppermute(sum_sib[0], ("m", "c"), straight),
            lax.ppermute(sum_sib[1], ("m", "c"), across),
        ]
    return finish(pos, meta, pieces)


def solution(mesh):
    grid = Mesh(mesh.devices.reshape(NM, NX, NZ, NC), ("m", "x", "z", "c"))
    in_specs = (
        P(TENSOR, None, None),
        P("m", TENSOR, None, None),
        P("m", TENSOR, None, None),
        P("m", None),
        P("m", None),
        P(TENSOR),
        P(TENSOR, None),
        P(TENSOR),
    )
    out_specs = P(TENSOR, "m", None)
    return jax.shard_map(body, mesh=grid, in_specs=in_specs, out_specs=out_specs, check_vma=False)
```

time: 660 us -> 213 us (0.32)
  the two profiles are of different devices: /device:TPU:1 before, /device:TPU:32 now
where the time goes in v1:
time: 213 us
  Pallas kernels  98 us (46%)
  waiting for transfers between devices  70 us (33%)
  starting transfers between devices  38.5 us (18%)
  other arithmetic  5.56 us (3%)
    pallas_call x1, Pallas kernels, gather_blocks(): pl.pallas_call(gather_kernel, out_shape=jax.ShapeDtypeStruct((half, N, N)...  66.2 us
    ppermute x15, waiting for transfers between devices, shift(): lax.ppermute(array, axis, [(i, (i + step) % size) for i in range(size)])  42.8 us
    pallas_call x3, Pallas kernels, work(): pl.pallas_call(functools.partial(work_kernel, names), out_shape=(piece,)...  29.3 us
    ppermute x15, starting transfers between devices, shift(): lax.ppermute(array, axis, [(i, (i + step) % size) for i in range(size)])  16.4 us
    ppermute x3, waiting for transfers between devices, body(): sum_own = keep_own + lax.ppermute(send_own, 'm', near)  13.7 us
    ppermute x6, starting transfers between devices, by_core(): return lax.ppermute(array, TENSOR, pairs)  7.6 us
    ppermute x3, waiting for transfers between devices, body(): lax.ppermute(sum_own[1], 'm', far)  6.2 us
    ppermute x3, starting transfers between devices, body(): lax.ppermute(sum_own[1], 'm', far)  4.92 us
  transfers between devices with their start and end apart: 37, of which 14 were waited for; matrix products, arithmetic and copies ran while one was open for 2% of the time, Pallas kernels for 40%

profile of v1, /device:TPU:32, one launch (start us, length us, event | category | flops | bytes accessed | tf_op | source)
XLA Modules:
  0.0 213.2 jit_solution(5200233867293060586)
XLA Ops:
  0.8 1.8 bitcast_select_fusion
  2.5 1.5 collective-permute-start.5
  4.0 1.9 collective-permute-start.3
  6.0 1.7 collective-permute-start.6
  7.8 4.2 %collective-permute-done.5.rest_3_ = f32[4,128,128]{2,1,0:T(8,128)S(1)} collective-permute-done((f32[4,128,128]{2,1,0:T(8,128)}, f32[4,128,128]{2,1,0:T(8,128)S(1)}, u32[]{:S(2)}, u32[]{:S(2)}) %collective-permute-start.5) | collective-permute-done | bytes 262176 | tf_op jit(solution)/shard_map/ppermute | solution.py:239
  12.3 1.9 collective-permute-start.8
  14.2 1.3 pad_add_fusion.1.meta.meta_own
  16.1 66.2 %gather_blocks.1 = f32[32,128,128]{2,1,0:T(8,128)} custom-call(s32[128]{0:T(128)} %pad_add_fusion.1.meta.meta_own, s32[4]{0:T(128)} %pad_add_fusion.pos, f32[64,128,128]{2,1,0:T(8,128)} %blocks.7), custom_call_target="tpu_custom_call" | custom-call | bytes 4194304 | tf_op jit(solution)/shard_map/gather_blocks/pallas_call | solution.py:188
  83.7 2.5 %collective-permute-start.10 = (f32[3,4,128,128]{3,2,1,0:T(8,128)S(1)}, f32[3,4,128,128]{3,2,1,0:T(8,128)S(1)}, u32[]{:S(2)}, u32[]{:S(2)}) collective-permute-start(f32[3,4,128,128]{3,2,1,0:T(8,128)S(1)} %maximum_select_fusion), channel_id=1, source_target_pairs={{0,2},{1,17},{2,4},{3,19},{4,6},{5,21},{6,8},{7,23},{8,10},{9,25},... | collective-permute-start | bytes 2359304 | tf_op jit(solution)/shard_map/ppermute | solution.py:252
  86.1 3.0 %collective-permute-start.9 = (f32[4,128,128]{2,1,0:T(8,128)S(1)}, f32[4,128,128]{2,1,0:T(8,128)S(1)}, u32[]{:S(2)}, u32[]{:S(2)}) collective-permute-start(f32[4,128,128]{2,1,0:T(8,128)S(1)} %collective-permute-done.4.rest_2_), channel_id=1, source_target_pairs={{0,14},{2,0},{4,2},{6,4},{8,6},{10,8},{12,10},{14,12},{1,15},{3,1}... | collective-permute-start | bytes 786440 | tf_op jit(solution)/shard_map/ppermute | solution.py:239
  89.7 17.3 %collective-permute-done.9.rest_7_ = f32[4,128,128]{2,1,0:T(8,128)S(1)} collective-permute-done((f32[4,128,128]{2,1,0:T(8,128)S(1)}, f32[4,128,128]{2,1,0:T(8,128)S(1)}, u32[]{:S(2)}, u32[]{:S(2)}) %collective-permute-start.9) | collective-permute-done | bytes 262176 | tf_op jit(solution)/shard_map/ppermute | solution.py:239
  107.0 8.8 %collective-permute-done.18.rest_1_ = f32[4,128,128]{2,1,0:T(8,128)S(1)} collective-permute-done((f32[4,128,128]{2,1,0:T(8,128)S(1)}, f32[4,128,128]{2,1,0:T(8,128)S(1)}, u32[]{:S(2)}, u32[]{:S(2)}) %collective-permute-start.18) | collective-permute-done | bytes 262176 | tf_op jit(solution)/shard_map/ppermute | solution.py:239
  115.8 2.2 %collective-permute-start.19 = (f32[4,128,128]{2,1,0:T(8,128)S(1)}, f32[4,128,128]{2,1,0:T(8,128)S(1)}, u32[]{:S(2)}, u32[]{:S(2)}) collective-permute-start(f32[4,128,128]{2,1,0:T(8,128)S(1)} %broadcast_select_fusion.1), channel_id=1, source_target_pairs={{0,2},{1,15},{2,4},{3,1},{4,6},{5,3},{6,8},{7,5},{8,10},{9,7},{10,... | collective-permute-start | bytes 786440 | tf_op jit(solution)/shard_map/ppermute | solution.py:261
  118.2 3.0 %collective-permute-start.20 = (f32[3,4,128,128]{3,2,1,0:T(8,128)S(1)}, f32[3,4,128,128]{3,2,1,0:T(8,128)S(1)}, u32[]{:S(2)}, u32[]{:S(2)}) collective-permute-start(f32[3,4,128,128]{3,2,1,0:T(8,128)S(1)} %get-tuple-element.30), channel_id=1, source_target_pairs={{0,2},{1,17},{2,4},{3,19},{4,6},{5,21},{6,8},{7,23},{8,10},{9,25},... | collective-permute-start | bytes 2359304 | tf_op jit(solution)/shard_map/ppermute | solution.py:252
  122.6 1.5 collective-permute-start.23
  124.9 6.2 %collective-permute-done.23.rest_6_ = f32[4,128,128]{2,1,0:T(8,128)S(1)} collective-permute-done((f32[4,128,128]{2,1,0:T(8,128)S(1)}, f32[4,128,128]{2,1,0:T(8,128)S(1)}, u32[]{:S(2)}, u32[]{:S(2)}) %collective-permute-start.23) | collective-permute-done | bytes 262176 | tf_op jit(solution)/shard_map/ppermute | solution.py:239
  131.1 2.7 %collective-permute-start.24 = (f32[4,128,128]{2,1,0:T(8,128)S(1)}, f32[4,128,128]{2,1,0:T(8,128)S(1)}, u32[]{:S(2)}, u32[]{:S(2)}) collective-permute-start(f32[4,128,128]{2,1,0:T(8,128)S(1)} %collective-permute-done.23.rest_6_), channel_id=1, source_target_pairs={{0,48},{16,0},{32,16},{48,32},{1,49},{17,1},{33,17},{49,33},{2,50}... | collective-permute-start | bytes 786440 | tf_op jit(solution)/shard_map/ppermute | solution.py:239
  133.8 5.2 %collective-permute-done.24.rest_7_ = f32[4,128,128]{2,1,0:T(8,128)S(1)} collective-permute-done((f32[4,128,128]{2,1,0:T(8,128)S(1)}, f32[4,128,128]{2,1,0:T(8,128)S(1)}, u32[]{:S(2)}, u32[]{:S(2)}) %collective-permute-start.24) | collective-permute-done | bytes 262176 | tf_op jit(solution)/shard_map/ppermute | solution.py:239
  139.1 10.8 %work.4 = (f32[2,12,32,128]{3,2,1,0:T(8,128)S(1)}, f32[2,12,32,128]{3,2,1,0:T(8,128)S(1)}, f32[2,12,32,128]{3,2,1,0:T(8,128)S(1)}, f32[2,12,32,128]{3,2,1,0:T(8,128)S(1)}) custom-call(s32[4]{0:T(128)S(1)} %copy-done.3, s32[128]{0:T(128)S(1)} %copy-done.4, s32[128]{0:T(128)S(1)} %collective-permute-done.meta_sib, f32[4,16]{1,0:T(4,128)S(1)} %copy-done.1, ...), custom_call_target="tpu_custom_call" | custom-call | flops 2415919104 | bytes 7864320 | tf_op jit(solution)/shard_map/work/pallas_call | solution.py:202
  149.9 1.7 collective-permute-start.25
  151.6 2.2 %collective-permute-start.27 = (f32[2,12,32,128]{3,2,1,0:T(8,128)S(1)}, f32[2,12,32,128]{3,2,1,0:T(8,128)S(1)}, u32[]{:S(2)}, u32[]{:S(2)}) collective-permute-start(f32[2,12,32,128]{3,2,1,0:T(8,128)S(1)} %get-tuple-element.24), channel_id=1, source_target_pairs={{0,192},{64,128},{128,64},{192,0},{1,193},{65,129},{129,65},{193,1... | collective-permute-start | bytes 1179656 | tf_op jit(solution)/shard_map/ppermute | solution.py:306
  153.8 1.8 collective-permute-start.30
  155.9 12.2 %work.3 = (f32[2,14,32,128]{3,2,1,0:T(8,128)S(1)}, f32[2,14,32,128]{3,2,1,0:T(8,128)S(1)}, f32[2,14,32,128]{3,2,1,0:T(8,128)S(1)}, f32[2,14,32,128]{3,2,1,0:T(8,128)S(1)}) custom-call(s32[4]{0:T(128)S(1)} %copy-done.3, s32[128]{0:T(128)S(1)} %copy-done.4, s32[128]{0:T(128)S(1)} %collective-permute-done.meta_sib, f32[4,16]{1,0:T(4,128)S(1)} %copy-done.1, ...), custom_call_target="tpu_custom_call" | custom-call | flops 2818572288 | bytes 9175040 | tf_op jit(solution)/shard_map/work/pallas_call | solution.py:202
  169.6 2.7 %collective-permute-start.26 = (f32[12,32,128]{2,1,0:T(8,128)S(1)}, f32[12,32,128]{2,1,0:T(8,128)S(1)}, u32[]{:S(2)}, u32[]{:S(2)}) collective-permute-start(f32[12,32,128]{2,1,0:T(8,128)S(1)} %get-tuple-element.37), channel_id=1, source_target_pairs={{0,192},{64,128},{128,64},{192,0},{1,193},{65,129},{129,65},{193,1... | collective-permute-start | bytes 589832 | tf_op jit(solution)/shard_map/ppermute | solution.py:309
  172.4 7.7 %collective-permute-done.12 = f32[2,14,32,128]{3,2,1,0:T(8,128)S(1)} collective-permute-done((f32[2,14,32,128]{3,2,1,0:T(8,128)S(1)}, f32[2,14,32,128]{3,2,1,0:T(8,128)S(1)}, u32[]{:S(2)}, u32[]{:S(2)}) %collective-permute-start.12) | collective-permute-done | bytes 458784 | tf_op jit(solution)/shard_map/ppermute | solution.py:305
  180.2 3.4 %collective-permute-done.14 = f32[2,14,32,128]{3,2,1,0:T(8,128)S(1)} collective-permute-done((f32[2,14,32,128]{3,2,1,0:T(8,128)S(1)}, f32[2,14,32,128]{3,2,1,0:T(8,128)S(1)}, u32[]{:S(2)}, u32[]{:S(2)}) %collective-permute-start.14) | collective-permute-done | bytes 458784 | tf_op jit(solution)/shard_map/ppermute | solution.py:306
  183.7 6.3 %work.5 = (f32[2,6,32,128]{3,2,1,0:T(8,128)S(1)}, f32[2,6,32,128]{3,2,1,0:T(8,128)S(1)}, f32[2,6,32,128]{3,2,1,0:T(8,128)S(1)}, f32[2,6,32,128]{3,2,1,0:T(8,128)S(1)}) custom-call(s32[4]{0:T(128)S(1)} %copy-done.3, s32[128]{0:T(128)S(1)} %copy-done.4, s32[128]{0:T(128)S(1)} %collective-permute-done.meta_sib, f32[4,16]{1,0:T(4,128)S(1)} %copy-done.1, ...), custom_call_target="tpu_custom_call" | custom-call | flops 1207959552 | bytes 3932160 | tf_op jit(solution)/shard_map/work/pallas_call | solution.py:202
  191.4 6.0 %collective-permute-done.32 = f32[2,6,32,128]{3,2,1,0:T(8,128)S(1)} collective-permute-done((f32[2,6,32,128]{3,2,1,0:T(8,128)S(1)}, f32[2,6,32,128]{3,2,1,0:T(8,128)S(1)}, u32[]{:S(2)}, u32[]{:S(2)}) %collective-permute-start.32) | collective-permute-done | bytes 196640 | tf_op jit(solution)/shard_map/ppermute | solution.py:305
  199.7 1.3 collective-permute-start.33
  201.2 5.5 %collective-permute-done.13.rest_1_ = f32[14,32,128]{2,1,0:T(8,128)S(1)} collective-permute-done((f32[14,32,128]{2,1,0:T(8,128)S(1)}, f32[14,32,128]{2,1,0:T(8,128)S(1)}, u32[]{:S(2)}, u32[]{:S(2)}) %collective-permute-start.13) | collective-permute-done | bytes 229408 | tf_op jit(solution)/shard_map/ppermute | solution.py:309
  207.8 3.0 %collective-permute-done.36.rest_11_ = f32[6,32,128]{2,1,0:T(8,128)S(1)} collective-permute-done((f32[6,32,128]{2,1,0:T(8,128)S(1)}, f32[6,32,128]{2,1,0:T(8,128)S(1)}, u32[]{:S(2)}, u32[]{:S(2)}) %collective-permute-start.36) | collective-permute-done | bytes 98336 | tf_op jit(solution)/shard_map/ppermute | solution.py:311
  210.8 2.5 %finish.1 = f32[64,32,128]{2,1,0:T(8,128)} custom-call(s32[4]{0:T(128)S(1)} %copy-done.3, s32[128]{0:T(128)S(1)} %copy-done.4, f32[14,32,128]{2,1,0:T(8,128)S(1)} %get-tuple-element.34.rest_0_, f32[14,32,128]{2,1,0:T(8,128)S(1)} %collective-permute-done.13.rest_1_, f32[14,32,128]{2,1,0:T(8,128)S(1)} %collective-permute-done.15.rest_2_, ...), custom_call_target="tpu_custom_call" | custom-call | tf_op jit(solution)/shard_map/finish/pallas_call | solution.py:226
  (78 shorter events, 12.4 us)
Async XLA Ops:
  2.5 9.5 %collective-permute-start.5 = (f32[4,128,128]{2,1,0:T(8,128)}, f32[4,128,128]{2,1,0:T(8,128)S(1)}, u32[]{:S(2)}, u32[]{:S(2)}) collective-permute-start(f32[4,128,128]{2,1,0:T(8,128)} %get-tuple-element.43.rest_0_), channel_id=1, source_target_pairs={{0,16},{16,32},{32,48},{48,0},{1,17},{17,33},{33,49},{49,1},{2,18}... | collective-permute-start | bytes 786440 | tf_op jit(solution)/shard_map/ppermute | solution.py:239
  4.0 8.3 %collective-permute-start.3 = (f32[4,128,128]{2,1,0:T(8,128)}, f32[4,128,128]{2,1,0:T(8,128)S(1)}, u32[]{:S(2)}, u32[]{:S(2)}) collective-permute-start(f32[4,128,128]{2,1,0:T(8,128)} %get-tuple-element.43.rest_0_), channel_id=1, source_target_pairs={{0,2},{2,4},{4,6},{6,8},{8,10},{10,12},{12,14},{14,0},{1,3},{3,5},... | collective-permute-start | bytes 786440 | tf_op jit(solution)/shard_map/ppermute | solution.py:239
  5.9 76.5 %collective-permute-start.4 = (f32[4,128,128]{2,1,0:T(8,128)}, f32[4,128,128]{2,1,0:T(8,128)S(1)}, u32[]{:S(2)}, u32[]{:S(2)}) collective-permute-start(f32[4,128,128]{2,1,0:T(8,128)} %get-tuple-element.43.rest_0_), channel_id=1, source_target_pairs={{0,14},{2,0},{4,2},{6,4},{8,6},{10,8},{12,10},{14,12},{1,15},{3,1}... | collective-permute-start | bytes 786440 | tf_op jit(solution)/shard_map/ppermute | solution.py:239
  6.0 76.4 %collective-permute-start.6 = (f32[4,128,128]{2,1,0:T(8,128)}, f32[4,128,128]{2,1,0:T(8,128)S(1)}, u32[]{:S(2)}, u32[]{:S(2)}) collective-permute-start(f32[4,128,128]{2,1,0:T(8,128)} %get-tuple-element.43.rest_0_), channel_id=1, source_target_pairs={{0,48},{16,0},{32,16},{48,32},{1,49},{17,1},{33,17},{49,33},{2,50}... | collective-permute-start | bytes 786440 | tf_op jit(solution)/shard_map/ppermute | solution.py:239
  12.0 70.5 %collective-permute-start.7 = (f32[4,128,128]{2,1,0:T(8,128)S(1)}, f32[4,128,128]{2,1,0:T(8,128)}, u32[]{:S(2)}, u32[]{:S(2)}) collective-permute-start(f32[4,128,128]{2,1,0:T(8,128)S(1)} %collective-permute-done.5.rest_3_), channel_id=1, source_target_pairs={{0,16},{16,32},{32,48},{48,0},{1,17},{17,33},{33,49},{49,1},{2,18}... | collective-permute-start | bytes 786440 | tf_op jit(solution)/shard_map/ppermute | solution.py:239
  12.3 70.2 %collective-permute-start.8 = (f32[4,128,128]{2,1,0:T(8,128)S(1)}, f32[4,128,128]{2,1,0:T(8,128)}, u32[]{:S(2)}, u32[]{:S(2)}) collective-permute-start(f32[4,128,128]{2,1,0:T(8,128)S(1)} %collective-permute-done.3.rest_1_), channel_id=1, source_target_pairs={{0,2},{2,4},{4,6},{6,8},{8,10},{10,12},{12,14},{14,0},{1,3},{3,5},... | collective-permute-start | bytes 786440 | tf_op jit(solution)/shard_map/ppermute | solution.py:239
  82.3 56.7 %collective-permute-start.2 = (f32[32,128,128]{2,1,0:T(8,128)}, f32[32,128,128]{2,1,0:T(8,128)S(1)}, u32[]{:S(2)}, u32[]{:S(2)}) collective-permute-start(f32[32,128,128]{2,1,0:T(8,128)} %gather_blocks.1), channel_id=1, source_target_pairs={{0,1},{1,0},{2,3},{3,2},{4,5},{5,4},{6,7},{7,6},{8,9},{9,8},{10,11... | collective-permute-start | bytes 6291464 | tf_op jit(solution)/shard_map/ppermute | solution.py:239
  83.7 34.4 %collective-permute-start.10 = (f32[3,4,128,128]{3,2,1,0:T(8,128)S(1)}, f32[3,4,128,128]{3,2,1,0:T(8,128)S(1)}, u32[]{:S(2)}, u32[]{:S(2)}) collective-permute-start(f32[3,4,128,128]{3,2,1,0:T(8,128)S(1)} %maximum_select_fusion), channel_id=1, source_target_pairs={{0,2},{1,17},{2,4},{3,19},{4,6},{5,21},{6,8},{7,23},{8,10},{9,25},... | collective-permute-start | bytes 2359304 | tf_op jit(solution)/shard_map/ppermute | solution.py:252
  86.1 31.9 %collective-permute-start.11 = (f32[3,4,128,128]{3,2,1,0:T(8,128)S(1)}, f32[3,4,128,128]{3,2,1,0:T(8,128)S(1)}, u32[]{:S(2)}, u32[]{:S(2)}) collective-permute-start(f32[3,4,128,128]{3,2,1,0:T(8,128)S(1)} %maximum_select_fusion), channel_id=1, source_target_pairs={{0,14},{1,49},{2,0},{3,51},{4,2},{5,53},{6,4},{7,55},{8,6},{9,57},... | collective-permute-start | bytes 2359304 | tf_op jit(solution)/shard_map/ppermute | solution.py:252
  86.1 20.8 %collective-permute-start.9 = (f32[4,128,128]{2,1,0:T(8,128)S(1)}, f32[4,128,128]{2,1,0:T(8,128)S(1)}, u32[]{:S(2)}, u32[]{:S(2)}) collective-permute-start(f32[4,128,128]{2,1,0:T(8,128)S(1)} %collective-permute-done.4.rest_2_), channel_id=1, source_target_pairs={{0,14},{2,0},{4,2},{6,4},{8,6},{10,8},{12,10},{14,12},{1,15},{3,1}... | collective-permute-start | bytes 786440 | tf_op jit(solution)/shard_map/ppermute | solution.py:239
  89.1 17.9 %collective-permute-start.17 = (f32[4,128,128]{2,1,0:T(8,128)}, f32[4,128,128]{2,1,0:T(8,128)S(1)}, u32[]{:S(2)}, u32[]{:S(2)}) collective-permute-start(f32[4,128,128]{2,1,0:T(8,128)} %collective-permute-done.8.rest_6_), channel_id=1, source_target_pairs={{0,2},{2,4},{4,6},{6,8},{8,10},{10,12},{12,14},{14,0},{1,3},{3,5},... | collective-permute-start | bytes 786440 | tf_op jit(solution)/shard_map/ppermute | solution.py:239
  107.0 8.8 %collective-permute-start.18 = (f32[4,128,128]{2,1,0:T(8,128)S(1)}, f32[4,128,128]{2,1,0:T(8,128)S(1)}, u32[]{:S(2)}, u32[]{:S(2)}) collective-permute-start(f32[4,128,128]{2,1,0:T(8,128)S(1)} %collective-permute-done.9.rest_7_), channel_id=1, source_target_pairs={{0,14},{2,0},{4,2},{6,4},{8,6},{10,8},{12,10},{14,12},{1,15},{3,1}... | collective-permute-start | bytes 786440 | tf_op jit(solution)/shard_map/ppermute | solution.py:239
  118.2 20.8 %collective-permute-start.20 = (f32[3,4,128,128]{3,2,1,0:T(8,128)S(1)}, f32[3,4,128,128]{3,2,1,0:T(8,128)S(1)}, u32[]{:S(2)}, u32[]{:S(2)}) collective-permute-start(f32[3,4,128,128]{3,2,1,0:T(8,128)S(1)} %get-tuple-element.30), channel_id=1, source_target_pairs={{0,2},{1,17},{2,4},{3,19},{4,6},{5,21},{6,8},{7,23},{8,10},{9,25},... | collective-permute-start | bytes 2359304 | tf_op jit(solution)/shard_map/ppermute | solution.py:252
  121.2 17.8 %collective-permute-start.21 = (f32[3,4,128,128]{3,2,1,0:T(8,128)S(1)}, f32[3,4,128,128]{3,2,1,0:T(8,128)S(1)}, u32[]{:S(2)}, u32[]{:S(2)}) collective-permute-start(f32[3,4,128,128]{3,2,1,0:T(8,128)S(1)} %get-tuple-element.29), channel_id=1, source_target_pairs={{0,14},{1,49},{2,0},{3,51},{4,2},{5,53},{6,4},{7,55},{8,6},{9,57},... | collective-permute-start | bytes 2359304 | tf_op jit(solution)/shard_map/ppermute | solution.py:252
  122.6 8.5 %collective-permute-start.23 = (f32[4,128,128]{2,1,0:T(8,128)S(1)}, f32[4,128,128]{2,1,0:T(8,128)S(1)}, u32[]{:S(2)}, u32[]{:S(2)}) collective-permute-start(f32[4,128,128]{2,1,0:T(8,128)S(1)} %collective-permute-done.19.rest_2_), channel_id=1, source_target_pairs={{0,48},{16,0},{32,16},{48,32},{1,49},{17,1},{33,17},{49,33},{2,50}... | collective-permute-start | bytes 786440 | tf_op jit(solution)/shard_map/ppermute | solution.py:239
  124.1 9.7 %collective-permute-start.22 = (f32[4,128,128]{2,1,0:T(8,128)S(1)}, f32[4,128,128]{2,1,0:T(8,128)S(1)}, u32[]{:S(2)}, u32[]{:S(2)}) collective-permute-start(f32[4,128,128]{2,1,0:T(8,128)S(1)} %collective-permute-done.19.rest_2_), channel_id=1, source_target_pairs={{0,16},{16,32},{32,48},{48,0},{1,17},{17,33},{33,49},{49,1},{2,18}... | collective-permute-start | bytes 786440 | tf_op jit(solution)/shard_map/ppermute | solution.py:239
  131.1 7.9 %collective-permute-start.24 = (f32[4,128,128]{2,1,0:T(8,128)S(1)}, f32[4,128,128]{2,1,0:T(8,128)S(1)}, u32[]{:S(2)}, u32[]{:S(2)}) collective-permute-start(f32[4,128,128]{2,1,0:T(8,128)S(1)} %collective-permute-done.23.rest_6_), channel_id=1, source_target_pairs={{0,48},{16,0},{32,16},{48,32},{1,49},{17,1},{33,17},{49,33},{2,50}... | collective-permute-start | bytes 786440 | tf_op jit(solution)/shard_map/ppermute | solution.py:239
  149.9 19.0 %collective-permute-start.25 = (f32[2,12,32,128]{3,2,1,0:T(8,128)S(1)}, f32[2,12,32,128]{3,2,1,0:T(8,128)S(1)}, u32[]{:S(2)}, u32[]{:S(2)}) collective-permute-start(f32[2,12,32,128]{3,2,1,0:T(8,128)S(1)} %get-tuple-element.22), channel_id=1, source_target_pairs={{0,64},{64,0},{128,192},{192,128},{1,65},{65,1},{129,193},{193,129... | collective-permute-start | bytes 1179656 | tf_op jit(solution)/shard_map/ppermute | solution.py:305
  151.6 18.0 %collective-permute-start.27 = (f32[2,12,32,128]{3,2,1,0:T(8,128)S(1)}, f32[2,12,32,128]{3,2,1,0:T(8,128)S(1)}, u32[]{:S(2)}, u32[]{:S(2)}) collective-permute-start(f32[2,12,32,128]{3,2,1,0:T(8,128)S(1)} %get-tuple-element.24), channel_id=1, source_target_pairs={{0,192},{64,128},{128,64},{192,0},{1,193},{65,129},{129,65},{193,1... | collective-permute-start | bytes 1179656 | tf_op jit(solution)/shard_map/ppermute | solution.py:306
  153.8 29.9 %collective-permute-start.30 = (f32[3,4,128,128]{3,2,1,0:T(8,128)S(1)}, f32[3,4,128,128]{3,2,1,0:T(8,128)S(1)}, u32[]{:S(2)}, u32[]{:S(2)}) collective-permute-start(f32[3,4,128,128]{3,2,1,0:T(8,128)S(1)} %broadcast_select_fusion), channel_id=1, source_target_pairs={{0,2},{1,17},{2,4},{3,19},{4,6},{5,21},{6,8},{7,23},{8,10},{9,25},... | collective-permute-start | bytes 2359304 | tf_op jit(solution)/shard_map/ppermute | solution.py:252
  155.6 28.1 %collective-permute-start.31 = (f32[3,4,128,128]{3,2,1,0:T(8,128)S(1)}, f32[3,4,128,128]{3,2,1,0:T(8,128)S(1)}, u32[]{:S(2)}, u32[]{:S(2)}) collective-permute-start(f32[3,4,128,128]{3,2,1,0:T(8,128)S(1)} %collective-permute-done.21.rest_4_), channel_id=1, source_target_pairs={{0,14},{1,49},{2,0},{3,51},{4,2},{5,53},{6,4},{7,55},{8,6},{9,57},... | collective-permute-start | bytes 2359304 | tf_op jit(solution)/shard_map/ppermute | solution.py:252
  168.1 12.0 %collective-permute-start.12 = (f32[2,14,32,128]{3,2,1,0:T(8,128)S(1)}, f32[2,14,32,128]{3,2,1,0:T(8,128)S(1)}, u32[]{:S(2)}, u32[]{:S(2)}) collective-permute-start(f32[2,14,32,128]{3,2,1,0:T(8,128)S(1)} %get-tuple-element.18), channel_id=1, source_target_pairs={{0,64},{64,0},{128,192},{192,128},{1,65},{65,1},{129,193},{193,129... | collective-permute-start | bytes 1376264 | tf_op jit(solution)/shard_map/ppermute | solution.py:305
  168.9 14.7 %collective-permute-start.14 = (f32[2,14,32,128]{3,2,1,0:T(8,128)S(1)}, f32[2,14,32,128]{3,2,1,0:T(8,128)S(1)}, u32[]{:S(2)}, u32[]{:S(2)}) collective-permute-start(f32[2,14,32,128]{3,2,1,0:T(8,128)S(1)} %get-tuple-element.20), channel_id=1, source_target_pairs={{0,192},{64,128},{128,64},{192,0},{1,193},{65,129},{129,65},{193,1... | collective-permute-start | bytes 1376264 | tf_op jit(solution)/shard_map/ppermute | solution.py:306
  169.6 29.7 %collective-permute-start.26 = (f32[12,32,128]{2,1,0:T(8,128)S(1)}, f32[12,32,128]{2,1,0:T(8,128)S(1)}, u32[]{:S(2)}, u32[]{:S(2)}) collective-permute-start(f32[12,32,128]{2,1,0:T(8,128)S(1)} %get-tuple-element.37), channel_id=1, source_target_pairs={{0,192},{64,128},{128,64},{192,0},{1,193},{65,129},{129,65},{193,1... | collective-permute-start | bytes 589832 | tf_op jit(solution)/shard_map/ppermute | solution.py:309
  180.1 19.6 %collective-permute-start.28 = (f32[12,32,128]{2,1,0:T(8,128)S(1)}, f32[12,32,128]{2,1,0:T(8,128)S(1)}, u32[]{:S(2)}, u32[]{:S(2)}) collective-permute-start(f32[12,32,128]{2,1,0:T(8,128)S(1)} %get-tuple-element.36), channel_id=1, source_target_pairs={{0,1},{1,0},{64,65},{65,64},{128,129},{129,128},{192,193},{193,192... | collective-permute-start | bytes 589832 | tf_op jit(solution)/shard_map/ppermute | solution.py:310
  183.6 17.5 %collective-permute-start.29 = (f32[12,32,128]{2,1,0:T(8,128)S(1)}, f32[12,32,128]{2,1,0:T(8,128)S(1)}, u32[]{:S(2)}, u32[]{:S(2)}) collective-permute-start(f32[12,32,128]{2,1,0:T(8,128)S(1)} %get-tuple-element.35), channel_id=1, source_target_pairs={{0,65},{1,64},{64,1},{65,0},{128,193},{129,192},{192,129},{193,128... | collective-permute-start | bytes 589832 | tf_op jit(solution)/shard_map/ppermute | solution.py:311
  190.1 7.3 %collective-permute-start.32 = (f32[2,6,32,128]{3,2,1,0:T(8,128)S(1)}, f32[2,6,32,128]{3,2,1,0:T(8,128)S(1)}, u32[]{:S(2)}, u32[]{:S(2)}) collective-permute-start(f32[2,6,32,128]{3,2,1,0:T(8,128)S(1)} %get-tuple-element.26), channel_id=1, source_target_pairs={{0,64},{64,0},{128,192},{192,128},{1,65},{65,1},{129,193},{193,129... | collective-permute-start | bytes 589832 | tf_op jit(solution)/shard_map/ppermute | solution.py:305
  190.3 8.7 %collective-permute-start.34 = (f32[2,6,32,128]{3,2,1,0:T(8,128)S(1)}, f32[2,6,32,128]{3,2,1,0:T(8,128)S(1)}, u32[]{:S(2)}, u32[]{:S(2)}) collective-permute-start(f32[2,6,32,128]{3,2,1,0:T(8,128)S(1)} %get-tuple-element.28), channel_id=1, source_target_pairs={{0,192},{64,128},{128,64},{192,0},{1,193},{65,129},{129,65},{193,1... | collective-permute-start | bytes 589832 | tf_op jit(solution)/shard_map/ppermute | solution.py:306
  197.3 9.4 %collective-permute-start.13 = (f32[14,32,128]{2,1,0:T(8,128)S(1)}, f32[14,32,128]{2,1,0:T(8,128)S(1)}, u32[]{:S(2)}, u32[]{:S(2)}) collective-permute-start(f32[14,32,128]{2,1,0:T(8,128)S(1)} %get-tuple-element.33), channel_id=1, source_target_pairs={{0,192},{64,128},{128,64},{192,0},{1,193},{65,129},{129,65},{193,1... | collective-permute-start | bytes 688136 | tf_op jit(solution)/shard_map/ppermute | solution.py:309
  198.9 7.8 %collective-permute-start.15 = (f32[14,32,128]{2,1,0:T(8,128)S(1)}, f32[14,32,128]{2,1,0:T(8,128)S(1)}, u32[]{:S(2)}, u32[]{:S(2)}) collective-permute-start(f32[14,32,128]{2,1,0:T(8,128)S(1)} %get-tuple-element.32), channel_id=1, source_target_pairs={{0,1},{1,0},{64,65},{65,64},{128,129},{129,128},{192,193},{193,192... | collective-permute-start | bytes 688136 | tf_op jit(solution)/shard_map/ppermute | solution.py:310
  199.3 7.7 %collective-permute-start.16 = (f32[14,32,128]{2,1,0:T(8,128)S(1)}, f32[14,32,128]{2,1,0:T(8,128)S(1)}, u32[]{:S(2)}, u32[]{:S(2)}) collective-permute-start(f32[14,32,128]{2,1,0:T(8,128)S(1)} %get-tuple-element.31), channel_id=1, source_target_pairs={{0,65},{1,64},{64,1},{65,0},{128,193},{129,192},{192,129},{193,128... | collective-permute-start | bytes 688136 | tf_op jit(solution)/shard_map/ppermute | solution.py:311
  199.7 8.1 %collective-permute-start.33 = (f32[6,32,128]{2,1,0:T(8,128)S(1)}, f32[6,32,128]{2,1,0:T(8,128)S(1)}, u32[]{:S(2)}, u32[]{:S(2)}) collective-permute-start(f32[6,32,128]{2,1,0:T(8,128)S(1)} %get-tuple-element.41), channel_id=1, source_target_pairs={{0,192},{64,128},{128,64},{192,0},{1,193},{65,129},{129,65},{193,1... | collective-permute-start | bytes 294920 | tf_op jit(solution)/shard_map/ppermute | solution.py:309
  (10 other events, 119.1 us)

commit v2 on v1

v2 whole, which is shorter than its diff:
```python
import functools

import jax
import jax.numpy as jnp
from jax import lax
from jax.experimental import pallas as pl
from jax.experimental.pallas import tpu as pltpu
from jax.sharding import Mesh
from jax.sharding import PartitionSpec as P

NX, NZ, NC, NM = 4, 8, 2, 4
N = 128
TENSOR = ("x", "z", "c")
HALF = NX * NZ

SYM = dict(
    own=(0, 0), zf1=(0, -1), zb1=(0, 1), zf2=(0, -2), zb2=(0, 2), zf3=(0, -3), zb3=(0, 3), z4=(0, 4),
    xf1=(-1, 0), xb1=(1, 0), x2=(2, 0), df1=(-1, 4), db1=(1, 4), d2=(2, 4),
)
STEPS = dict(
    k1f=([(-1, -1), (1, -1)], [(-1, -1), (-1, 1)]),
    k1b=([(-1, 1), (1, 1)], [(1, -1), (1, 1)]),
    k2f=([(-1, -2), (1, -2), (2, -1)], [(-1, -2), (-1, 2), (-2, -1)]),
    k2b=([(-1, 2), (1, 2), (2, 1)], [(1, -2), (1, 2), (2, 1)]),
    k3f=([(-1, -3), (1, -3), (2, -2)], [(-1, -3), (-1, 3), (-2, -2)]),
    k3b=([(-1, 3), (1, 3), (2, 2)], [(1, -3), (1, 3), (2, 2)]),
    k4f=([(2, -3)], [(-2, -3)]),
    k4b=([(2, 3)], [(2, 3)]),
)
BATCHES = (
    ("own", "zf1", "zb1", "xf1", "xb1", "zf2", "zb2", "x2", "k1f", "k1b"),
    ("zf3", "zb3", "k2f", "k2b", "z4"),
    ("k3f", "k3b", "df1", "db1"),
    ("k4f", "k4b", "d2"),
)

LIMITS = (60, 12, 12, 12)


def slots_of(names):
    slots = []
    for name in names:
        slots += [(SYM[name], SYM[name])] if name in SYM else list(zip(*STEPS[name]))
    return slots


def width(name):
    return 1 if name in SYM else len(STEPS[name][0])


def sector(pos, core, slot):
    (x0, z0), (x1, z1) = slot
    first = core == 0
    x = (pos[1] + jnp.where(first, x0 % NX, x1 % NX)) % NX
    z = (pos[2] + jnp.where(first, z0 % NZ, z1 % NZ)) % NZ
    return (x * NZ + z) * NC + core


def split(value):
    high = value.astype(jnp.bfloat16)
    return high, (value - high.astype(jnp.float32)).astype(jnp.bfloat16)


def dot_nt(a, b):
    return lax.dot_general(a, b, (((1,), (1,)), ((), ())), preferred_element_type=jnp.float32)


def work_kernel(names, pos, inverse, side_own, side_sib, blocks, blocks_sib, *rest):
    arrays, rest = dict(zip(names, rest)), rest[len(names):]
    send, keep, table, sectors, right, wave, lefts, total, sem_r, sem_a, sem_b, sem_t = rest
    slots = slots_of(names)
    n = len(slots)

    tables = []
    for side, ref in enumerate((side_own, side_sib)):
        tables.append(pltpu.make_async_copy(ref.at[NM * N:], table.at[side], sem_t.at[side]))
        tables[side].start()
    core = pos[3]
    at = 0
    for name in names:
        if width(name) == 1:
            pltpu.make_async_copy(arrays[name], right.at[at], sem_r.at[at]).start()
        else:
            for t in range(width(name)):
                pltpu.make_async_copy(arrays[name].at[t], right.at[at + t], sem_r.at[at + t]).start()
        at += width(name)
    for i, slot in enumerate(slots):
        sectors[i] = sector(pos, core, slot)

    def own_copy(i):
        return pltpu.make_async_copy(blocks.at[inverse[sectors[i]]], wave.at[i, 0], sem_a.at[i])

    def sib_copy(i):
        place = table[1, NM, sectors[i]].astype(jnp.int32)
        return pltpu.make_async_copy(blocks_sib.at[place], wave.at[i, 1], sem_b.at[i])

    tables[0].wait()
    tables[1].wait()

    def start(i, carry):
        own_copy(i).start()
        sib_copy(i).start()
        return carry

    lax.fori_loop(0, n, start, 0)
    for side, ref in enumerate((side_own, side_sib)):
        for w in range(NM):
            high, low = split(ref[w * N:(w + 1) * N])
            lefts[side, w * N:(w + 1) * N, :N] = high
            lefts[side, w * N:(w + 1) * N, N:] = low

    m = pos[0]
    zero = jnp.zeros((N, N), jnp.bfloat16)

    def step(i, carry):
        pltpu.make_async_copy(right.at[i], right.at[i], sem_r.at[i]).wait()
        own_copy(i).wait()
        sib_copy(i).wait()
        parts = []
        for side in range(2):
            high, low = split(wave[i, side])
            weights = jnp.concatenate(
                [jnp.concatenate([high, low], 1), jnp.concatenate([high, zero], 1)], 0)
            both = jnp.dot(lefts[side], weights, preferred_element_type=jnp.float32)
            both = both[:, :N] + both[:, N:]
            parts.append([split(both[w * N:(w + 1) * N] * table[side, w, sectors[i]]) for w in range(NM)])
        acc = None
        for w in range(0, NM, 2):
            high = jnp.concatenate([jnp.concatenate([parts[s][w][0], parts[s][w + 1][0]], 1) for s in range(2)], 0)
            low = jnp.concatenate([jnp.concatenate([parts[s][w][1], parts[s][w + 1][1]], 1) for s in range(2)], 0)
            r0, r1 = split(right[i, w]), split(right[i, w + 1])
            r_high = jnp.concatenate([r0[0], r1[0]], 1)
            r_low = jnp.concatenate([r0[1], r1[1]], 1)
            big = dot_nt(high, jnp.concatenate([r_high, r_low], 0))
            small = dot_nt(low, r_high)
            now = big[:, :N] + big[:, N:] + small
            acc = now if acc is None else acc + now
        total[...] = acc
        share = N // NM
        near = jnp.where(core == 0, 1, 3)
        for side in range(2):
            def rows(q):
                return total[pl.ds(pl.multiple_of(side * N + q * share, share), share), :]

            send[0, side, i] = rows(m ^ near)
            send[1, side, i] = rows(m ^ 2)
            keep[0, side, i] = rows(m)
            keep[1, side, i] = rows(m ^ near ^ 2)
        return carry

    lax.fori_loop(0, n, step, 0)


def final_kernel(batches, pos, inverse, *rest):
    out = rest[-1]
    core = pos[3]
    for b, names in enumerate(batches):
        mine, term, other = rest[3 * b:3 * b + 3]
        for i, slot in enumerate(slots_of(names)):
            out[inverse[sector(pos, core, slot)]] = mine[i] + term[i]
            out[inverse[sector(pos, 1 - core, slot)]] = other[i]


SMEM = pl.BlockSpec(memory_space=pltpu.SMEM)
VMEM = pl.BlockSpec(memory_space=pltpu.VMEM)
ANY = pl.BlockSpec(memory_space=pl.ANY)


def work(limit, names, pos, inverse, side_own, side_sib, blocks, blocks_sib, got):
    n = sum(width(name) for name in names)
    arrays = [got[name] for name in names]
    piece = jax.ShapeDtypeStruct((2, 2, n, N // NM, N), jnp.float32)
    return pl.pallas_call(
        functools.partial(work_kernel, names),
        out_shape=(piece,) * 2,
        in_specs=[SMEM] * 2 + [VMEM] * 2 + [ANY] * (2 + len(arrays)),
        out_specs=(VMEM,) * 2,
        scratch_shapes=[
            pltpu.SMEM((2, 8, N), jnp.float32),
            pltpu.SMEM((n,), jnp.int32),
            pltpu.VMEM((n, NM, N, N), jnp.float32),
            pltpu.VMEM((n, 2, N, N), jnp.float32),
            pltpu.VMEM((2, NM * N, 2 * N), jnp.bfloat16),
            pltpu.VMEM((2 * N, N), jnp.float32),
            pltpu.SemaphoreType.DMA((n,)),
            pltpu.SemaphoreType.DMA((n,)),
            pltpu.SemaphoreType.DMA((n,)),
            pltpu.SemaphoreType.DMA((2,)),
        ],
        compiler_params=pltpu.CompilerParams(vmem_limit_bytes=limit * 2**20),
        name="work",
    )(pos, inverse, side_own, side_sib, blocks, blocks_sib, *arrays)


def finish(batches, pos, inverse, pieces):
    return pl.pallas_call(
        functools.partial(final_kernel, batches),
        out_shape=jax.ShapeDtypeStruct((NX * NZ * NC, N // NM, N), jnp.float32),
        in_specs=[SMEM, SMEM] + [VMEM] * len(pieces),
        out_specs=VMEM,
        compiler_params=pltpu.CompilerParams(vmem_limit_bytes=16 * 2**20),
        name="finish",
    )(pos, inverse, *pieces)


def shift(array, axis, step):
    size = {"x": NX, "z": NZ, "c": NC}[axis]
    return lax.ppermute(array, axis, [(i, (i + step) % size) for i in range(size)])


def place(x, z, c):
    return ((x % NX) * NZ + z % NZ) * NC + c


def by_core(array, step, cores=(0, 1)):
    pairs = []
    for x in range(NX):
        for z in range(NZ):
            pairs += [(place(x, z, c), place(x + step * c, z + step * (1 - c), c)) for c in cores]
    return lax.ppermute(array, TENSOR, pairs)


def by_core_far(array, axis, length=1):
    pairs = []
    for x in range(NX):
        for z in range(NZ):
            for c, step in ((0, length), (1, -length)):
                to = place(x + step, z, c) if axis == "x" else place(x, z + step, c)
                pairs.append((place(x, z, c), to))
    return lax.ppermute(array, TENSOR, pairs)


def fence(values):
    return lax.optimization_barrier(values)


def hops(first, second):
    return [(i * NC + c, (i ^ (first, second)[c]) * NC + c) for i in range(NM) for c in range(NC)]


def halve(parts):
    send, keep = parts
    return keep + lax.ppermute(send, ("m", "c"), hops(1, 3))


def quarter(sums):
    got = lax.ppermute(sums[1], ("m", "c"), hops(3, 1))
    return sums[0, 0], got[0], sums[0, 1] + got[1]


def swap(terms):
    return terms[0], terms[1], shift(terms[2], "c", 1)


def body(wavefunction, left_env, right_env, mpo_values, mpo_pattern, physical, right_sector, sector_size):
    m, x, z, c = (lax.axis_index(a) for a in ("m", "x", "z", "c"))
    first = c == 0
    live = jnp.arange(N, dtype=jnp.int32) < sector_size[0]
    own = jnp.where(live[:, None] & live[None, :], right_env[:, 0], 0.0)

    def pick(one, two):
        return jnp.where(first, one, two)

    got = dict(own=own)

    def tie(*names):
        for name, value in zip(names, lax.optimization_barrier([got[name] for name in names])):
            got[name] = value

    def arrive(**arrays):
        got.update(arrays)

    pos = jnp.stack([m, x, z, c]).astype(jnp.int32)
    block = jnp.arange(NC * HALF, dtype=jnp.int32)
    weights = mpo_values * mpo_pattern.astype(jnp.float32)
    is_state = physical[None, :] == jnp.arange(weights.shape[1], dtype=jnp.int32)[:, None]
    coef = jnp.sum(jnp.where(is_state[None], weights[:, :, None], 0.0), axis=1)
    is_sector = right_sector == block[None, :]
    inverse = jnp.sum(jnp.where(is_sector, block[:, None], 0), axis=0)
    coef = jnp.sum(jnp.where(is_sector[None], coef[:, :, None], 0.0), axis=1)
    table = jnp.concatenate([coef, inverse.astype(jnp.float32)[None]], axis=0)
    table = jnp.pad(table, ((0, 8 - NM - 1), (0, N - NC * HALF)))
    left = jnp.where(live[:, None] & live[None, :], left_env[:, 0], 0.0).reshape(NM * N, N)
    side = jnp.concatenate([left, table], axis=0)

    def run(batch):
        return work(LIMITS[batch], BATCHES[batch], pos, inverse, side, got["side_sib"], wavefunction, got["blocks_sib"], got)

    arrive(zf1=shift(own, "z", 1), zb1=shift(own, "z", -1))
    arrive(xf1=shift(own, "x", 1), xb1=shift(own, "x", -1))
    arrive(side=side, blocks_sib=shift(wavefunction, "c", 1))
    tie("zf1", "zb1", "xf1", "xb1", "side", "blocks_sib")

    zf1, zb1, xf1, xb1 = (got[name] for name in ("zf1", "zb1", "xf1", "xb1"))
    arrive(zf2=shift(zf1, "z", 1), zb2=shift(zb1, "z", -1))
    k1 = pick(jnp.stack([xf1, xb1]), jnp.stack([zf1, zb1]))
    arrive(k1f=by_core(k1, 1), k1b=by_core(k1, -1))
    arrive(side_sib=shift(got["side"], "c", 1))
    xb1, got["side_sib"] = fence((xb1, got["side_sib"]))
    arrive(x2=shift(xb1, "x", -1))
    tie("zf2", "zb2", "x2", "k1f", "k1b")

    zf2, zb2, x2, k1f, k1b = (got[name] for name in ("zf2", "zb2", "x2", "k1f", "k1b"))
    arrive(zf3=shift(zf2, "z", 1), zb3=shift(zb2, "z", -1))
    arrive(
        k2f=by_core(pick(jnp.stack([k1f[0], k1f[1], x2]), jnp.stack([zf2, zb2, k1f[0]])), 1),
        k2b=by_core(pick(jnp.stack([k1b[0], k1b[1], x2]), jnp.stack([zf2, zb2, k1b[1]])), -1),
    )
    got["a"] = run(0)
    tie("zf3", "zb3", "k2f", "k2b", "a")

    zf3, zb3, k2f, k2b = (got[name] for name in ("zf3", "zb3", "k2f", "k2b"))
    arrive(z4=by_core_far(pick(zf3, zb3), "z"))
    arrive(
        k3f=by_core(pick(k2f, jnp.stack([zf3, zb3, k2f[0]])), 1),
        k3b=by_core(pick(k2b, jnp.stack([zf3, zb3, k2b[1]])), -1),
    )
    a = halve(got["a"])
    tie("z4")
    arrive(df1=shift(got["z4"], "x", 1), db1=shift(got["z4"], "x", -1))
    b = run(1)
    got["done"] = a, b
    tie("df1", "db1", "k3f", "k3b", "done")

    k3f, k3b = got["k3f"], got["k3b"]
    a, b = got["done"]
    arrive(d2=shift(got["df1"], "x", 1))
    arrive(k4f=by_core(pick(k3f[2], k3f[0]), 1), k4b=by_core(pick(k3b[2], k3b[1]), -1))
    d = run(2)
    a = quarter(a)
    b = halve(b)
    got["done"] = a, b, d
    tie("d2", "k4f", "k4b", "done")

    a, b, d = got["done"]
    e = run(3)
    d = halve(d)
    b = quarter(b)
    a = swap(a)
    a, b, d, e = fence((a, b, d, e))

    e = halve(e)
    d = quarter(d)
    b = swap(b)
    b, d, e = fence((b, d, e))

    e = swap(quarter(e))
    d = swap(d)
    return finish(BATCHES, pos, inverse, a + b + d + e)


def solution(mesh):
    grid = Mesh(mesh.devices.reshape(NM, NX, NZ, NC), ("m", "x", "z", "c"))
    in_specs = (
        P(TENSOR, None, None),
        P("m", TENSOR, None, None),
        P("m", TENSOR, None, None),
        P("m", None),
        P("m", None),
        P(TENSOR),
        P(TENSOR, None),
        P(TENSOR),
    )
    out_specs = P(TENSOR, "m", None)
    return jax.shard_map(body, mesh=grid, in_specs=in_specs, out_specs=out_specs, check_vma=False)
```

time: 213 us -> 134 us (0.63)
  the two profiles are of different devices: /device:TPU:32 before, /device:TPU:1 now
where the time goes in v2:
time: 134 us; the launch traced here: 133 us
  starting transfers between devices  74.3 us (55%)
  Pallas kernels  29 us (22%)
  waiting for transfers between devices  19.6 us (15%)
  other arithmetic  8.93 us (7%)
    ppermute x18, starting transfers between devices, shift(): lax.ppermute(array, axis, [(i, (i + step) % size) for i in range(size)])  49.1 us
    pallas_call x4, Pallas kernels, work(): pl.pallas_call(functools.partial(work_kernel, names), out_shape=(piece,)...  27.3 us
    ppermute x8, starting transfers between devices, by_core(): return lax.ppermute(array, TENSOR, pairs)  11.7 us
    ppermute x18, waiting for transfers between devices, shift(): lax.ppermute(array, axis, [(i, (i + step) % size) for i in range(size)])  9.79 us
    ppermute x4, starting transfers between devices, halve(): return keep + lax.ppermute(send, ('m', 'c'), hops(1, 3))  8.31 us
    ppermute x1, waiting for transfers between devices, by_core_far(): return lax.ppermute(array, TENSOR, pairs)  6.25 us
    ppermute x4, starting transfers between devices, quarter(): got = lax.ppermute(sums[1], ('m', 'c'), hops(3, 1))  4.87 us
    ppermute x8, waiting for transfers between devices, by_core(): return lax.ppermute(array, TENSOR, pairs)  3.13 us
  transfers between devices with their start and end apart: 35, of which 8 were waited for; matrix products, arithmetic and copies ran while one was open for 5% of the time, Pallas kernels for 20%

profile of v2, /device:TPU:1, one launch (start us, length us, event | category | flops | bytes accessed | tf_op | source)
XLA Modules:
  0.0 133.4 jit_solution(13762295405114991116)
XLA Ops:
  0.0 3.2 %collective-permute-start.4 = (f32[64,128,128]{2,1,0:T(8,128)}, f32[64,128,128]{2,1,0:T(8,128)}, u32[]{:S(2)}, u32[]{:S(2)}) collective-permute-start(f32[64,128,128]{2,1,0:T(8,128)} %blocks.7), channel_id=1, source_target_pairs={{0,1},{1,0},{2,3},{3,2},{4,5},{5,4},{6,7},{7,6},{8,9},{9,8},{10,11... | collective-permute-start | bytes 12582920 | tf_op jit(solution)/shard_map/ppermute | solution.py:208
  5.1 3.9 %collective-permute-start.1 = (f32[4,128,128]{2,1,0:T(8,128)S(1)}, f32[4,128,128]{2,1,0:T(8,128)S(1)}, u32[]{:S(2)}, u32[]{:S(2)}) collective-permute-start(f32[4,128,128]{2,1,0:T(8,128)S(1)} %bitcast_select_fusion.1.rest_0_), channel_id=1, source_target_pairs={{0,14},{2,0},{4,2},{6,4},{8,6},{10,8},{12,10},{14,12},{1,15},{3,1}... | collective-permute-start | bytes 786440 | tf_op jit(solution)/shard_map/ppermute | solution.py:208
  10.2 1.5 %collective-permute-start.3 = (f32[4,128,128]{2,1,0:T(8,128)S(1)}, f32[4,128,128]{2,1,0:T(8,128)S(1)}, u32[]{:S(2)}, u32[]{:S(2)}) collective-permute-start(f32[4,128,128]{2,1,0:T(8,128)S(1)} %bitcast_select_fusion.1.rest_0_), channel_id=1, source_target_pairs={{0,48},{16,0},{32,16},{48,32},{1,49},{17,1},{33,17},{49,33},{2,50}... | collective-permute-start | bytes 786440 | tf_op jit(solution)/shard_map/ppermute | solution.py:208
  15.8 2.0 %collective-permute-done.2.rest_3_ = f32[4,128,128]{2,1,0:T(8,128)S(1)} collective-permute-done((f32[4,128,128]{2,1,0:T(8,128)S(1)}, f32[4,128,128]{2,1,0:T(8,128)S(1)}, u32[]{:S(2)}, u32[]{:S(2)}) %collective-permute-start.2) | collective-permute-done | bytes 262176 | tf_op jit(solution)/shard_map/ppermute | solution.py:208
  19.1 2.7 %collective-permute-start.10 = (f32[2,4,128,128]{3,2,1,0:T(8,128)S(1)}, f32[2,4,128,128]{3,2,1,0:T(8,128)S(1)}, u32[]{:S(2)}, u32[]{:S(2)}) collective-permute-start(f32[2,4,128,128]{3,2,1,0:T(8,128)S(1)} %maximum_select_fusion.2), channel_id=1, source_target_pairs={{0,14},{1,49},{2,0},{3,51},{4,2},{5,53},{6,4},{7,55},{8,6},{9,57},... | collective-permute-start | bytes 1572872 | tf_op jit(solution)/shard_map/ppermute | solution.py:220
  21.8 2.7 %collective-permute-start.6 = (f32[4,128,128]{2,1,0:T(8,128)S(1)}, f32[4,128,128]{2,1,0:T(8,128)}, u32[]{:S(2)}, u32[]{:S(2)}) collective-permute-start(f32[4,128,128]{2,1,0:T(8,128)S(1)} %collective-permute-done.1.rest_2_), channel_id=1, source_target_pairs={{0,14},{2,0},{4,2},{6,4},{8,6},{10,8},{12,10},{14,12},{1,15},{3,1}... | collective-permute-start | bytes 786440 | tf_op jit(solution)/shard_map/ppermute | solution.py:208
  24.5 2.7 %collective-permute-start.8 = (f32[4,128,128]{2,1,0:T(8,128)S(1)}, f32[4,128,128]{2,1,0:T(8,128)S(1)}, u32[]{:S(2)}, u32[]{:S(2)}) collective-permute-start(f32[4,128,128]{2,1,0:T(8,128)S(1)} %collective-permute-done.3.rest_4_), channel_id=1, source_target_pairs={{0,48},{16,0},{32,16},{48,32},{1,49},{17,1},{33,17},{49,33},{2,50}... | collective-permute-start | bytes 786440 | tf_op jit(solution)/shard_map/ppermute | solution.py:208
  27.2 4.1 %collective-permute-done.5.rest_5_ = f32[4,128,128]{2,1,0:T(8,128)S(1)} collective-permute-done((f32[4,128,128]{2,1,0:T(8,128)S(1)}, f32[4,128,128]{2,1,0:T(8,128)S(1)}, u32[]{:S(2)}, u32[]{:S(2)}) %collective-permute-start.5) | collective-permute-done | bytes 262176 | tf_op jit(solution)/shard_map/ppermute | solution.py:208
  31.4 1.9 %collective-permute-done.8.rest_7_ = f32[4,128,128]{2,1,0:T(8,128)S(1)} collective-permute-done((f32[4,128,128]{2,1,0:T(8,128)S(1)}, f32[4,128,128]{2,1,0:T(8,128)S(1)}, u32[]{:S(2)}, u32[]{:S(2)}) %collective-permute-start.8) | collective-permute-done | bytes 262176 | tf_op jit(solution)/shard_map/ppermute | solution.py:208
  33.3 2.4 %fusion.1 = (f32[3,4,128,128]{3,2,1,0:T(8,128)}, f32[3,4,128,128]{3,2,1,0:T(8,128)}) fusion(f32[1,4,128,128]{3,2,1,0:T(8,128)S(1)} %bitcast.79, f32[2,4,128,128]{3,2,1,0:T(8,128)S(1)} %collective-permute-done.10.rest_9_, f32[1,4,128,128]{3,2,1,0:T(8,128)S(1)} %slice.91, f32[1,4,128,128]{3,2,1,0:T(8,128)} %bitcast.16, f32[1,4,128,128]{3,2,1,0:T(8,128)S(1)} %bitcast.78, ...), kind=kLoop, calls=%fused_computation.3 | loop fusion | flops 1376256 | bytes 3932161 | tf_op jit(solution)/shard_map/jit(_where)/select_n | solution.py:262
  36.6 2.7 %collective-permute-start.14 = (f32[3,4,128,128]{3,2,1,0:T(8,128)}, f32[3,4,128,128]{3,2,1,0:T(8,128)S(1)}, u32[]{:S(2)}, u32[]{:S(2)}) collective-permute-start(f32[3,4,128,128]{3,2,1,0:T(8,128)} %get-tuple-element.123), channel_id=1, source_target_pairs={{0,14},{1,49},{2,0},{3,51},{4,2},{5,53},{6,4},{7,55},{8,6},{9,57},... | collective-permute-start | bytes 2359304 | tf_op jit(solution)/shard_map/ppermute | solution.py:220
  39.2 2.7 %collective-permute-start.12 = (f32[4,128,128]{2,1,0:T(8,128)}, f32[4,128,128]{2,1,0:T(8,128)S(1)}, u32[]{:S(2)}, u32[]{:S(2)}) collective-permute-start(f32[4,128,128]{2,1,0:T(8,128)} %collective-permute-done.6.rest_6_), channel_id=1, source_target_pairs={{0,14},{2,0},{4,2},{6,4},{8,6},{10,8},{12,10},{14,12},{1,15},{3,1}... | collective-permute-start | bytes 786440 | tf_op jit(solution)/shard_map/ppermute | solution.py:208
  42.5 10.4 %work.4 = (f32[2,2,12,32,128]{4,3,2,1,0:T(8,128)}, f32[2,2,12,32,128]{4,3,2,1,0:T(8,128)}) custom-call(s32[4]{0:T(128)} %pad_add_fusion.pos, s32[64]{0:T(128)} %copy-done.6, f32[520,128]{1,0:T(8,128)} %copy-done.1, f32[520,128]{1,0:T(8,128)} %copy-done.3, f32[64,128,128]{2,1,0:T(8,128)} %blocks.7, f32[64,128,128]{2,1,0:T(8,128)} %collective-permute-done.4.blocks_sib, ...), custom_call_target="tpu_custom_call" | custom-call | tf_op jit(solution)/shard_map/work/pallas_call | solution.py:173
  53.0 2.8 %collective-permute-start.20 = (f32[2,2,12,32,128]{4,3,2,1,0:T(8,128)}, f32[2,2,12,32,128]{4,3,2,1,0:T(8,128)S(1)}, u32[]{:S(2)}, u32[]{:S(2)}) collective-permute-start(f32[2,2,12,32,128]{4,3,2,1,0:T(8,128)} %get-tuple-element.84), channel_id=1, source_target_pairs={{0,64},{1,193},{64,0},{65,129},{128,192},{129,65},{192,128},{193,1... | collective-permute-start | bytes 2359304 | tf_op jit(solution)/shard_map/ppermute | solution.py:243
  56.2 2.7 %collective-permute-start.19 = (f32[3,4,128,128]{3,2,1,0:T(8,128)S(1)}, f32[3,4,128,128]{3,2,1,0:T(8,128)S(1)}, u32[]{:S(2)}, u32[]{:S(2)}) collective-permute-start(f32[3,4,128,128]{3,2,1,0:T(8,128)S(1)} %get-tuple-element.125), channel_id=1, source_target_pairs={{0,14},{1,49},{2,0},{3,51},{4,2},{5,53},{6,4},{7,55},{8,6},{9,57},... | collective-permute-start | bytes 2359304 | tf_op jit(solution)/shard_map/ppermute | solution.py:220
  59.2 6.2 %collective-permute-done.15.rest_4_ = f32[4,128,128]{2,1,0:T(8,128)S(1)} collective-permute-done((f32[4,128,128]{2,1,0:T(8,128)S(1)}, f32[4,128,128]{2,1,0:T(8,128)S(1)}, u32[]{:S(2)}, u32[]{:S(2)}) %collective-permute-start.15) | collective-permute-done | bytes 262176 | tf_op jit(solution)/shard_map/ppermute | solution.py:230
  65.5 2.7 %collective-permute-start.17 = (f32[4,128,128]{2,1,0:T(8,128)S(1)}, f32[4,128,128]{2,1,0:T(8,128)S(1)}, u32[]{:S(2)}, u32[]{:S(2)}) collective-permute-start(f32[4,128,128]{2,1,0:T(8,128)S(1)} %collective-permute-done.15.rest_4_), channel_id=1, source_target_pairs={{0,48},{16,0},{32,16},{48,32},{1,49},{17,1},{33,17},{49,33},{2,50}... | collective-permute-start | bytes 786440 | tf_op jit(solution)/shard_map/ppermute | solution.py:208
  68.2 6.9 %work.5 = (f32[2,2,9,32,128]{4,3,2,1,0:T(8,128)S(1)}, f32[2,2,9,32,128]{4,3,2,1,0:T(8,128)S(1)}) custom-call(s32[4]{0:T(128)S(1)} %copy-done.5, s32[64]{0:T(128)S(1)} %copy-done.7, f32[520,128]{1,0:T(8,128)S(1)} %copy-done.2, f32[520,128]{1,0:T(8,128)S(1)} %copy-done.4, f32[64,128,128]{2,1,0:T(8,128)S(1)} %copy-done, ...), custom_call_target="tpu_custom_call" | custom-call | tf_op jit(solution)/shard_map/work/pallas_call | solution.py:173
  75.7 6.3 %work.6 = (f32[2,2,8,32,128]{4,3,2,1,0:T(8,128)S(1)}, f32[2,2,8,32,128]{4,3,2,1,0:T(8,128)S(1)}) custom-call(s32[4]{0:T(128)S(1)} %copy-done.5, s32[64]{0:T(128)S(1)} %copy-done.7, f32[520,128]{1,0:T(8,128)S(1)} %copy-done.2, f32[520,128]{1,0:T(8,128)S(1)} %copy-done.4, f32[64,128,128]{2,1,0:T(8,128)S(1)} %copy-done, ...), custom_call_target="tpu_custom_call" | custom-call | tf_op jit(solution)/shard_map/work/pallas_call | solution.py:173
  82.1 2.7 %collective-permute-start.23 = (f32[4,128,128]{2,1,0:T(8,128)S(1)}, f32[4,128,128]{2,1,0:T(8,128)S(1)}, u32[]{:S(2)}, u32[]{:S(2)}) collective-permute-start(f32[4,128,128]{2,1,0:T(8,128)S(1)} %select_bitcast_fusion), channel_id=1, source_target_pairs={{0,14},{1,49},{2,0},{3,51},{4,2},{5,53},{6,4},{7,55},{8,6},{9,57},... | collective-permute-start | bytes 786440 | tf_op jit(solution)/shard_map/ppermute | solution.py:220
  85.4 3.1 %collective-permute-done.22.rest_0_ = f32[4,128,128]{2,1,0:T(8,128)S(1)} collective-permute-done((f32[4,128,128]{2,1,0:T(8,128)S(1)}, f32[4,128,128]{2,1,0:T(8,128)S(1)}, u32[]{:S(2)}, u32[]{:S(2)}) %collective-permute-start.22) | collective-permute-done | bytes 262176 | tf_op jit(solution)/shard_map/ppermute | solution.py:220
  88.5 1.5 %collective-permute-start.27 = (f32[2,9,32,128]{3,2,1,0:T(8,128)S(1)}, f32[2,9,32,128]{3,2,1,0:T(8,128)S(1)}, u32[]{:S(2)}, u32[]{:S(2)}) collective-permute-start(f32[2,9,32,128]{3,2,1,0:T(8,128)S(1)} %slice_bitcast_fusion.1), channel_id=1, source_target_pairs={{0,192},{1,65},{64,128},{65,1},{128,64},{129,193},{192,0},{193,129... | collective-permute-start | bytes 884744 | tf_op jit(solution)/shard_map/ppermute | solution.py:247
  90.1 2.7 %collective-permute-start.28 = (f32[2,2,8,32,128]{4,3,2,1,0:T(8,128)S(1)}, f32[2,2,8,32,128]{4,3,2,1,0:T(8,128)S(1)}, u32[]{:S(2)}, u32[]{:S(2)}) collective-permute-start(f32[2,2,8,32,128]{4,3,2,1,0:T(8,128)S(1)} %get-tuple-element.101), channel_id=1, source_target_pairs={{0,64},{1,193},{64,0},{65,129},{128,192},{129,65},{192,128},{193,1... | collective-permute-start | bytes 1572872 | tf_op jit(solution)/shard_map/ppermute | solution.py:243
  92.7 12.0 %collective-permute-start.26 = (f32[12,32,128]{2,1,0:T(8,128)S(1)}, f32[12,32,128]{2,1,0:T(8,128)S(1)}, u32[]{:S(2)}, u32[]{:S(2)}) collective-permute-start(f32[12,32,128]{2,1,0:T(8,128)S(1)} %fusion.2), channel_id=1, source_target_pairs={{0,1},{1,0},{2,3},{3,2},{4,5},{5,4},{6,7},{7,6},{8,9},{9,8},{10,11... | collective-permute-start | bytes 589832 | tf_op jit(solution)/shard_map/ppermute | solution.py:208
  104.8 3.7 %work.7 = (f32[2,2,3,32,128]{4,3,2,1,0:T(8,128)S(1)}, f32[2,2,3,32,128]{4,3,2,1,0:T(8,128)S(1)}) custom-call(s32[4]{0:T(128)S(1)} %copy-done.5, s32[64]{0:T(128)S(1)} %copy-done.7, f32[520,128]{1,0:T(8,128)S(1)} %copy-done.2, f32[520,128]{1,0:T(8,128)S(1)} %copy-done.4, f32[64,128,128]{2,1,0:T(8,128)S(1)} %copy-done, ...), custom_call_target="tpu_custom_call" | custom-call | tf_op jit(solution)/shard_map/work/pallas_call | solution.py:173
  108.7 1.5 %collective-permute-start.30 = (f32[2,8,32,128]{3,2,1,0:T(8,128)S(1)}, f32[2,8,32,128]{3,2,1,0:T(8,128)S(1)}, u32[]{:S(2)}, u32[]{:S(2)}) collective-permute-start(f32[2,8,32,128]{3,2,1,0:T(8,128)S(1)} %slice_bitcast_fusion.2), channel_id=1, source_target_pairs={{0,192},{1,65},{64,128},{65,1},{128,64},{129,193},{192,0},{193,129... | collective-permute-start | bytes 786440 | tf_op jit(solution)/shard_map/ppermute | solution.py:247
  110.2 2.7 %collective-permute-start.31 = (f32[2,2,3,32,128]{4,3,2,1,0:T(8,128)S(1)}, f32[2,2,3,32,128]{4,3,2,1,0:T(8,128)S(1)}, u32[]{:S(2)}, u32[]{:S(2)}) collective-permute-start(f32[2,2,3,32,128]{4,3,2,1,0:T(8,128)S(1)} %get-tuple-element.115), channel_id=1, source_target_pairs={{0,64},{1,193},{64,0},{65,129},{128,192},{129,65},{192,128},{193,1... | collective-permute-start | bytes 589832 | tf_op jit(solution)/shard_map/ppermute | solution.py:243
  112.9 5.0 %collective-permute-start.29 = (f32[9,32,128]{2,1,0:T(8,128)S(1)}, f32[9,32,128]{2,1,0:T(8,128)S(1)}, u32[]{:S(2)}, u32[]{:S(2)}) collective-permute-start(f32[9,32,128]{2,1,0:T(8,128)S(1)} %fusion.3), channel_id=1, source_target_pairs={{0,1},{1,0},{2,3},{3,2},{4,5},{5,4},{6,7},{7,6},{8,9},{9,8},{10,11... | collective-permute-start | bytes 442376 | tf_op jit(solution)/shard_map/ppermute | solution.py:208
  118.9 1.8 %collective-permute-start.33 = (f32[2,3,32,128]{3,2,1,0:T(8,128)S(1)}, f32[2,3,32,128]{3,2,1,0:T(8,128)S(1)}, u32[]{:S(2)}, u32[]{:S(2)}) collective-permute-start(f32[2,3,32,128]{3,2,1,0:T(8,128)S(1)} %slice_bitcast_fusion.12), channel_id=1, source_target_pairs={{0,192},{1,65},{64,128},{65,1},{128,64},{129,193},{192,0},{193,129... | collective-permute-start | bytes 294920 | tf_op jit(solution)/shard_map/ppermute | solution.py:247
  120.7 4.9 %collective-permute-start.32 = (f32[8,32,128]{2,1,0:T(8,128)S(1)}, f32[8,32,128]{2,1,0:T(8,128)S(1)}, u32[]{:S(2)}, u32[]{:S(2)}) collective-permute-start(f32[8,32,128]{2,1,0:T(8,128)S(1)} %fusion.4), channel_id=1, source_target_pairs={{0,1},{1,0},{2,3},{3,2},{4,5},{5,4},{6,7},{7,6},{8,9},{9,8},{10,11... | collective-permute-start | bytes 393224 | tf_op jit(solution)/shard_map/ppermute | solution.py:208
  125.7 5.1 %collective-permute-start.34 = (f32[3,32,128]{2,1,0:T(8,128)S(1)}, f32[3,32,128]{2,1,0:T(8,128)S(1)}, u32[]{:S(2)}, u32[]{:S(2)}) collective-permute-start(f32[3,32,128]{2,1,0:T(8,128)S(1)} %fusion.5), channel_id=1, source_target_pairs={{0,1},{1,0},{2,3},{3,2},{4,5},{5,4},{6,7},{7,6},{8,9},{9,8},{10,11... | collective-permute-start | bytes 147464 | tf_op jit(solution)/shard_map/ppermute | solution.py:208
  131.7 1.8 %finish.1 = f32[64,32,128]{2,1,0:T(8,128)} custom-call(s32[4]{0:T(128)S(1)} %copy-done.5, s32[64]{0:T(128)S(1)} %copy-done.7, f32[12,32,128]{2,1,0:T(8,128)S(1)} %slice_bitcast_fusion.5.rest_0_, f32[12,32,128]{2,1,0:T(8,128)S(1)} %slice_bitcast_fusion.4.rest_1_, f32[12,32,128]{2,1,0:T(8,128)S(1)} %collective-permute-done.26.rest_2_, ...), custom_call_target="tpu_custom_call" | custom-call | tf_op jit(solution)/shard_map/finish/pallas_call | solution.py:196
  (123 shorter events, 13.2 us)
Async XLA Ops:
  0.0 17.8 %collective-permute-start.4 = (f32[64,128,128]{2,1,0:T(8,128)}, f32[64,128,128]{2,1,0:T(8,128)}, u32[]{:S(2)}, u32[]{:S(2)}) collective-permute-start(f32[64,128,128]{2,1,0:T(8,128)} %blocks.7), channel_id=1, source_target_pairs={{0,1},{1,0},{2,3},{3,2},{4,5},{5,4},{6,7},{7,6},{8,9},{9,8},{10,11... | collective-permute-start | bytes 12582920 | tf_op jit(solution)/shard_map/ppermute | solution.py:208
  5.0 10.8 %collective-permute-start = (f32[4,128,128]{2,1,0:T(8,128)S(1)}, f32[4,128,128]{2,1,0:T(8,128)S(1)}, u32[]{:S(2)}, u32[]{:S(2)}) collective-permute-start(f32[4,128,128]{2,1,0:T(8,128)S(1)} %bitcast_select_fusion.1.rest_0_), channel_id=1, source_target_pairs={{0,2},{2,4},{4,6},{6,8},{8,10},{10,12},{12,14},{14,0},{1,3},{3,5},... | collective-permute-start | bytes 786440 | tf_op jit(solution)/shard_map/ppermute | solution.py:208
  5.1 10.7 %collective-permute-start.1 = (f32[4,128,128]{2,1,0:T(8,128)S(1)}, f32[4,128,128]{2,1,0:T(8,128)S(1)}, u32[]{:S(2)}, u32[]{:S(2)}) collective-permute-start(f32[4,128,128]{2,1,0:T(8,128)S(1)} %bitcast_select_fusion.1.rest_0_), channel_id=1, source_target_pairs={{0,14},{2,0},{4,2},{6,4},{8,6},{10,8},{12,10},{14,12},{1,15},{3,1}... | collective-permute-start | bytes 786440 | tf_op jit(solution)/shard_map/ppermute | solution.py:208
  9.0 8.8 %collective-permute-start.2 = (f32[4,128,128]{2,1,0:T(8,128)S(1)}, f32[4,128,128]{2,1,0:T(8,128)S(1)}, u32[]{:S(2)}, u32[]{:S(2)}) collective-permute-start(f32[4,128,128]{2,1,0:T(8,128)S(1)} %bitcast_select_fusion.1.rest_0_), channel_id=1, source_target_pairs={{0,16},{16,32},{32,48},{48,0},{1,17},{17,33},{33,49},{49,1},{2,18}... | collective-permute-start | bytes 786440 | tf_op jit(solution)/shard_map/ppermute | solution.py:208
  10.2 7.6 %collective-permute-start.3 = (f32[4,128,128]{2,1,0:T(8,128)S(1)}, f32[4,128,128]{2,1,0:T(8,128)S(1)}, u32[]{:S(2)}, u32[]{:S(2)}) collective-permute-start(f32[4,128,128]{2,1,0:T(8,128)S(1)} %bitcast_select_fusion.1.rest_0_), channel_id=1, source_target_pairs={{0,48},{16,0},{32,16},{48,32},{1,49},{17,1},{33,17},{49,33},{2,50}... | collective-permute-start | bytes 786440 | tf_op jit(solution)/shard_map/ppermute | solution.py:208
  17.8 6.6 %collective-permute-start.7 = (f32[520,128]{1,0:T(8,128)S(1)}, f32[520,128]{1,0:T(8,128)S(1)}, u32[]{:S(2)}, u32[]{:S(2)}) collective-permute-start(f32[520,128]{1,0:T(8,128)S(1)} %pad_maximum_fusion.4.side_own), channel_id=1, source_target_pairs={{0,1},{1,0},{2,3},{3,2},{4,5},{5,4},{6,7},{7,6},{8,9},{9,8},{10,11... | collective-permute-start | bytes 798728 | tf_op jit(solution)/shard_map/ppermute | solution.py:208
  19.1 12.2 %collective-permute-start.10 = (f32[2,4,128,128]{3,2,1,0:T(8,128)S(1)}, f32[2,4,128,128]{3,2,1,0:T(8,128)S(1)}, u32[]{:S(2)}, u32[]{:S(2)}) collective-permute-start(f32[2,4,128,128]{3,2,1,0:T(8,128)S(1)} %maximum_select_fusion.2), channel_id=1, source_target_pairs={{0,14},{1,49},{2,0},{3,51},{4,2},{5,53},{6,4},{7,55},{8,6},{9,57},... | collective-permute-start | bytes 1572872 | tf_op jit(solution)/shard_map/ppermute | solution.py:220
  21.8 9.6 %collective-permute-start.9 = (f32[2,4,128,128]{3,2,1,0:T(8,128)S(1)}, f32[2,4,128,128]{3,2,1,0:T(8,128)S(1)}, u32[]{:S(2)}, u32[]{:S(2)}) collective-permute-start(f32[2,4,128,128]{3,2,1,0:T(8,128)S(1)} %maximum_select_fusion.2), channel_id=1, source_target_pairs={{0,2},{1,17},{2,4},{3,19},{4,6},{5,21},{6,8},{7,23},{8,10},{9,25},... | collective-permute-start | bytes 1572872 | tf_op jit(solution)/shard_map/ppermute | solution.py:220
  21.8 9.5 %collective-permute-start.5 = (f32[4,128,128]{2,1,0:T(8,128)S(1)}, f32[4,128,128]{2,1,0:T(8,128)S(1)}, u32[]{:S(2)}, u32[]{:S(2)}) collective-permute-start(f32[4,128,128]{2,1,0:T(8,128)S(1)} %collective-permute-done.rest_1_), channel_id=1, source_target_pairs={{0,2},{2,4},{4,6},{6,8},{8,10},{10,12},{12,14},{14,0},{1,3},{3,5},... | collective-permute-start | bytes 786440 | tf_op jit(solution)/shard_map/ppermute | solution.py:208
  21.8 9.5 %collective-permute-start.6 = (f32[4,128,128]{2,1,0:T(8,128)S(1)}, f32[4,128,128]{2,1,0:T(8,128)}, u32[]{:S(2)}, u32[]{:S(2)}) collective-permute-start(f32[4,128,128]{2,1,0:T(8,128)S(1)} %collective-permute-done.1.rest_2_), channel_id=1, source_target_pairs={{0,14},{2,0},{4,2},{6,4},{8,6},{10,8},{12,10},{14,12},{1,15},{3,1}... | collective-permute-start | bytes 786440 | tf_op jit(solution)/shard_map/ppermute | solution.py:208
  24.5 8.8 %collective-permute-start.8 = (f32[4,128,128]{2,1,0:T(8,128)S(1)}, f32[4,128,128]{2,1,0:T(8,128)S(1)}, u32[]{:S(2)}, u32[]{:S(2)}) collective-permute-start(f32[4,128,128]{2,1,0:T(8,128)S(1)} %collective-permute-done.3.rest_4_), channel_id=1, source_target_pairs={{0,48},{16,0},{32,16},{48,32},{1,49},{17,1},{33,17},{49,33},{2,50}... | collective-permute-start | bytes 786440 | tf_op jit(solution)/shard_map/ppermute | solution.py:208
  35.7 17.3 %collective-permute-start.13 = (f32[3,4,128,128]{3,2,1,0:T(8,128)}, f32[3,4,128,128]{3,2,1,0:T(8,128)S(1)}, u32[]{:S(2)}, u32[]{:S(2)}) collective-permute-start(f32[3,4,128,128]{3,2,1,0:T(8,128)} %get-tuple-element.124), channel_id=1, source_target_pairs={{0,2},{1,17},{2,4},{3,19},{4,6},{5,21},{6,8},{7,23},{8,10},{9,25},... | collective-permute-start | bytes 2359304 | tf_op jit(solution)/shard_map/ppermute | solution.py:220
  36.6 16.4 %collective-permute-start.14 = (f32[3,4,128,128]{3,2,1,0:T(8,128)}, f32[3,4,128,128]{3,2,1,0:T(8,128)S(1)}, u32[]{:S(2)}, u32[]{:S(2)}) collective-permute-start(f32[3,4,128,128]{3,2,1,0:T(8,128)} %get-tuple-element.123), channel_id=1, source_target_pairs={{0,14},{1,49},{2,0},{3,51},{4,2},{5,53},{6,4},{7,55},{8,6},{9,57},... | collective-permute-start | bytes 2359304 | tf_op jit(solution)/shard_map/ppermute | solution.py:220
  39.2 13.7 %collective-permute-start.11 = (f32[4,128,128]{2,1,0:T(8,128)S(1)}, f32[4,128,128]{2,1,0:T(8,128)S(1)}, u32[]{:S(2)}, u32[]{:S(2)}) collective-permute-start(f32[4,128,128]{2,1,0:T(8,128)S(1)} %collective-permute-done.5.rest_5_), channel_id=1, source_target_pairs={{0,2},{2,4},{4,6},{6,8},{8,10},{10,12},{12,14},{14,0},{1,3},{3,5},... | collective-permute-start | bytes 786440 | tf_op jit(solution)/shard_map/ppermute | solution.py:208
  39.2 13.7 %collective-permute-start.12 = (f32[4,128,128]{2,1,0:T(8,128)}, f32[4,128,128]{2,1,0:T(8,128)S(1)}, u32[]{:S(2)}, u32[]{:S(2)}) collective-permute-start(f32[4,128,128]{2,1,0:T(8,128)} %collective-permute-done.6.rest_6_), channel_id=1, source_target_pairs={{0,14},{2,0},{4,2},{6,4},{8,6},{10,8},{12,10},{14,12},{1,15},{3,1}... | collective-permute-start | bytes 786440 | tf_op jit(solution)/shard_map/ppermute | solution.py:208
  53.0 22.1 %collective-permute-start.20 = (f32[2,2,12,32,128]{4,3,2,1,0:T(8,128)}, f32[2,2,12,32,128]{4,3,2,1,0:T(8,128)S(1)}, u32[]{:S(2)}, u32[]{:S(2)}) collective-permute-start(f32[2,2,12,32,128]{4,3,2,1,0:T(8,128)} %get-tuple-element.84), channel_id=1, source_target_pairs={{0,64},{1,193},{64,0},{65,129},{128,192},{129,65},{192,128},{193,1... | collective-permute-start | bytes 2359304 | tf_op jit(solution)/shard_map/ppermute | solution.py:243
  56.1 19.2 %collective-permute-start.18 = (f32[3,4,128,128]{3,2,1,0:T(8,128)S(1)}, f32[3,4,128,128]{3,2,1,0:T(8,128)S(1)}, u32[]{:S(2)}, u32[]{:S(2)}) collective-permute-start(f32[3,4,128,128]{3,2,1,0:T(8,128)S(1)} %get-tuple-element.126), channel_id=1, source_target_pairs={{0,2},{1,17},{2,4},{3,19},{4,6},{5,21},{6,8},{7,23},{8,10},{9,25},... | collective-permute-start | bytes 2359304 | tf_op jit(solution)/shard_map/ppermute | solution.py:220
  56.2 19.1 %collective-permute-start.19 = (f32[3,4,128,128]{3,2,1,0:T(8,128)S(1)}, f32[3,4,128,128]{3,2,1,0:T(8,128)S(1)}, u32[]{:S(2)}, u32[]{:S(2)}) collective-permute-start(f32[3,4,128,128]{3,2,1,0:T(8,128)S(1)} %get-tuple-element.125), channel_id=1, source_target_pairs={{0,14},{1,49},{2,0},{3,51},{4,2},{5,53},{6,4},{7,55},{8,6},{9,57},... | collective-permute-start | bytes 2359304 | tf_op jit(solution)/shard_map/ppermute | solution.py:220
  58.9 6.6 %collective-permute-start.15 = (f32[4,128,128]{2,1,0:T(8,128)S(1)}, f32[4,128,128]{2,1,0:T(8,128)S(1)}, u32[]{:S(2)}, u32[]{:S(2)}) collective-permute-start(f32[4,128,128]{2,1,0:T(8,128)S(1)} %broadcast_select_fusion), channel_id=1, source_target_pairs={{0,2},{1,15},{2,4},{3,1},{4,6},{5,3},{6,8},{7,5},{8,10},{9,7},{10,... | collective-permute-start | bytes 786440 | tf_op jit(solution)/shard_map/ppermute | solution.py:230
  65.5 9.8 %collective-permute-start.16 = (f32[4,128,128]{2,1,0:T(8,128)S(1)}, f32[4,128,128]{2,1,0:T(8,128)S(1)}, u32[]{:S(2)}, u32[]{:S(2)}) collective-permute-start(f32[4,128,128]{2,1,0:T(8,128)S(1)} %collective-permute-done.15.rest_4_), channel_id=1, source_target_pairs={{0,16},{16,32},{32,48},{48,0},{1,17},{17,33},{33,49},{49,1},{2,18}... | collective-permute-start | bytes 786440 | tf_op jit(solution)/shard_map/ppermute | solution.py:208
  65.5 9.8 %collective-permute-start.17 = (f32[4,128,128]{2,1,0:T(8,128)S(1)}, f32[4,128,128]{2,1,0:T(8,128)S(1)}, u32[]{:S(2)}, u32[]{:S(2)}) collective-permute-start(f32[4,128,128]{2,1,0:T(8,128)S(1)} %collective-permute-done.15.rest_4_), channel_id=1, source_target_pairs={{0,48},{16,0},{32,16},{48,32},{1,49},{17,1},{33,17},{49,33},{2,50}... | collective-permute-start | bytes 786440 | tf_op jit(solution)/shard_map/ppermute | solution.py:208
  75.3 10.0 %collective-permute-start.25 = (f32[2,2,9,32,128]{4,3,2,1,0:T(8,128)S(1)}, f32[2,2,9,32,128]{4,3,2,1,0:T(8,128)S(1)}, u32[]{:S(2)}, u32[]{:S(2)}) collective-permute-start(f32[2,2,9,32,128]{4,3,2,1,0:T(8,128)S(1)} %get-tuple-element.92), channel_id=1, source_target_pairs={{0,64},{1,193},{64,0},{65,129},{128,192},{129,65},{192,128},{193,1... | collective-permute-start | bytes 1769480 | tf_op jit(solution)/shard_map/ppermute | solution.py:243
  75.4 9.4 %collective-permute-start.24 = (f32[2,12,32,128]{3,2,1,0:T(8,128)S(1)}, f32[2,12,32,128]{3,2,1,0:T(8,128)S(1)}, u32[]{:S(2)}, u32[]{:S(2)}) collective-permute-start(f32[2,12,32,128]{3,2,1,0:T(8,128)S(1)} %slice_bitcast_fusion), channel_id=1, source_target_pairs={{0,192},{1,65},{64,128},{65,1},{128,64},{129,193},{192,0},{193,129... | collective-permute-start | bytes 1179656 | tf_op jit(solution)/shard_map/ppermute | solution.py:247
  75.6 12.9 %collective-permute-start.21 = (f32[4,128,128]{2,1,0:T(8,128)S(1)}, f32[4,128,128]{2,1,0:T(8,128)S(1)}, u32[]{:S(2)}, u32[]{:S(2)}) collective-permute-start(f32[4,128,128]{2,1,0:T(8,128)S(1)} %collective-permute-done.16.rest_2_), channel_id=1, source_target_pairs={{0,16},{16,32},{32,48},{48,0},{1,17},{17,33},{33,49},{49,1},{2,18}... | collective-permute-start | bytes 786440 | tf_op jit(solution)/shard_map/ppermute | solution.py:208
  82.0 6.5 %collective-permute-start.22 = (f32[4,128,128]{2,1,0:T(8,128)S(1)}, f32[4,128,128]{2,1,0:T(8,128)S(1)}, u32[]{:S(2)}, u32[]{:S(2)}) collective-permute-start(f32[4,128,128]{2,1,0:T(8,128)S(1)} %select_bitcast_fusion.1), channel_id=1, source_target_pairs={{0,2},{1,17},{2,4},{3,19},{4,6},{5,21},{6,8},{7,23},{8,10},{9,25},... | collective-permute-start | bytes 786440 | tf_op jit(solution)/shard_map/ppermute | solution.py:220
  88.5 20.0 %collective-permute-start.27 = (f32[2,9,32,128]{3,2,1,0:T(8,128)S(1)}, f32[2,9,32,128]{3,2,1,0:T(8,128)S(1)}, u32[]{:S(2)}, u32[]{:S(2)}) collective-permute-start(f32[2,9,32,128]{3,2,1,0:T(8,128)S(1)} %slice_bitcast_fusion.1), channel_id=1, source_target_pairs={{0,192},{1,65},{64,128},{65,1},{128,64},{129,193},{192,0},{193,129... | collective-permute-start | bytes 884744 | tf_op jit(solution)/shard_map/ppermute | solution.py:247
  90.1 18.5 %collective-permute-start.28 = (f32[2,2,8,32,128]{4,3,2,1,0:T(8,128)S(1)}, f32[2,2,8,32,128]{4,3,2,1,0:T(8,128)S(1)}, u32[]{:S(2)}, u32[]{:S(2)}) collective-permute-start(f32[2,2,8,32,128]{4,3,2,1,0:T(8,128)S(1)} %get-tuple-element.101), channel_id=1, source_target_pairs={{0,64},{1,193},{64,0},{65,129},{128,192},{129,65},{192,128},{193,1... | collective-permute-start | bytes 1572872 | tf_op jit(solution)/shard_map/ppermute | solution.py:243
  92.7 15.9 %collective-permute-start.26 = (f32[12,32,128]{2,1,0:T(8,128)S(1)}, f32[12,32,128]{2,1,0:T(8,128)S(1)}, u32[]{:S(2)}, u32[]{:S(2)}) collective-permute-start(f32[12,32,128]{2,1,0:T(8,128)S(1)} %fusion.2), channel_id=1, source_target_pairs={{0,1},{1,0},{2,3},{3,2},{4,5},{5,4},{6,7},{7,6},{8,9},{9,8},{10,11... | collective-permute-start | bytes 589832 | tf_op jit(solution)/shard_map/ppermute | solution.py:208
  108.7 9.3 %collective-permute-start.30 = (f32[2,8,32,128]{3,2,1,0:T(8,128)S(1)}, f32[2,8,32,128]{3,2,1,0:T(8,128)S(1)}, u32[]{:S(2)}, u32[]{:S(2)}) collective-permute-start(f32[2,8,32,128]{3,2,1,0:T(8,128)S(1)} %slice_bitcast_fusion.2), channel_id=1, source_target_pairs={{0,192},{1,65},{64,128},{65,1},{128,64},{129,193},{192,0},{193,129... | collective-permute-start | bytes 786440 | tf_op jit(solution)/shard_map/ppermute | solution.py:247
  110.2 7.8 %collective-permute-start.31 = (f32[2,2,3,32,128]{4,3,2,1,0:T(8,128)S(1)}, f32[2,2,3,32,128]{4,3,2,1,0:T(8,128)S(1)}, u32[]{:S(2)}, u32[]{:S(2)}) collective-permute-start(f32[2,2,3,32,128]{4,3,2,1,0:T(8,128)S(1)} %get-tuple-element.115), channel_id=1, source_target_pairs={{0,64},{1,193},{64,0},{65,129},{128,192},{129,65},{192,128},{193,1... | collective-permute-start | bytes 589832 | tf_op jit(solution)/shard_map/ppermute | solution.py:243
  118.9 6.7 %collective-permute-start.33 = (f32[2,3,32,128]{3,2,1,0:T(8,128)S(1)}, f32[2,3,32,128]{3,2,1,0:T(8,128)S(1)}, u32[]{:S(2)}, u32[]{:S(2)}) collective-permute-start(f32[2,3,32,128]{3,2,1,0:T(8,128)S(1)} %slice_bitcast_fusion.12), channel_id=1, source_target_pairs={{0,192},{1,65},{64,128},{65,1},{128,64},{129,193},{192,0},{193,129... | collective-permute-start | bytes 294920 | tf_op jit(solution)/shard_map/ppermute | solution.py:247
  120.7 10.0 %collective-permute-start.32 = (f32[8,32,128]{2,1,0:T(8,128)S(1)}, f32[8,32,128]{2,1,0:T(8,128)S(1)}, u32[]{:S(2)}, u32[]{:S(2)}) collective-permute-start(f32[8,32,128]{2,1,0:T(8,128)S(1)} %fusion.4), channel_id=1, source_target_pairs={{0,1},{1,0},{2,3},{3,2},{4,5},{5,4},{6,7},{7,6},{8,9},{9,8},{10,11... | collective-permute-start | bytes 393224 | tf_op jit(solution)/shard_map/ppermute | solution.py:208
  (21 other events, 288.2 us)

commit v3 on v2

--- a/solution.py
+++ b/solution.py
@@ -22,19 +22,20 @@
     k1b=([(-1, 1), (1, 1)], [(1, -1), (1, 1)]),
     k2f=([(-1, -2), (1, -2), (2, -1)], [(-1, -2), (-1, 2), (-2, -1)]),
     k2b=([(-1, 2), (1, 2), (2, 1)], [(1, -2), (1, 2), (2, 1)]),
-    k3f=([(-1, -3), (1, -3), (2, -2)], [(-1, -3), (-1, 3), (-2, -2)]),
-    k3b=([(-1, 3), (1, 3), (2, 2)], [(1, -3), (1, 3), (2, 2)]),
+    k3f=([(-1, -3), (1, -3), (2, -2)], [(-1, 3), (-2, -2), (-1, -3)]),
+    k3b=([(-1, 3), (1, 3), (2, 2)], [(1, -3), (2, 2), (1, 3)]),
     k4f=([(2, -3)], [(-2, -3)]),
     k4b=([(2, 3)], [(2, 3)]),
 )
 BATCHES = (
     ("own", "zf1", "zb1", "xf1", "xb1", "zf2", "zb2", "x2", "k1f", "k1b"),
-    ("zf3", "zb3", "k2f", "k2b", "z4"),
+    ("zf3", "zb3", "z4", "k2f", "k2b"),
     ("k3f", "k3b", "df1", "db1"),
     ("k4f", "k4b", "d2"),
 )
 
-LIMITS = (60, 12, 12, 12)
+EARLY = ("own", "zf1", "zb1", "xf1", "xb1", "x2")
+LIMITS = (12, 12, 12, 12)
 
 
 def slots_of(names):
@@ -166,9 +167,14 @@
 ANY = pl.BlockSpec(memory_space=pl.ANY)
 
 
+def in_hbm(array):
+    return pltpu.with_memory_space_constraint(array, pltpu.HBM)
+
+
 def work(limit, names, pos, inverse, side_own, side_sib, blocks, blocks_sib, got):
     n = sum(width(name) for name in names)
-    arrays = [got[name] for name in names]
+    arrays = [in_hbm(got[name]) if name in EARLY else got[name] for name in names]
+    blocks, blocks_sib = in_hbm(blocks), in_hbm(blocks_sib)
     piece = jax.ShapeDtypeStruct((2, 2, n, N // NM, N), jnp.float32)
     return pl.pallas_call(
         functools.partial(work_kernel, names),
@@ -248,6 +254,15 @@
     return sums[0, 0], got[0], sums[0, 1] + got[1]
 
 
+def direct(parts):
+    send, keep = parts
+    one = lax.ppermute(send[0], ("m", "c"), hops(1, 3))
+    two = lax.ppermute(send[1], ("m", "c"), hops(2, 2))
+    three = lax.ppermute(keep[1], ("m", "c"), hops(3, 1))
+    here, there = keep[0] + one, two + three
+    return here[0], there[0], here[1] + there[1]
+
+
 def swap(terms):
     return terms[0], terms[1], shift(terms[2], "c", 1)
 
@@ -307,17 +322,18 @@
         k2b=by_core(pick(jnp.stack([k1b[0], k1b[1], x2]), jnp.stack([zf2, zb2, k1b[1]])), -1),
     )
     got["a"] = run(0)
-    tie("zf3", "zb3", "k2f", "k2b", "a")
-
-    zf3, zb3, k2f, k2b = (got[name] for name in ("zf3", "zb3", "k2f", "k2b"))
+    tie("zf3", "zb3", "a")
+    zf3, zb3 = got["zf3"], got["zb3"]
     arrive(z4=by_core_far(pick(zf3, zb3), "z"))
+    tie("k2f", "k2b", "z4")
+
+    k2f, k2b, z4 = (got[name] for name in ("k2f", "k2b", "z4"))
+    arrive(df1=shift(z4, "x", 1), db1=shift(z4, "x", -1))
     arrive(
-        k3f=by_core(pick(k2f, jnp.stack([zf3, zb3, k2f[0]])), 1),
-        k3b=by_core(pick(k2b, jnp.stack([zf3, zb3, k2b[1]])), -1),
+        k3f=by_core(pick(k2f, jnp.stack([zb3, k2f[0], zf3])), 1),
+        k3b=by_core(pick(k2b, jnp.stack([zf3, k2b[1], zb3])), -1),
     )
     a = halve(got["a"])
-    tie("z4")
-    arrive(df1=shift(got["z4"], "x", 1), db1=shift(got["z4"], "x", -1))
     b = run(1)
     got["done"] = a, b
     tie("df1", "db1", "k3f", "k3b", "done")
@@ -325,27 +341,23 @@
     k3f, k3b = got["k3f"], got["k3b"]
     a, b = got["done"]
     arrive(d2=shift(got["df1"], "x", 1))
-    arrive(k4f=by_core(pick(k3f[2], k3f[0]), 1), k4b=by_core(pick(k3b[2], k3b[1]), -1))
+    arrive(k4f=by_core(k3f[2], 1), k4b=by_core(k3b[2], -1))
     d = run(2)
-    a = quarter(a)
     b = halve(b)
-    got["done"] = a, b, d
+    got["done"] = b, d
     tie("d2", "k4f", "k4b", "done")
 
-    a, b, d = got["done"]
+    b, d = got["done"]
     e = run(3)
     d = halve(d)
+    a = quarter(a)
+    a, d, e = fence((a, d, e))
+
+    e = direct(e)
     b = quarter(b)
-    a = swap(a)
+    d = quarter(d)
     a, b, d, e = fence((a, b, d, e))
-
-    e = halve(e)
-    d = quarter(d)
-    b = swap(b)
-    b, d, e = fence((b, d, e))
-
-    e = swap(quarter(e))
-    d = swap(d)
+    a, b, d, e = (swap(part) for part in (a, b, d, e))
     return finish(BATCHES, pos, inverse, a + b + d + e)
 
 

time: 134 us -> 126 us (0.940)
  starting transfers between devices: 74.3 us -> 47.8 us
  waiting for transfers between devices: 19.6 us -> 39.2 us
  Pallas kernels: 29 us -> 26.9 us
  other arithmetic: 8.93 us -> 10.4 us
    ppermute x18, starting transfers between devices: 49.1 us -> 23.8 us  [shift(): lax.ppermute(array, axis, [(i, (i + step) % size) for i in range(size)])]
    ppermute x4 -> x3, waiting for transfers between devices: 0.43 us -> 11.5 us  [halve(): return keep + lax.ppermute(send, ('m', 'c'), hops(1, 3))]
    ppermute x18, waiting for transfers between devices: 9.79 us -> 18.7 us  [shift(): lax.ppermute(array, axis, [(i, (i + step) % size) for i in range(size)])]
    ppermute x0 -> x3, waiting for transfers between devices: none -> 4.16 us  [the longest x1 1.98 us: direct(): two = lax.ppermute(send[1], ('m', 'c'), hops(2, 2))]
    ppermute x0 -> x3, starting transfers between devices: none -> 4.02 us  [the longest x1 2.26 us: direct(): two = lax.ppermute(send[1], ('m', 'c'), hops(2, 2))]
    ppermute x1, waiting for transfers between devices: 6.25 us -> 2.3 us  [by_core_far(): return lax.ppermute(array, TENSOR, pairs)]
    ppermute x4 -> x3, starting transfers between devices: 4.87 us -> 1.48 us  [quarter(): got = lax.ppermute(sums[1], ('m', 'c'), hops(3, 1))]
    ppermute x8, waiting for transfers between devices: 3.13 us -> 0.02 us  [by_core(): return lax.ppermute(array, TENSOR, pairs)]
  transfers between devices with their start and end apart: 35 -> 36, of which waited for: 8 -> 15; matrix products, arithmetic and copies ran while one was open for 5% -> 6% of each run, Pallas kernels for 20% -> 20%
where the time goes in v3:
time: 126 us
  starting transfers between devices  47.8 us (38%)
  waiting for transfers between devices  39.2 us (31%)
  Pallas kernels  26.9 us (21%)
  other arithmetic  10.4 us (8%)
    pallas_call x4, Pallas kernels, work(): pl.pallas_call(functools.partial(work_kernel, names), out_shape=(piece,)...  25.1 us
    ppermute x18, starting transfers between devices, shift(): lax.ppermute(array, axis, [(i, (i + step) % size) for i in range(size)])  23.8 us
    ppermute x18, waiting for transfers between devices, shift(): lax.ppermute(array, axis, [(i, (i + step) % size) for i in range(size)])  18.7 us
    ppermute x3, waiting for transfers between devices, halve(): return keep + lax.ppermute(send, ('m', 'c'), hops(1, 3))  11.5 us
    ppermute x8, starting transfers between devices, by_core(): return lax.ppermute(array, TENSOR, pairs)  10.6 us
    ppermute x3, starting transfers between devices, halve(): return keep + lax.ppermute(send, ('m', 'c'), hops(1, 3))  6.55 us
    select_n x4, other arithmetic, pick(): return jnp.where(first, one, two)  4.78 us
  transfers between devices with their start and end apart: 36, of which 15 were waited for; matrix products, arithmetic and copies ran while one was open for 6% of the time, Pallas kernels for 20%

profile of v3, /device:TPU:1, one launch (start us, length us, event | category | flops | bytes accessed | tf_op | source)
XLA Modules:
  0.0 125.6 jit_solution(1028804770379186881)
XLA Ops:
  0.0 3.2 %collective-permute-start.4 = (f32[64,128,128]{2,1,0:T(8,128)}, f32[64,128,128]{2,1,0:T(8,128)}, u32[]{:S(2)}, u32[]{:S(2)}) collective-permute-start(f32[64,128,128]{2,1,0:T(8,128)} %blocks.7), channel_id=1, source_target_pairs={{0,1},{1,0},{2,3},{3,2},{4,5},{5,4},{6,7},{7,6},{8,9},{9,8},{10,11... | collective-permute-start | bytes 12582920 | tf_op jit(solution)/shard_map/ppermute | solution.py:214
  6.5 4.9 %collective-permute-start.1 = (f32[4,128,128]{2,1,0:T(8,128)S(1)}, f32[4,128,128]{2,1,0:T(8,128)S(1)}, u32[]{:S(2)}, u32[]{:S(2)}) collective-permute-start(f32[4,128,128]{2,1,0:T(8,128)S(1)} %bitcast_select_fusion.1.rest_0_), channel_id=1, source_target_pairs={{0,14},{2,0},{4,2},{6,4},{8,6},{10,8},{12,10},{14,12},{1,15},{3,1}... | collective-permute-start | bytes 786440 | tf_op jit(solution)/shard_map/ppermute | solution.py:214
  16.8 3.1 %collective-permute-done.rest_1_ = f32[4,128,128]{2,1,0:T(8,128)S(1)} collective-permute-done((f32[4,128,128]{2,1,0:T(8,128)S(1)}, f32[4,128,128]{2,1,0:T(8,128)S(1)}, u32[]{:S(2)}, u32[]{:S(2)}) %collective-permute-start) | collective-permute-done | bytes 262176 | tf_op jit(solution)/shard_map/ppermute | solution.py:214
  19.9 1.4 %collective-permute-start.7 = (f32[520,128]{1,0:T(8,128)S(1)}, f32[520,128]{1,0:T(8,128)S(1)}, u32[]{:S(2)}, u32[]{:S(2)}) collective-permute-start(f32[520,128]{1,0:T(8,128)S(1)} %pad_maximum_fusion.3.side_own), channel_id=1, source_target_pairs={{0,1},{1,0},{2,3},{3,2},{4,5},{5,4},{6,7},{7,6},{8,9},{9,8},{10,11... | collective-permute-start | bytes 798728 | tf_op jit(solution)/shard_map/ppermute | solution.py:214
  21.4 2.8 %collective-permute-start.10 = (f32[2,4,128,128]{3,2,1,0:T(8,128)S(1)}, f32[2,4,128,128]{3,2,1,0:T(8,128)S(1)}, u32[]{:S(2)}, u32[]{:S(2)}) collective-permute-start(f32[2,4,128,128]{3,2,1,0:T(8,128)S(1)} %maximum_select_fusion.2), channel_id=1, source_target_pairs={{0,14},{1,49},{2,0},{3,51},{4,2},{5,53},{6,4},{7,55},{8,6},{9,57},... | collective-permute-start | bytes 1572872 | tf_op jit(solution)/shard_map/ppermute | solution.py:226
  24.1 2.7 %collective-permute-start.6 = (f32[4,128,128]{2,1,0:T(8,128)S(1)}, f32[4,128,128]{2,1,0:T(8,128)}, u32[]{:S(2)}, u32[]{:S(2)}) collective-permute-start(f32[4,128,128]{2,1,0:T(8,128)S(1)} %collective-permute-done.1.rest_2_), channel_id=1, source_target_pairs={{0,14},{2,0},{4,2},{6,4},{8,6},{10,8},{12,10},{14,12},{1,15},{3,1}... | collective-permute-start | bytes 786440 | tf_op jit(solution)/shard_map/ppermute | solution.py:214
  26.8 2.7 %collective-permute-start.8 = (f32[4,128,128]{2,1,0:T(8,128)S(1)}, f32[4,128,128]{2,1,0:T(8,128)S(1)}, u32[]{:S(2)}, u32[]{:S(2)}) collective-permute-start(f32[4,128,128]{2,1,0:T(8,128)S(1)} %collective-permute-done.3.rest_4_), channel_id=1, source_target_pairs={{0,48},{16,0},{32,16},{48,32},{1,49},{17,1},{33,17},{49,33},{2,50}... | collective-permute-start | bytes 786440 | tf_op jit(solution)/shard_map/ppermute | solution.py:214
  29.5 4.2 %collective-permute-done.5.rest_5_ = f32[4,128,128]{2,1,0:T(8,128)} collective-permute-done((f32[4,128,128]{2,1,0:T(8,128)S(1)}, f32[4,128,128]{2,1,0:T(8,128)}, u32[]{:S(2)}, u32[]{:S(2)}) %collective-permute-start.5) | collective-permute-done | bytes 262176 | tf_op jit(solution)/shard_map/ppermute | solution.py:214
  33.8 1.9 %collective-permute-done.8.rest_7_ = f32[4,128,128]{2,1,0:T(8,128)S(1)} collective-permute-done((f32[4,128,128]{2,1,0:T(8,128)S(1)}, f32[4,128,128]{2,1,0:T(8,128)S(1)}, u32[]{:S(2)}, u32[]{:S(2)}) %collective-permute-start.8) | collective-permute-done | bytes 262176 | tf_op jit(solution)/shard_map/ppermute | solution.py:214
  35.7 2.4 %fusion.1 = (f32[3,4,128,128]{3,2,1,0:T(8,128)}, f32[3,4,128,128]{3,2,1,0:T(8,128)}) fusion(f32[1,4,128,128]{3,2,1,0:T(8,128)S(1)} %bitcast.79, f32[2,4,128,128]{3,2,1,0:T(8,128)S(1)} %collective-permute-done.10.rest_9_, f32[1,4,128,128]{3,2,1,0:T(8,128)S(1)} %slice.94, f32[1,4,128,128]{3,2,1,0:T(8,128)} %bitcast.16, f32[1,4,128,128]{3,2,1,0:T(8,128)} %bitcast.15, ...), kind=kLoop, calls=%fused_computation.3 | loop fusion | flops 1376256 | bytes 3932161 | tf_op jit(solution)/shard_map/jit(_where)/select_n | solution.py:277
  38.2 3.5 %collective-permute-start.12 = (f32[3,4,128,128]{3,2,1,0:T(8,128)}, f32[3,4,128,128]{3,2,1,0:T(8,128)S(1)}, u32[]{:S(2)}, u32[]{:S(2)}) collective-permute-start(f32[3,4,128,128]{3,2,1,0:T(8,128)} %get-tuple-element.123), channel_id=1, source_target_pairs={{0,14},{1,49},{2,0},{3,51},{4,2},{5,53},{6,4},{7,55},{8,6},{9,57},... | collective-permute-start | bytes 2359304 | tf_op jit(solution)/shard_map/ppermute | solution.py:226
  41.9 2.7 %collective-permute-start.14 = (f32[4,128,128]{2,1,0:T(8,128)}, f32[4,128,128]{2,1,0:T(8,128)}, u32[]{:S(2)}, u32[]{:S(2)}) collective-permute-start(f32[4,128,128]{2,1,0:T(8,128)} %collective-permute-done.6.rest_6_), channel_id=1, source_target_pairs={{0,14},{2,0},{4,2},{6,4},{8,6},{10,8},{12,10},{14,12},{1,15},{3,1}... | collective-permute-start | bytes 786440 | tf_op jit(solution)/shard_map/ppermute | solution.py:214
  44.6 8.4 %work.4 = (f32[2,2,12,32,128]{4,3,2,1,0:T(8,128)S(1)}, f32[2,2,12,32,128]{4,3,2,1,0:T(8,128)S(1)}) custom-call(s32[4]{0:T(128)S(1)} %pad_add_fusion.pos, s32[64]{0:T(128)S(1)} %select_reduce_fusion.2.inverse, f32[520,128]{1,0:T(8,128)S(1)} %pad_maximum_fusion.3.side_own, f32[520,128]{1,0:T(8,128)S(1)} %collective-permute-done.7.side_sib, ...), custom_call_target="tpu_custom_call" | custom-call | tf_op jit(solution)/shard_map/work/pallas_call | solution.py:179
  55.4 2.7 %collective-permute-start.20 = (f32[2,2,12,32,128]{4,3,2,1,0:T(8,128)S(1)}, f32[2,2,12,32,128]{4,3,2,1,0:T(8,128)S(1)}, u32[]{:S(2)}, u32[]{:S(2)}) collective-permute-start(f32[2,2,12,32,128]{4,3,2,1,0:T(8,128)S(1)} %get-tuple-element.85), channel_id=1, source_target_pairs={{0,64},{1,193},{64,0},{65,129},{128,192},{129,65},{192,128},{193,1... | collective-permute-start | bytes 2359304 | tf_op jit(solution)/shard_map/ppermute | solution.py:249
  58.2 2.3 %collective-permute-done.15.rest_2_ = f32[4,128,128]{2,1,0:T(8,128)S(1)} collective-permute-done((f32[4,128,128]{2,1,0:T(8,128)S(1)}, f32[4,128,128]{2,1,0:T(8,128)S(1)}, u32[]{:S(2)}, u32[]{:S(2)}) %collective-permute-start.15) | collective-permute-done | bytes 262176 | tf_op jit(solution)/shard_map/ppermute | solution.py:236
  61.8 2.7 %collective-permute-start.19 = (f32[3,4,128,128]{3,2,1,0:T(8,128)S(1)}, f32[3,4,128,128]{3,2,1,0:T(8,128)S(1)}, u32[]{:S(2)}, u32[]{:S(2)}) collective-permute-start(f32[3,4,128,128]{3,2,1,0:T(8,128)S(1)} %get-tuple-element.125), channel_id=1, source_target_pairs={{0,14},{1,49},{2,0},{3,51},{4,2},{5,53},{6,4},{7,55},{8,6},{9,57},... | collective-permute-start | bytes 2359304 | tf_op jit(solution)/shard_map/ppermute | solution.py:226
  64.5 2.7 %collective-permute-start.17 = (f32[4,128,128]{2,1,0:T(8,128)S(1)}, f32[4,128,128]{2,1,0:T(8,128)S(1)}, u32[]{:S(2)}, u32[]{:S(2)}) collective-permute-start(f32[4,128,128]{2,1,0:T(8,128)S(1)} %collective-permute-done.15.rest_2_), channel_id=1, source_target_pairs={{0,48},{16,0},{32,16},{48,32},{1,49},{17,1},{33,17},{49,33},{2,50}... | collective-permute-start | bytes 786440 | tf_op jit(solution)/shard_map/ppermute | solution.py:214
  67.2 6.8 %work.5 = (f32[2,2,9,32,128]{4,3,2,1,0:T(8,128)S(1)}, f32[2,2,9,32,128]{4,3,2,1,0:T(8,128)S(1)}) custom-call(s32[4]{0:T(128)S(1)} %pad_add_fusion.pos, s32[64]{0:T(128)S(1)} %select_reduce_fusion.2.inverse, f32[520,128]{1,0:T(8,128)S(1)} %pad_maximum_fusion.3.side_own, f32[520,128]{1,0:T(8,128)S(1)} %collective-permute-done.7.side_sib, ...), custom_call_target="tpu_custom_call" | custom-call | tf_op jit(solution)/shard_map/work/pallas_call | solution.py:179
  74.1 3.9 %collective-permute-done.17.rest_3_ = f32[4,128,128]{2,1,0:T(8,128)S(1)} collective-permute-done((f32[4,128,128]{2,1,0:T(8,128)S(1)}, f32[4,128,128]{2,1,0:T(8,128)S(1)}, u32[]{:S(2)}, u32[]{:S(2)}) %collective-permute-start.17) | collective-permute-done | bytes 262176 | tf_op jit(solution)/shard_map/ppermute | solution.py:214
  78.1 3.1 %collective-permute-done.16.rest_2_ = f32[4,128,128]{2,1,0:T(8,128)S(1)} collective-permute-done((f32[4,128,128]{2,1,0:T(8,128)S(1)}, f32[4,128,128]{2,1,0:T(8,128)S(1)}, u32[]{:S(2)}, u32[]{:S(2)}) %collective-permute-start.16) | collective-permute-done | bytes 262176 | tf_op jit(solution)/shard_map/ppermute | solution.py:214
  82.6 1.9 %collective-permute-start.25 = (f32[2,2,9,32,128]{4,3,2,1,0:T(8,128)S(1)}, f32[2,2,9,32,128]{4,3,2,1,0:T(8,128)S(1)}, u32[]{:S(2)}, u32[]{:S(2)}) collective-permute-start(f32[2,2,9,32,128]{4,3,2,1,0:T(8,128)S(1)} %get-tuple-element.93), channel_id=1, source_target_pairs={{0,64},{1,193},{64,0},{65,129},{128,192},{129,65},{192,128},{193,1... | collective-permute-start | bytes 1769480 | tf_op jit(solution)/shard_map/ppermute | solution.py:249
  86.2 6.2 %work.6 = (f32[2,2,8,32,128]{4,3,2,1,0:T(8,128)S(1)}, f32[2,2,8,32,128]{4,3,2,1,0:T(8,128)S(1)}) custom-call(s32[4]{0:T(128)S(1)} %pad_add_fusion.pos, s32[64]{0:T(128)S(1)} %select_reduce_fusion.2.inverse, f32[520,128]{1,0:T(8,128)S(1)} %pad_maximum_fusion.3.side_own, f32[520,128]{1,0:T(8,128)S(1)} %collective-permute-done.7.side_sib, ...), custom_call_target="tpu_custom_call" | custom-call | tf_op jit(solution)/shard_map/work/pallas_call | solution.py:179
  92.4 4.7 %collective-permute-done.25 = f32[2,2,9,32,128]{4,3,2,1,0:T(8,128)S(1)} collective-permute-done((f32[2,2,9,32,128]{4,3,2,1,0:T(8,128)S(1)}, f32[2,2,9,32,128]{4,3,2,1,0:T(8,128)S(1)}, u32[]{:S(2)}, u32[]{:S(2)}) %collective-permute-start.25) | collective-permute-done | bytes 589856 | tf_op jit(solution)/shard_map/ppermute | solution.py:249
  97.4 1.9 %collective-permute-start.26 = (f32[2,2,8,32,128]{4,3,2,1,0:T(8,128)S(1)}, f32[2,2,8,32,128]{4,3,2,1,0:T(8,128)S(1)}, u32[]{:S(2)}, u32[]{:S(2)}) collective-permute-start(f32[2,2,8,32,128]{4,3,2,1,0:T(8,128)S(1)} %get-tuple-element.98), channel_id=1, source_target_pairs={{0,64},{1,193},{64,0},{65,129},{128,192},{129,65},{192,128},{193,1... | collective-permute-start | bytes 1572872 | tf_op jit(solution)/shard_map/ppermute | solution.py:249
  99.3 3.6 %work.7 = (f32[2,2,3,32,128]{4,3,2,1,0:T(8,128)S(1)}, f32[2,2,3,32,128]{4,3,2,1,0:T(8,128)S(1)}) custom-call(s32[4]{0:T(128)S(1)} %pad_add_fusion.pos, s32[64]{0:T(128)S(1)} %select_reduce_fusion.2.inverse, f32[520,128]{1,0:T(8,128)S(1)} %pad_maximum_fusion.3.side_own, f32[520,128]{1,0:T(8,128)S(1)} %collective-permute-done.7.side_sib, ...), custom_call_target="tpu_custom_call" | custom-call | tf_op jit(solution)/shard_map/work/pallas_call | solution.py:179
  103.3 6.8 %collective-permute-done.26 = f32[2,2,8,32,128]{4,3,2,1,0:T(8,128)S(1)} collective-permute-done((f32[2,2,8,32,128]{4,3,2,1,0:T(8,128)S(1)}, f32[2,2,8,32,128]{4,3,2,1,0:T(8,128)S(1)}, u32[]{:S(2)}, u32[]{:S(2)}) %collective-permute-start.26) | collective-permute-done | bytes 524320 | tf_op jit(solution)/shard_map/ppermute | solution.py:249
  110.3 1.7 %collective-permute-start.29 = (f32[2,3,32,128]{3,2,1,0:T(8,128)S(1)}, f32[2,3,32,128]{3,2,1,0:T(8,128)S(1)}, u32[]{:S(2)}, u32[]{:S(2)}) collective-permute-start(f32[2,3,32,128]{3,2,1,0:T(8,128)S(1)} %get-tuple-element.128), channel_id=1, source_target_pairs={{0,64},{1,193},{64,0},{65,129},{128,192},{129,65},{192,128},{193,1... | collective-permute-start | bytes 294920 | tf_op jit(solution)/shard_map/ppermute | solution.py:259
  112.0 2.3 %collective-permute-start.30 = (f32[2,3,32,128]{3,2,1,0:T(8,128)S(1)}, f32[2,3,32,128]{3,2,1,0:T(8,128)S(1)}, u32[]{:S(2)}, u32[]{:S(2)}) collective-permute-start(f32[2,3,32,128]{3,2,1,0:T(8,128)S(1)} %get-tuple-element.127), channel_id=1, source_target_pairs={{0,128},{1,129},{64,192},{65,193},{128,0},{129,1},{192,64},{193,65... | collective-permute-start | bytes 294920 | tf_op jit(solution)/shard_map/ppermute | solution.py:260
  114.3 2.0 %collective-permute-done.29 = f32[2,3,32,128]{3,2,1,0:T(8,128)S(1)} collective-permute-done((f32[2,3,32,128]{3,2,1,0:T(8,128)S(1)}, f32[2,3,32,128]{3,2,1,0:T(8,128)S(1)}, u32[]{:S(2)}, u32[]{:S(2)}) %collective-permute-start.29) | collective-permute-done | bytes 98336 | tf_op jit(solution)/shard_map/ppermute | solution.py:259
  116.5 2.0 %collective-permute-done.30 = f32[2,3,32,128]{3,2,1,0:T(8,128)S(1)} collective-permute-done((f32[2,3,32,128]{3,2,1,0:T(8,128)S(1)}, f32[2,3,32,128]{3,2,1,0:T(8,128)S(1)}, u32[]{:S(2)}, u32[]{:S(2)}) %collective-permute-start.30) | collective-permute-done | bytes 98336 | tf_op jit(solution)/shard_map/ppermute | solution.py:260
  118.5 2.2 %collective-permute-done.28 = f32[2,8,32,128]{3,2,1,0:T(8,128)S(1)} collective-permute-done((f32[2,8,32,128]{3,2,1,0:T(8,128)S(1)}, f32[2,8,32,128]{3,2,1,0:T(8,128)S(1)}, u32[]{:S(2)}, u32[]{:S(2)}) %collective-permute-start.28) | collective-permute-done | bytes 262176 | tf_op jit(solution)/shard_map/ppermute | solution.py:253
  123.8 1.8 %finish.1 = f32[64,32,128]{2,1,0:T(8,128)} custom-call(s32[4]{0:T(128)S(1)} %pad_add_fusion.pos, s32[64]{0:T(128)S(1)} %select_reduce_fusion.2.inverse, f32[12,32,128]{2,1,0:T(8,128)S(1)} %slice_bitcast_fusion.7.rest_0_, f32[12,32,128]{2,1,0:T(8,128)S(1)} %slice_bitcast_fusion.6.rest_1_, f32[12,32,128]{2,1,0:T(8,128)S(1)} %collective-permute-done.32.rest_2_, ...), custom_call_target="tpu_custom_call" | custom-call | tf_op jit(solution)/shard_map/finish/pallas_call | solution.py:202
  (101 shorter events, 19.3 us)
Async XLA Ops:
  0.0 19.9 %collective-permute-start.4 = (f32[64,128,128]{2,1,0:T(8,128)}, f32[64,128,128]{2,1,0:T(8,128)}, u32[]{:S(2)}, u32[]{:S(2)}) collective-permute-start(f32[64,128,128]{2,1,0:T(8,128)} %blocks.7), channel_id=1, source_target_pairs={{0,1},{1,0},{2,3},{3,2},{4,5},{5,4},{6,7},{7,6},{8,9},{9,8},{10,11... | collective-permute-start | bytes 12582920 | tf_op jit(solution)/shard_map/ppermute | solution.py:214
  5.0 10.5 %collective-permute-start.3 = (f32[4,128,128]{2,1,0:T(8,128)S(1)}, f32[4,128,128]{2,1,0:T(8,128)S(1)}, u32[]{:S(2)}, u32[]{:S(2)}) collective-permute-start(f32[4,128,128]{2,1,0:T(8,128)S(1)} %bitcast_select_fusion.1.rest_0_), channel_id=1, source_target_pairs={{0,48},{16,0},{32,16},{48,32},{1,49},{17,1},{33,17},{49,33},{2,50}... | collective-permute-start | bytes 786440 | tf_op jit(solution)/shard_map/ppermute | solution.py:214
  5.8 9.7 %collective-permute-start.2 = (f32[4,128,128]{2,1,0:T(8,128)S(1)}, f32[4,128,128]{2,1,0:T(8,128)S(1)}, u32[]{:S(2)}, u32[]{:S(2)}) collective-permute-start(f32[4,128,128]{2,1,0:T(8,128)S(1)} %bitcast_select_fusion.1.rest_0_), channel_id=1, source_target_pairs={{0,16},{16,32},{32,48},{48,0},{1,17},{17,33},{33,49},{49,1},{2,18}... | collective-permute-start | bytes 786440 | tf_op jit(solution)/shard_map/ppermute | solution.py:214
  6.5 10.3 %collective-permute-start.1 = (f32[4,128,128]{2,1,0:T(8,128)S(1)}, f32[4,128,128]{2,1,0:T(8,128)S(1)}, u32[]{:S(2)}, u32[]{:S(2)}) collective-permute-start(f32[4,128,128]{2,1,0:T(8,128)S(1)} %bitcast_select_fusion.1.rest_0_), channel_id=1, source_target_pairs={{0,14},{2,0},{4,2},{6,4},{8,6},{10,8},{12,10},{14,12},{1,15},{3,1}... | collective-permute-start | bytes 786440 | tf_op jit(solution)/shard_map/ppermute | solution.py:214
  11.4 8.5 %collective-permute-start = (f32[4,128,128]{2,1,0:T(8,128)S(1)}, f32[4,128,128]{2,1,0:T(8,128)S(1)}, u32[]{:S(2)}, u32[]{:S(2)}) collective-permute-start(f32[4,128,128]{2,1,0:T(8,128)S(1)} %bitcast_select_fusion.1.rest_0_), channel_id=1, source_target_pairs={{0,2},{2,4},{4,6},{6,8},{8,10},{10,12},{12,14},{14,0},{1,3},{3,5},... | collective-permute-start | bytes 786440 | tf_op jit(solution)/shard_map/ppermute | solution.py:214
  19.9 6.9 %collective-permute-start.7 = (f32[520,128]{1,0:T(8,128)S(1)}, f32[520,128]{1,0:T(8,128)S(1)}, u32[]{:S(2)}, u32[]{:S(2)}) collective-permute-start(f32[520,128]{1,0:T(8,128)S(1)} %pad_maximum_fusion.3.side_own), channel_id=1, source_target_pairs={{0,1},{1,0},{2,3},{3,2},{4,5},{5,4},{6,7},{7,6},{8,9},{9,8},{10,11... | collective-permute-start | bytes 798728 | tf_op jit(solution)/shard_map/ppermute | solution.py:214
  21.4 12.4 %collective-permute-start.10 = (f32[2,4,128,128]{3,2,1,0:T(8,128)S(1)}, f32[2,4,128,128]{3,2,1,0:T(8,128)S(1)}, u32[]{:S(2)}, u32[]{:S(2)}) collective-permute-start(f32[2,4,128,128]{3,2,1,0:T(8,128)S(1)} %maximum_select_fusion.2), channel_id=1, source_target_pairs={{0,14},{1,49},{2,0},{3,51},{4,2},{5,53},{6,4},{7,55},{8,6},{9,57},... | collective-permute-start | bytes 1572872 | tf_op jit(solution)/shard_map/ppermute | solution.py:226
  24.1 9.6 %collective-permute-start.9 = (f32[2,4,128,128]{3,2,1,0:T(8,128)S(1)}, f32[2,4,128,128]{3,2,1,0:T(8,128)S(1)}, u32[]{:S(2)}, u32[]{:S(2)}) collective-permute-start(f32[2,4,128,128]{3,2,1,0:T(8,128)S(1)} %maximum_select_fusion.2), channel_id=1, source_target_pairs={{0,2},{1,17},{2,4},{3,19},{4,6},{5,21},{6,8},{7,23},{8,10},{9,25},... | collective-permute-start | bytes 1572872 | tf_op jit(solution)/shard_map/ppermute | solution.py:226
  24.1 9.6 %collective-permute-start.5 = (f32[4,128,128]{2,1,0:T(8,128)S(1)}, f32[4,128,128]{2,1,0:T(8,128)}, u32[]{:S(2)}, u32[]{:S(2)}) collective-permute-start(f32[4,128,128]{2,1,0:T(8,128)S(1)} %collective-permute-done.rest_1_), channel_id=1, source_target_pairs={{0,2},{2,4},{4,6},{6,8},{8,10},{10,12},{12,14},{14,0},{1,3},{3,5},... | collective-permute-start | bytes 786440 | tf_op jit(solution)/shard_map/ppermute | solution.py:214
  24.1 9.6 %collective-permute-start.6 = (f32[4,128,128]{2,1,0:T(8,128)S(1)}, f32[4,128,128]{2,1,0:T(8,128)}, u32[]{:S(2)}, u32[]{:S(2)}) collective-permute-start(f32[4,128,128]{2,1,0:T(8,128)S(1)} %collective-permute-done.1.rest_2_), channel_id=1, source_target_pairs={{0,14},{2,0},{4,2},{6,4},{8,6},{10,8},{12,10},{14,12},{1,15},{3,1}... | collective-permute-start | bytes 786440 | tf_op jit(solution)/shard_map/ppermute | solution.py:214
  26.8 8.9 %collective-permute-start.8 = (f32[4,128,128]{2,1,0:T(8,128)S(1)}, f32[4,128,128]{2,1,0:T(8,128)S(1)}, u32[]{:S(2)}, u32[]{:S(2)}) collective-permute-start(f32[4,128,128]{2,1,0:T(8,128)S(1)} %collective-permute-done.3.rest_4_), channel_id=1, source_target_pairs={{0,48},{16,0},{32,16},{48,32},{1,49},{17,1},{33,17},{49,33},{2,50}... | collective-permute-start | bytes 786440 | tf_op jit(solution)/shard_map/ppermute | solution.py:214
  38.2 22.3 %collective-permute-start.12 = (f32[3,4,128,128]{3,2,1,0:T(8,128)}, f32[3,4,128,128]{3,2,1,0:T(8,128)S(1)}, u32[]{:S(2)}, u32[]{:S(2)}) collective-permute-start(f32[3,4,128,128]{3,2,1,0:T(8,128)} %get-tuple-element.123), channel_id=1, source_target_pairs={{0,14},{1,49},{2,0},{3,51},{4,2},{5,53},{6,4},{7,55},{8,6},{9,57},... | collective-permute-start | bytes 2359304 | tf_op jit(solution)/shard_map/ppermute | solution.py:226
  41.7 18.8 %collective-permute-start.11 = (f32[3,4,128,128]{3,2,1,0:T(8,128)}, f32[3,4,128,128]{3,2,1,0:T(8,128)S(1)}, u32[]{:S(2)}, u32[]{:S(2)}) collective-permute-start(f32[3,4,128,128]{3,2,1,0:T(8,128)} %get-tuple-element.124), channel_id=1, source_target_pairs={{0,2},{1,17},{2,4},{3,19},{4,6},{5,21},{6,8},{7,23},{8,10},{9,25},... | collective-permute-start | bytes 2359304 | tf_op jit(solution)/shard_map/ppermute | solution.py:226
  41.8 11.3 %collective-permute-start.13 = (f32[4,128,128]{2,1,0:T(8,128)}, f32[4,128,128]{2,1,0:T(8,128)S(1)}, u32[]{:S(2)}, u32[]{:S(2)}) collective-permute-start(f32[4,128,128]{2,1,0:T(8,128)} %collective-permute-done.5.rest_5_), channel_id=1, source_target_pairs={{0,2},{2,4},{4,6},{6,8},{8,10},{10,12},{12,14},{14,0},{1,3},{3,5},... | collective-permute-start | bytes 786440 | tf_op jit(solution)/shard_map/ppermute | solution.py:214
  41.9 11.2 %collective-permute-start.14 = (f32[4,128,128]{2,1,0:T(8,128)}, f32[4,128,128]{2,1,0:T(8,128)}, u32[]{:S(2)}, u32[]{:S(2)}) collective-permute-start(f32[4,128,128]{2,1,0:T(8,128)} %collective-permute-done.6.rest_6_), channel_id=1, source_target_pairs={{0,14},{2,0},{4,2},{6,4},{8,6},{10,8},{12,10},{14,12},{1,15},{3,1}... | collective-permute-start | bytes 786440 | tf_op jit(solution)/shard_map/ppermute | solution.py:214
  54.1 6.4 %collective-permute-start.15 = (f32[4,128,128]{2,1,0:T(8,128)S(1)}, f32[4,128,128]{2,1,0:T(8,128)S(1)}, u32[]{:S(2)}, u32[]{:S(2)}) collective-permute-start(f32[4,128,128]{2,1,0:T(8,128)S(1)} %broadcast_select_fusion), channel_id=1, source_target_pairs={{0,2},{1,15},{2,4},{3,1},{4,6},{5,3},{6,8},{7,5},{8,10},{9,7},{10,... | collective-permute-start | bytes 786440 | tf_op jit(solution)/shard_map/ppermute | solution.py:236
  55.4 18.6 %collective-permute-start.20 = (f32[2,2,12,32,128]{4,3,2,1,0:T(8,128)S(1)}, f32[2,2,12,32,128]{4,3,2,1,0:T(8,128)S(1)}, u32[]{:S(2)}, u32[]{:S(2)}) collective-permute-start(f32[2,2,12,32,128]{4,3,2,1,0:T(8,128)S(1)} %get-tuple-element.85), channel_id=1, source_target_pairs={{0,64},{1,193},{64,0},{65,129},{128,192},{129,65},{192,128},{193,1... | collective-permute-start | bytes 2359304 | tf_op jit(solution)/shard_map/ppermute | solution.py:249
  61.8 19.4 %collective-permute-start.19 = (f32[3,4,128,128]{3,2,1,0:T(8,128)S(1)}, f32[3,4,128,128]{3,2,1,0:T(8,128)S(1)}, u32[]{:S(2)}, u32[]{:S(2)}) collective-permute-start(f32[3,4,128,128]{3,2,1,0:T(8,128)S(1)} %get-tuple-element.125), channel_id=1, source_target_pairs={{0,14},{1,49},{2,0},{3,51},{4,2},{5,53},{6,4},{7,55},{8,6},{9,57},... | collective-permute-start | bytes 2359304 | tf_op jit(solution)/shard_map/ppermute | solution.py:226
  64.5 16.7 %collective-permute-start.18 = (f32[3,4,128,128]{3,2,1,0:T(8,128)S(1)}, f32[3,4,128,128]{3,2,1,0:T(8,128)S(1)}, u32[]{:S(2)}, u32[]{:S(2)}) collective-permute-start(f32[3,4,128,128]{3,2,1,0:T(8,128)S(1)} %get-tuple-element.126), channel_id=1, source_target_pairs={{0,2},{1,17},{2,4},{3,19},{4,6},{5,21},{6,8},{7,23},{8,10},{9,25},... | collective-permute-start | bytes 2359304 | tf_op jit(solution)/shard_map/ppermute | solution.py:226
  64.5 13.5 %collective-permute-start.17 = (f32[4,128,128]{2,1,0:T(8,128)S(1)}, f32[4,128,128]{2,1,0:T(8,128)S(1)}, u32[]{:S(2)}, u32[]{:S(2)}) collective-permute-start(f32[4,128,128]{2,1,0:T(8,128)S(1)} %collective-permute-done.15.rest_2_), channel_id=1, source_target_pairs={{0,48},{16,0},{32,16},{48,32},{1,49},{17,1},{33,17},{49,33},{2,50}... | collective-permute-start | bytes 786440 | tf_op jit(solution)/shard_map/ppermute | solution.py:214
  67.2 14.0 %collective-permute-start.16 = (f32[4,128,128]{2,1,0:T(8,128)S(1)}, f32[4,128,128]{2,1,0:T(8,128)S(1)}, u32[]{:S(2)}, u32[]{:S(2)}) collective-permute-start(f32[4,128,128]{2,1,0:T(8,128)S(1)} %collective-permute-done.15.rest_2_), channel_id=1, source_target_pairs={{0,16},{16,32},{32,48},{48,0},{1,17},{17,33},{33,49},{49,1},{2,18}... | collective-permute-start | bytes 786440 | tf_op jit(solution)/shard_map/ppermute | solution.py:214
  81.3 11.1 %collective-permute-start.21 = (f32[2,12,32,128]{3,2,1,0:T(8,128)S(1)}, f32[2,12,32,128]{3,2,1,0:T(8,128)S(1)}, u32[]{:S(2)}, u32[]{:S(2)}) collective-permute-start(f32[2,12,32,128]{3,2,1,0:T(8,128)S(1)} %slice_bitcast_fusion), channel_id=1, source_target_pairs={{0,192},{1,65},{64,128},{65,1},{128,64},{129,193},{192,0},{193,129... | collective-permute-start | bytes 1179656 | tf_op jit(solution)/shard_map/ppermute | solution.py:253
  82.6 14.5 %collective-permute-start.25 = (f32[2,2,9,32,128]{4,3,2,1,0:T(8,128)S(1)}, f32[2,2,9,32,128]{4,3,2,1,0:T(8,128)S(1)}, u32[]{:S(2)}, u32[]{:S(2)}) collective-permute-start(f32[2,2,9,32,128]{4,3,2,1,0:T(8,128)S(1)} %get-tuple-element.93), channel_id=1, source_target_pairs={{0,64},{1,193},{64,0},{65,129},{128,192},{129,65},{192,128},{193,1... | collective-permute-start | bytes 1769480 | tf_op jit(solution)/shard_map/ppermute | solution.py:249
  84.6 12.6 %collective-permute-start.24 = (f32[4,128,128]{2,1,0:T(8,128)S(1)}, f32[4,128,128]{2,1,0:T(8,128)S(1)}, u32[]{:S(2)}, u32[]{:S(2)}) collective-permute-start(f32[4,128,128]{2,1,0:T(8,128)S(1)} %slice_bitcast_fusion.3), channel_id=1, source_target_pairs={{0,14},{1,49},{2,0},{3,51},{4,2},{5,53},{6,4},{7,55},{8,6},{9,57},... | collective-permute-start | bytes 786440 | tf_op jit(solution)/shard_map/ppermute | solution.py:226
  84.9 12.3 %collective-permute-start.23 = (f32[4,128,128]{2,1,0:T(8,128)S(1)}, f32[4,128,128]{2,1,0:T(8,128)S(1)}, u32[]{:S(2)}, u32[]{:S(2)}) collective-permute-start(f32[4,128,128]{2,1,0:T(8,128)S(1)} %slice_bitcast_fusion.4), channel_id=1, source_target_pairs={{0,2},{1,17},{2,4},{3,19},{4,6},{5,21},{6,8},{7,23},{8,10},{9,25},... | collective-permute-start | bytes 786440 | tf_op jit(solution)/shard_map/ppermute | solution.py:226
  86.1 11.1 %collective-permute-start.22 = (f32[4,128,128]{2,1,0:T(8,128)S(1)}, f32[4,128,128]{2,1,0:T(8,128)S(1)}, u32[]{:S(2)}, u32[]{:S(2)}) collective-permute-start(f32[4,128,128]{2,1,0:T(8,128)S(1)} %collective-permute-done.16.rest_2_), channel_id=1, source_target_pairs={{0,16},{16,32},{32,48},{48,0},{1,17},{17,33},{33,49},{49,1},{2,18}... | collective-permute-start | bytes 786440 | tf_op jit(solution)/shard_map/ppermute | solution.py:214
  97.2 6.0 %collective-permute-start.27 = (f32[2,9,32,128]{3,2,1,0:T(8,128)S(1)}, f32[2,9,32,128]{3,2,1,0:T(8,128)S(1)}, u32[]{:S(2)}, u32[]{:S(2)}) collective-permute-start(f32[2,9,32,128]{3,2,1,0:T(8,128)S(1)} %slice_bitcast_fusion.1), channel_id=1, source_target_pairs={{0,192},{1,65},{64,128},{65,1},{128,64},{129,193},{192,0},{193,129... | collective-permute-start | bytes 884744 | tf_op jit(solution)/shard_map/ppermute | solution.py:253
  97.4 12.7 %collective-permute-start.26 = (f32[2,2,8,32,128]{4,3,2,1,0:T(8,128)S(1)}, f32[2,2,8,32,128]{4,3,2,1,0:T(8,128)S(1)}, u32[]{:S(2)}, u32[]{:S(2)}) collective-permute-start(f32[2,2,8,32,128]{4,3,2,1,0:T(8,128)S(1)} %get-tuple-element.98), channel_id=1, source_target_pairs={{0,64},{1,193},{64,0},{65,129},{128,192},{129,65},{192,128},{193,1... | collective-permute-start | bytes 1572872 | tf_op jit(solution)/shard_map/ppermute | solution.py:249
  110.3 6.0 %collective-permute-start.29 = (f32[2,3,32,128]{3,2,1,0:T(8,128)S(1)}, f32[2,3,32,128]{3,2,1,0:T(8,128)S(1)}, u32[]{:S(2)}, u32[]{:S(2)}) collective-permute-start(f32[2,3,32,128]{3,2,1,0:T(8,128)S(1)} %get-tuple-element.128), channel_id=1, source_target_pairs={{0,64},{1,193},{64,0},{65,129},{128,192},{129,65},{192,128},{193,1... | collective-permute-start | bytes 294920 | tf_op jit(solution)/shard_map/ppermute | solution.py:259
  111.9 4.6 %collective-permute-start.31 = (f32[2,3,32,128]{3,2,1,0:T(8,128)S(1)}, f32[2,3,32,128]{3,2,1,0:T(8,128)S(1)}, u32[]{:S(2)}, u32[]{:S(2)}) collective-permute-start(f32[2,3,32,128]{3,2,1,0:T(8,128)S(1)} %slice_bitcast_fusion.14), channel_id=1, source_target_pairs={{0,192},{1,65},{64,128},{65,1},{128,64},{129,193},{192,0},{193,129... | collective-permute-start | bytes 294920 | tf_op jit(solution)/shard_map/ppermute | solution.py:261
  112.0 6.4 %collective-permute-start.30 = (f32[2,3,32,128]{3,2,1,0:T(8,128)S(1)}, f32[2,3,32,128]{3,2,1,0:T(8,128)S(1)}, u32[]{:S(2)}, u32[]{:S(2)}) collective-permute-start(f32[2,3,32,128]{3,2,1,0:T(8,128)S(1)} %get-tuple-element.127), channel_id=1, source_target_pairs={{0,128},{1,129},{64,192},{65,193},{128,0},{129,1},{192,64},{193,65... | collective-permute-start | bytes 294920 | tf_op jit(solution)/shard_map/ppermute | solution.py:260
  114.3 6.4 %collective-permute-start.28 = (f32[2,8,32,128]{3,2,1,0:T(8,128)S(1)}, f32[2,8,32,128]{3,2,1,0:T(8,128)S(1)}, u32[]{:S(2)}, u32[]{:S(2)}) collective-permute-start(f32[2,8,32,128]{3,2,1,0:T(8,128)S(1)} %slice_bitcast_fusion.2), channel_id=1, source_target_pairs={{0,192},{1,65},{64,128},{65,1},{128,64},{129,193},{192,0},{193,129... | collective-permute-start | bytes 786440 | tf_op jit(solution)/shard_map/ppermute | solution.py:253
  (10 other events, 132.1 us)

commit v4 on v3

--- a/solution.py
+++ b/solution.py
@@ -34,7 +34,7 @@
     ("k4f", "k4b", "d2"),
 )
 
-EARLY = ("own", "zf1", "zb1", "xf1", "xb1", "x2")
+EARLY = ("own", "zf1", "zb1", "xf1", "xb1", "x2", "zf2", "zb2", "k1f", "k1b")
 LIMITS = (12, 12, 12, 12)
 
 
@@ -95,20 +95,23 @@
         place = table[1, NM, sectors[i]].astype(jnp.int32)
         return pltpu.make_async_copy(blocks_sib.at[place], wave.at[i, 1], sem_b.at[i])
 
-    tables[0].wait()
-    tables[1].wait()
-
-    def start(i, carry):
+    def start_own(i, carry):
         own_copy(i).start()
+        return carry
+
+    def start_sib(i, carry):
         sib_copy(i).start()
         return carry
 
-    lax.fori_loop(0, n, start, 0)
+    lax.fori_loop(0, n, start_own, 0)
+    tables[1].wait()
+    lax.fori_loop(0, n, start_sib, 0)
     for side, ref in enumerate((side_own, side_sib)):
         for w in range(NM):
             high, low = split(ref[w * N:(w + 1) * N])
             lefts[side, w * N:(w + 1) * N, :N] = high
             lefts[side, w * N:(w + 1) * N, N:] = low
+    tables[0].wait()
 
     m = pos[0]
     zero = jnp.zeros((N, N), jnp.bfloat16)
@@ -155,11 +158,14 @@
 def final_kernel(batches, pos, inverse, *rest):
     out = rest[-1]
     core = pos[3]
+    others = rest[-2]
+    at = 0
     for b, names in enumerate(batches):
-        mine, term, other = rest[3 * b:3 * b + 3]
+        mine, term = rest[2 * b:2 * b + 2]
         for i, slot in enumerate(slots_of(names)):
             out[inverse[sector(pos, core, slot)]] = mine[i] + term[i]
-            out[inverse[sector(pos, 1 - core, slot)]] = other[i]
+            out[inverse[sector(pos, 1 - core, slot)]] = others[at]
+            at += 1
 
 
 SMEM = pl.BlockSpec(memory_space=pltpu.SMEM)
@@ -263,10 +269,6 @@
     return here[0], there[0], here[1] + there[1]
 
 
-def swap(terms):
-    return terms[0], terms[1], shift(terms[2], "c", 1)
-
-
 def body(wavefunction, left_env, right_env, mpo_values, mpo_pattern, physical, right_sector, sector_size):
     m, x, z, c = (lax.axis_index(a) for a in ("m", "x", "z", "c"))
     first = c == 0
@@ -357,8 +359,8 @@
     b = quarter(b)
     d = quarter(d)
     a, b, d, e = fence((a, b, d, e))
-    a, b, d, e = (swap(part) for part in (a, b, d, e))
-    return finish(BATCHES, pos, inverse, a + b + d + e)
+    others = shift(jnp.concatenate([part[2] for part in (a, b, d, e)]), "c", 1)
+    return finish(BATCHES, pos, inverse, a[:2] + b[:2] + d[:2] + e[:2] + (others,))
 
 
 def solution(mesh):

time: 126 us -> 124 us (0.984)
  other arithmetic: 10.4 us -> 8.35 us
  starting transfers between devices: 47.8 us -> 46.1 us
  waiting for transfers between devices: 39.2 us -> 40.6 us
    select_n x4, other arithmetic: 4.78 us -> 2.68 us  [pick(): return jnp.where(first, one, two)]
    ppermute x1, waiting for transfers between devices: 2.3 us -> 3.92 us  [by_core_far(): return lax.ppermute(array, TENSOR, pairs)]
    ppermute x18 -> x15, starting transfers between devices: 23.8 us -> 23.1 us  [shift(): lax.ppermute(array, axis, [(i, (i + step) % size) for i in range(size)])]
    ppermute x18 -> x15, waiting for transfers between devices: 18.7 us -> 18.6 us  [shift(): lax.ppermute(array, axis, [(i, (i + step) % size) for i in range(size)])]
  transfers between devices with their start and end apart: 36 -> 33, of which waited for: 15 -> 15; matrix products, arithmetic and copies ran while one was open for 6% -> 5% of each run, Pallas kernels for 20% -> 21%
where the time goes in v4:
time: 124 us
  starting transfers between devices  46.1 us (37%)
  waiting for transfers between devices  40.6 us (33%)
  Pallas kernels  27.4 us (22%)
  other arithmetic  8.35 us (7%)
    pallas_call x4, Pallas kernels, work(): pl.pallas_call(functools.partial(work_kernel, names), out_shape=(piece,)...  25.6 us
    ppermute x15, starting transfers between devices, shift(): lax.ppermute(array, axis, [(i, (i + step) % size) for i in range(size)])  23.1 us
    ppermute x15, waiting for transfers between devices, shift(): lax.ppermute(array, axis, [(i, (i + step) % size) for i in range(size)])  18.6 us
    ppermute x3, waiting for transfers between devices, halve(): return keep + lax.ppermute(send, ('m', 'c'), hops(1, 3))  11.5 us
    ppermute x8, starting transfers between devices, by_core(): return lax.ppermute(array, TENSOR, pairs)  10 us
    ppermute x3, starting transfers between devices, halve(): return keep + lax.ppermute(send, ('m', 'c'), hops(1, 3))  6.59 us
    ppermute x1, waiting for transfers between devices, by_core_far(): return lax.ppermute(array, TENSOR, pairs)  3.92 us
    select_n x4, other arithmetic, pick(): return jnp.where(first, one, two)  2.68 us
  transfers between devices with their start and end apart: 33, of which 15 were waited for; matrix products, arithmetic and copies ran while one was open for 5% of the time, Pallas kernels for 21%

profile of v4, /device:TPU:1, one launch (start us, length us, event | category | flops | bytes accessed | tf_op | source)
XLA Modules:
  0.0 123.9 jit_solution(16508061022146991260)
XLA Ops:
  0.0 3.2 %collective-permute-start.4 = (f32[64,128,128]{2,1,0:T(8,128)}, f32[64,128,128]{2,1,0:T(8,128)}, u32[]{:S(2)}, u32[]{:S(2)}) collective-permute-start(f32[64,128,128]{2,1,0:T(8,128)} %blocks.7), channel_id=1, source_target_pairs={{0,1},{1,0},{2,3},{3,2},{4,5},{5,4},{6,7},{7,6},{8,9},{9,8},{10,11... | collective-permute-start | bytes 12582920 | tf_op jit(solution)/shard_map/ppermute | solution.py:220
  6.5 4.9 %collective-permute-start.1 = (f32[4,128,128]{2,1,0:T(8,128)S(1)}, f32[4,128,128]{2,1,0:T(8,128)S(1)}, u32[]{:S(2)}, u32[]{:S(2)}) collective-permute-start(f32[4,128,128]{2,1,0:T(8,128)S(1)} %bitcast_select_fusion.1.rest_0_), channel_id=1, source_target_pairs={{0,14},{2,0},{4,2},{6,4},{8,6},{10,8},{12,10},{14,12},{1,15},{3,1}... | collective-permute-start | bytes 786440 | tf_op jit(solution)/shard_map/ppermute | solution.py:220
  16.8 3.1 %collective-permute-done.rest_1_ = f32[4,128,128]{2,1,0:T(8,128)S(1)} collective-permute-done((f32[4,128,128]{2,1,0:T(8,128)S(1)}, f32[4,128,128]{2,1,0:T(8,128)S(1)}, u32[]{:S(2)}, u32[]{:S(2)}) %collective-permute-start) | collective-permute-done | bytes 262176 | tf_op jit(solution)/shard_map/ppermute | solution.py:220
  21.4 2.8 %collective-permute-start.10 = (f32[2,4,128,128]{3,2,1,0:T(8,128)S(1)}, f32[2,4,128,128]{3,2,1,0:T(8,128)S(1)}, u32[]{:S(2)}, u32[]{:S(2)}) collective-permute-start(f32[2,4,128,128]{3,2,1,0:T(8,128)S(1)} %maximum_select_fusion.2), channel_id=1, source_target_pairs={{0,14},{1,49},{2,0},{3,51},{4,2},{5,53},{6,4},{7,55},{8,6},{9,57},... | collective-permute-start | bytes 1572872 | tf_op jit(solution)/shard_map/ppermute | solution.py:232
  24.2 2.7 %collective-permute-start.6 = (f32[4,128,128]{2,1,0:T(8,128)S(1)}, f32[4,128,128]{2,1,0:T(8,128)}, u32[]{:S(2)}, u32[]{:S(2)}) collective-permute-start(f32[4,128,128]{2,1,0:T(8,128)S(1)} %collective-permute-done.1.rest_2_), channel_id=1, source_target_pairs={{0,14},{2,0},{4,2},{6,4},{8,6},{10,8},{12,10},{14,12},{1,15},{3,1}... | collective-permute-start | bytes 786440 | tf_op jit(solution)/shard_map/ppermute | solution.py:220
  26.8 2.7 %collective-permute-start.8 = (f32[4,128,128]{2,1,0:T(8,128)S(1)}, f32[4,128,128]{2,1,0:T(8,128)S(1)}, u32[]{:S(2)}, u32[]{:S(2)}) collective-permute-start(f32[4,128,128]{2,1,0:T(8,128)S(1)} %collective-permute-done.3.rest_4_), channel_id=1, source_target_pairs={{0,48},{16,0},{32,16},{48,32},{1,49},{17,1},{33,17},{49,33},{2,50}... | collective-permute-start | bytes 786440 | tf_op jit(solution)/shard_map/ppermute | solution.py:220
  29.5 4.2 %collective-permute-done.5.rest_5_ = f32[4,128,128]{2,1,0:T(8,128)S(1)} collective-permute-done((f32[4,128,128]{2,1,0:T(8,128)S(1)}, f32[4,128,128]{2,1,0:T(8,128)S(1)}, u32[]{:S(2)}, u32[]{:S(2)}) %collective-permute-start.5) | collective-permute-done | bytes 262176 | tf_op jit(solution)/shard_map/ppermute | solution.py:220
  33.8 1.9 %collective-permute-done.8.rest_7_ = f32[4,128,128]{2,1,0:T(8,128)S(1)} collective-permute-done((f32[4,128,128]{2,1,0:T(8,128)S(1)}, f32[4,128,128]{2,1,0:T(8,128)S(1)}, u32[]{:S(2)}, u32[]{:S(2)}) %collective-permute-start.8) | collective-permute-done | bytes 262176 | tf_op jit(solution)/shard_map/ppermute | solution.py:220
  35.8 2.4 %fusion.1 = (f32[3,4,128,128]{3,2,1,0:T(8,128)}, f32[3,4,128,128]{3,2,1,0:T(8,128)}) fusion(f32[1,4,128,128]{3,2,1,0:T(8,128)S(1)} %bitcast.81, f32[2,4,128,128]{3,2,1,0:T(8,128)S(1)} %collective-permute-done.10.rest_9_, f32[1,4,128,128]{3,2,1,0:T(8,128)S(1)} %slice.94, f32[1,4,128,128]{3,2,1,0:T(8,128)} %bitcast.16, f32[1,4,128,128]{3,2,1,0:T(8,128)S(1)} %bitcast.80, ...), kind=kLoop, calls=%fused_computation.3 | loop fusion | flops 1376256 | bytes 3932161 | tf_op jit(solution)/shard_map/jit(_where)/select_n | solution.py:279
  38.1 3.4 %collective-permute-start.12 = (f32[3,4,128,128]{3,2,1,0:T(8,128)}, f32[3,4,128,128]{3,2,1,0:T(8,128)S(1)}, u32[]{:S(2)}, u32[]{:S(2)}) collective-permute-start(f32[3,4,128,128]{3,2,1,0:T(8,128)} %get-tuple-element.123), channel_id=1, source_target_pairs={{0,14},{1,49},{2,0},{3,51},{4,2},{5,53},{6,4},{7,55},{8,6},{9,57},... | collective-permute-start | bytes 2359304 | tf_op jit(solution)/shard_map/ppermute | solution.py:232
  41.7 2.7 %collective-permute-start.14 = (f32[4,128,128]{2,1,0:T(8,128)}, f32[4,128,128]{2,1,0:T(8,128)S(1)}, u32[]{:S(2)}, u32[]{:S(2)}) collective-permute-start(f32[4,128,128]{2,1,0:T(8,128)} %collective-permute-done.6.rest_6_), channel_id=1, source_target_pairs={{0,14},{2,0},{4,2},{6,4},{8,6},{10,8},{12,10},{14,12},{1,15},{3,1}... | collective-permute-start | bytes 786440 | tf_op jit(solution)/shard_map/ppermute | solution.py:220
  44.4 8.9 %work.4 = (f32[2,2,12,32,128]{4,3,2,1,0:T(8,128)S(1)}, f32[2,2,12,32,128]{4,3,2,1,0:T(8,128)S(1)}) custom-call(s32[4]{0:T(128)S(1)} %pad_add_fusion.pos, s32[64]{0:T(128)S(1)} %select_reduce_fusion.2.inverse, f32[520,128]{1,0:T(8,128)S(1)} %pad_maximum_fusion.4.side_own, f32[520,128]{1,0:T(8,128)S(1)} %collective-permute-done.7.side_sib, ...), custom_call_target="tpu_custom_call" | custom-call | tf_op jit(solution)/shard_map/work/pallas_call | solution.py:185
  54.2 2.7 %collective-permute-start.20 = (f32[2,2,12,32,128]{4,3,2,1,0:T(8,128)S(1)}, f32[2,2,12,32,128]{4,3,2,1,0:T(8,128)S(1)}, u32[]{:S(2)}, u32[]{:S(2)}) collective-permute-start(f32[2,2,12,32,128]{4,3,2,1,0:T(8,128)S(1)} %get-tuple-element.85), channel_id=1, source_target_pairs={{0,64},{1,193},{64,0},{65,129},{128,192},{129,65},{192,128},{193,1... | collective-permute-start | bytes 2359304 | tf_op jit(solution)/shard_map/ppermute | solution.py:255
  57.0 3.9 %collective-permute-done.15.rest_2_ = f32[4,128,128]{2,1,0:T(8,128)S(1)} collective-permute-done((f32[4,128,128]{2,1,0:T(8,128)S(1)}, f32[4,128,128]{2,1,0:T(8,128)S(1)}, u32[]{:S(2)}, u32[]{:S(2)}) %collective-permute-start.15) | collective-permute-done | bytes 262176 | tf_op jit(solution)/shard_map/ppermute | solution.py:242
  61.2 2.3 %collective-permute-start.19 = (f32[3,4,128,128]{3,2,1,0:T(8,128)S(1)}, f32[3,4,128,128]{3,2,1,0:T(8,128)S(1)}, u32[]{:S(2)}, u32[]{:S(2)}) collective-permute-start(f32[3,4,128,128]{3,2,1,0:T(8,128)S(1)} %get-tuple-element.125), channel_id=1, source_target_pairs={{0,14},{1,49},{2,0},{3,51},{4,2},{5,53},{6,4},{7,55},{8,6},{9,57},... | collective-permute-start | bytes 2359304 | tf_op jit(solution)/shard_map/ppermute | solution.py:232
  63.5 2.7 %collective-permute-start.17 = (f32[4,128,128]{2,1,0:T(8,128)S(1)}, f32[4,128,128]{2,1,0:T(8,128)S(1)}, u32[]{:S(2)}, u32[]{:S(2)}) collective-permute-start(f32[4,128,128]{2,1,0:T(8,128)S(1)} %collective-permute-done.15.rest_2_), channel_id=1, source_target_pairs={{0,48},{16,0},{32,16},{48,32},{1,49},{17,1},{33,17},{49,33},{2,50}... | collective-permute-start | bytes 786440 | tf_op jit(solution)/shard_map/ppermute | solution.py:220
  66.2 6.8 %work.5 = (f32[2,2,9,32,128]{4,3,2,1,0:T(8,128)S(1)}, f32[2,2,9,32,128]{4,3,2,1,0:T(8,128)S(1)}) custom-call(s32[4]{0:T(128)S(1)} %pad_add_fusion.pos, s32[64]{0:T(128)S(1)} %select_reduce_fusion.2.inverse, f32[520,128]{1,0:T(8,128)S(1)} %pad_maximum_fusion.4.side_own, f32[520,128]{1,0:T(8,128)S(1)} %collective-permute-done.7.side_sib, ...), custom_call_target="tpu_custom_call" | custom-call | tf_op jit(solution)/shard_map/work/pallas_call | solution.py:185
  73.1 3.4 %collective-permute-done.17.rest_3_ = f32[4,128,128]{2,1,0:T(8,128)S(1)} collective-permute-done((f32[4,128,128]{2,1,0:T(8,128)S(1)}, f32[4,128,128]{2,1,0:T(8,128)S(1)}, u32[]{:S(2)}, u32[]{:S(2)}) %collective-permute-start.17) | collective-permute-done | bytes 262176 | tf_op jit(solution)/shard_map/ppermute | solution.py:220
  76.5 3.1 %collective-permute-done.16.rest_2_ = f32[4,128,128]{2,1,0:T(8,128)S(1)} collective-permute-done((f32[4,128,128]{2,1,0:T(8,128)S(1)}, f32[4,128,128]{2,1,0:T(8,128)S(1)}, u32[]{:S(2)}, u32[]{:S(2)}) %collective-permute-start.16) | collective-permute-done | bytes 262176 | tf_op jit(solution)/shard_map/ppermute | solution.py:220
  81.1 1.9 %collective-permute-start.25 = (f32[2,2,9,32,128]{4,3,2,1,0:T(8,128)S(1)}, f32[2,2,9,32,128]{4,3,2,1,0:T(8,128)S(1)}, u32[]{:S(2)}, u32[]{:S(2)}) collective-permute-start(f32[2,2,9,32,128]{4,3,2,1,0:T(8,128)S(1)} %get-tuple-element.93), channel_id=1, source_target_pairs={{0,64},{1,193},{64,0},{65,129},{128,192},{129,65},{192,128},{193,1... | collective-permute-start | bytes 1769480 | tf_op jit(solution)/shard_map/ppermute | solution.py:255
  84.6 6.3 %work.6 = (f32[2,2,8,32,128]{4,3,2,1,0:T(8,128)S(1)}, f32[2,2,8,32,128]{4,3,2,1,0:T(8,128)S(1)}) custom-call(s32[4]{0:T(128)S(1)} %pad_add_fusion.pos, s32[64]{0:T(128)S(1)} %select_reduce_fusion.2.inverse, f32[520,128]{1,0:T(8,128)S(1)} %pad_maximum_fusion.4.side_own, f32[520,128]{1,0:T(8,128)S(1)} %collective-permute-done.7.side_sib, ...), custom_call_target="tpu_custom_call" | custom-call | tf_op jit(solution)/shard_map/work/pallas_call | solution.py:185
  90.9 4.6 %collective-permute-done.25 = f32[2,2,9,32,128]{4,3,2,1,0:T(8,128)S(1)} collective-permute-done((f32[2,2,9,32,128]{4,3,2,1,0:T(8,128)S(1)}, f32[2,2,9,32,128]{4,3,2,1,0:T(8,128)S(1)}, u32[]{:S(2)}, u32[]{:S(2)}) %collective-permute-start.25) | collective-permute-done | bytes 589856 | tf_op jit(solution)/shard_map/ppermute | solution.py:255
  95.9 2.0 %collective-permute-start.26 = (f32[2,2,8,32,128]{4,3,2,1,0:T(8,128)S(1)}, f32[2,2,8,32,128]{4,3,2,1,0:T(8,128)S(1)}, u32[]{:S(2)}, u32[]{:S(2)}) collective-permute-start(f32[2,2,8,32,128]{4,3,2,1,0:T(8,128)S(1)} %get-tuple-element.98), channel_id=1, source_target_pairs={{0,64},{1,193},{64,0},{65,129},{128,192},{129,65},{192,128},{193,1... | collective-permute-start | bytes 1572872 | tf_op jit(solution)/shard_map/ppermute | solution.py:255
  97.8 3.6 %work.7 = (f32[2,2,3,32,128]{4,3,2,1,0:T(8,128)S(1)}, f32[2,2,3,32,128]{4,3,2,1,0:T(8,128)S(1)}) custom-call(s32[4]{0:T(128)S(1)} %pad_add_fusion.pos, s32[64]{0:T(128)S(1)} %select_reduce_fusion.2.inverse, f32[520,128]{1,0:T(8,128)S(1)} %pad_maximum_fusion.4.side_own, f32[520,128]{1,0:T(8,128)S(1)} %collective-permute-done.7.side_sib, ...), custom_call_target="tpu_custom_call" | custom-call | tf_op jit(solution)/shard_map/work/pallas_call | solution.py:185
  101.7 6.8 %collective-permute-done.26 = f32[2,2,8,32,128]{4,3,2,1,0:T(8,128)S(1)} collective-permute-done((f32[2,2,8,32,128]{4,3,2,1,0:T(8,128)S(1)}, f32[2,2,8,32,128]{4,3,2,1,0:T(8,128)S(1)}, u32[]{:S(2)}, u32[]{:S(2)}) %collective-permute-start.26) | collective-permute-done | bytes 524320 | tf_op jit(solution)/shard_map/ppermute | solution.py:255
  108.7 1.7 %collective-permute-start.29 = (f32[2,3,32,128]{3,2,1,0:T(8,128)S(1)}, f32[2,3,32,128]{3,2,1,0:T(8,128)S(1)}, u32[]{:S(2)}, u32[]{:S(2)}) collective-permute-start(f32[2,3,32,128]{3,2,1,0:T(8,128)S(1)} %get-tuple-element.128), channel_id=1, source_target_pairs={{0,64},{1,193},{64,0},{65,129},{128,192},{129,65},{192,128},{193,1... | collective-permute-start | bytes 294920 | tf_op jit(solution)/shard_map/ppermute | solution.py:265
  110.6 2.2 %collective-permute-start.30 = (f32[2,3,32,128]{3,2,1,0:T(8,128)S(1)}, f32[2,3,32,128]{3,2,1,0:T(8,128)S(1)}, u32[]{:S(2)}, u32[]{:S(2)}) collective-permute-start(f32[2,3,32,128]{3,2,1,0:T(8,128)S(1)} %get-tuple-element.127), channel_id=1, source_target_pairs={{0,128},{1,129},{64,192},{65,193},{128,0},{129,1},{192,64},{193,65... | collective-permute-start | bytes 294920 | tf_op jit(solution)/shard_map/ppermute | solution.py:266
  112.8 2.0 %collective-permute-done.29 = f32[2,3,32,128]{3,2,1,0:T(8,128)S(1)} collective-permute-done((f32[2,3,32,128]{3,2,1,0:T(8,128)S(1)}, f32[2,3,32,128]{3,2,1,0:T(8,128)S(1)}, u32[]{:S(2)}, u32[]{:S(2)}) %collective-permute-start.29) | collective-permute-done | bytes 98336 | tf_op jit(solution)/shard_map/ppermute | solution.py:265
  115.0 2.0 %collective-permute-done.30 = f32[2,3,32,128]{3,2,1,0:T(8,128)S(1)} collective-permute-done((f32[2,3,32,128]{3,2,1,0:T(8,128)S(1)}, f32[2,3,32,128]{3,2,1,0:T(8,128)S(1)}, u32[]{:S(2)}, u32[]{:S(2)}) %collective-permute-start.30) | collective-permute-done | bytes 98336 | tf_op jit(solution)/shard_map/ppermute | solution.py:266
  117.1 2.2 %collective-permute-done.28 = f32[2,8,32,128]{3,2,1,0:T(8,128)S(1)} collective-permute-done((f32[2,8,32,128]{3,2,1,0:T(8,128)S(1)}, f32[2,8,32,128]{3,2,1,0:T(8,128)S(1)}, u32[]{:S(2)}, u32[]{:S(2)}) %collective-permute-start.28) | collective-permute-done | bytes 262176 | tf_op jit(solution)/shard_map/ppermute | solution.py:259
  120.5 1.5 %collective-permute-done.32.rest_8_ = f32[32,32,128]{2,1,0:T(8,128)S(1)} collective-permute-done((f32[32,32,128]{2,1,0:T(8,128)S(1)}, f32[32,32,128]{2,1,0:T(8,128)S(1)}, u32[]{:S(2)}, u32[]{:S(2)}) %collective-permute-start.32) | collective-permute-done | bytes 524320 | tf_op jit(solution)/shard_map/ppermute | solution.py:220
  122.1 1.8 %finish.1 = f32[64,32,128]{2,1,0:T(8,128)} custom-call(s32[4]{0:T(128)S(1)} %pad_add_fusion.pos, s32[64]{0:T(128)S(1)} %select_reduce_fusion.2.inverse, f32[12,32,128]{2,1,0:T(8,128)S(1)} %slice_bitcast_fusion.7.rest_0_, f32[12,32,128]{2,1,0:T(8,128)S(1)} %slice_bitcast_fusion.6.rest_1_, f32[9,32,128]{2,1,0:T(8,128)S(1)} %slice_bitcast_fusion.10.rest_2_, ...), custom_call_target="tpu_custom_call" | custom-call | tf_op jit(solution)/shard_map/finish/pallas_call | solution.py:208
  (102 shorter events, 16.4 us)
Async XLA Ops:
  0.0 19.9 %collective-permute-start.4 = (f32[64,128,128]{2,1,0:T(8,128)}, f32[64,128,128]{2,1,0:T(8,128)}, u32[]{:S(2)}, u32[]{:S(2)}) collective-permute-start(f32[64,128,128]{2,1,0:T(8,128)} %blocks.7), channel_id=1, source_target_pairs={{0,1},{1,0},{2,3},{3,2},{4,5},{5,4},{6,7},{7,6},{8,9},{9,8},{10,11... | collective-permute-start | bytes 12582920 | tf_op jit(solution)/shard_map/ppermute | solution.py:220
  5.0 10.5 %collective-permute-start.3 = (f32[4,128,128]{2,1,0:T(8,128)S(1)}, f32[4,128,128]{2,1,0:T(8,128)S(1)}, u32[]{:S(2)}, u32[]{:S(2)}) collective-permute-start(f32[4,128,128]{2,1,0:T(8,128)S(1)} %bitcast_select_fusion.1.rest_0_), channel_id=1, source_target_pairs={{0,48},{16,0},{32,16},{48,32},{1,49},{17,1},{33,17},{49,33},{2,50}... | collective-permute-start | bytes 786440 | tf_op jit(solution)/shard_map/ppermute | solution.py:220
  5.8 9.7 %collective-permute-start.2 = (f32[4,128,128]{2,1,0:T(8,128)S(1)}, f32[4,128,128]{2,1,0:T(8,128)S(1)}, u32[]{:S(2)}, u32[]{:S(2)}) collective-permute-start(f32[4,128,128]{2,1,0:T(8,128)S(1)} %bitcast_select_fusion.1.rest_0_), channel_id=1, source_target_pairs={{0,16},{16,32},{32,48},{48,0},{1,17},{17,33},{33,49},{49,1},{2,18}... | collective-permute-start | bytes 786440 | tf_op jit(solution)/shard_map/ppermute | solution.py:220
  6.5 10.3 %collective-permute-start.1 = (f32[4,128,128]{2,1,0:T(8,128)S(1)}, f32[4,128,128]{2,1,0:T(8,128)S(1)}, u32[]{:S(2)}, u32[]{:S(2)}) collective-permute-start(f32[4,128,128]{2,1,0:T(8,128)S(1)} %bitcast_select_fusion.1.rest_0_), channel_id=1, source_target_pairs={{0,14},{2,0},{4,2},{6,4},{8,6},{10,8},{12,10},{14,12},{1,15},{3,1}... | collective-permute-start | bytes 786440 | tf_op jit(solution)/shard_map/ppermute | solution.py:220
  11.4 8.5 %collective-permute-start = (f32[4,128,128]{2,1,0:T(8,128)S(1)}, f32[4,128,128]{2,1,0:T(8,128)S(1)}, u32[]{:S(2)}, u32[]{:S(2)}) collective-permute-start(f32[4,128,128]{2,1,0:T(8,128)S(1)} %bitcast_select_fusion.1.rest_0_), channel_id=1, source_target_pairs={{0,2},{2,4},{4,6},{6,8},{8,10},{10,12},{12,14},{14,0},{1,3},{3,5},... | collective-permute-start | bytes 786440 | tf_op jit(solution)/shard_map/ppermute | solution.py:220
  19.9 6.9 %collective-permute-start.7 = (f32[520,128]{1,0:T(8,128)S(1)}, f32[520,128]{1,0:T(8,128)S(1)}, u32[]{:S(2)}, u32[]{:S(2)}) collective-permute-start(f32[520,128]{1,0:T(8,128)S(1)} %pad_maximum_fusion.4.side_own), channel_id=1, source_target_pairs={{0,1},{1,0},{2,3},{3,2},{4,5},{5,4},{6,7},{7,6},{8,9},{9,8},{10,11... | collective-permute-start | bytes 798728 | tf_op jit(solution)/shard_map/ppermute | solution.py:220
  21.4 12.4 %collective-permute-start.10 = (f32[2,4,128,128]{3,2,1,0:T(8,128)S(1)}, f32[2,4,128,128]{3,2,1,0:T(8,128)S(1)}, u32[]{:S(2)}, u32[]{:S(2)}) collective-permute-start(f32[2,4,128,128]{3,2,1,0:T(8,128)S(1)} %maximum_select_fusion.2), channel_id=1, source_target_pairs={{0,14},{1,49},{2,0},{3,51},{4,2},{5,53},{6,4},{7,55},{8,6},{9,57},... | collective-permute-start | bytes 1572872 | tf_op jit(solution)/shard_map/ppermute | solution.py:232
  24.2 9.6 %collective-permute-start.9 = (f32[2,4,128,128]{3,2,1,0:T(8,128)S(1)}, f32[2,4,128,128]{3,2,1,0:T(8,128)S(1)}, u32[]{:S(2)}, u32[]{:S(2)}) collective-permute-start(f32[2,4,128,128]{3,2,1,0:T(8,128)S(1)} %maximum_select_fusion.2), channel_id=1, source_target_pairs={{0,2},{1,17},{2,4},{3,19},{4,6},{5,21},{6,8},{7,23},{8,10},{9,25},... | collective-permute-start | bytes 1572872 | tf_op jit(solution)/shard_map/ppermute | solution.py:232
  24.2 9.6 %collective-permute-start.5 = (f32[4,128,128]{2,1,0:T(8,128)S(1)}, f32[4,128,128]{2,1,0:T(8,128)S(1)}, u32[]{:S(2)}, u32[]{:S(2)}) collective-permute-start(f32[4,128,128]{2,1,0:T(8,128)S(1)} %collective-permute-done.rest_1_), channel_id=1, source_target_pairs={{0,2},{2,4},{4,6},{6,8},{8,10},{10,12},{12,14},{14,0},{1,3},{3,5},... | collective-permute-start | bytes 786440 | tf_op jit(solution)/shard_map/ppermute | solution.py:220
  24.2 9.6 %collective-permute-start.6 = (f32[4,128,128]{2,1,0:T(8,128)S(1)}, f32[4,128,128]{2,1,0:T(8,128)}, u32[]{:S(2)}, u32[]{:S(2)}) collective-permute-start(f32[4,128,128]{2,1,0:T(8,128)S(1)} %collective-permute-done.1.rest_2_), channel_id=1, source_target_pairs={{0,14},{2,0},{4,2},{6,4},{8,6},{10,8},{12,10},{14,12},{1,15},{3,1}... | collective-permute-start | bytes 786440 | tf_op jit(solution)/shard_map/ppermute | solution.py:220
  26.8 8.9 %collective-permute-start.8 = (f32[4,128,128]{2,1,0:T(8,128)S(1)}, f32[4,128,128]{2,1,0:T(8,128)S(1)}, u32[]{:S(2)}, u32[]{:S(2)}) collective-permute-start(f32[4,128,128]{2,1,0:T(8,128)S(1)} %collective-permute-done.3.rest_4_), channel_id=1, source_target_pairs={{0,48},{16,0},{32,16},{48,32},{1,49},{17,1},{33,17},{49,33},{2,50}... | collective-permute-start | bytes 786440 | tf_op jit(solution)/shard_map/ppermute | solution.py:220
  38.1 22.8 %collective-permute-start.12 = (f32[3,4,128,128]{3,2,1,0:T(8,128)}, f32[3,4,128,128]{3,2,1,0:T(8,128)S(1)}, u32[]{:S(2)}, u32[]{:S(2)}) collective-permute-start(f32[3,4,128,128]{3,2,1,0:T(8,128)} %get-tuple-element.123), channel_id=1, source_target_pairs={{0,14},{1,49},{2,0},{3,51},{4,2},{5,53},{6,4},{7,55},{8,6},{9,57},... | collective-permute-start | bytes 2359304 | tf_op jit(solution)/shard_map/ppermute | solution.py:232
  41.6 19.3 %collective-permute-start.11 = (f32[3,4,128,128]{3,2,1,0:T(8,128)}, f32[3,4,128,128]{3,2,1,0:T(8,128)S(1)}, u32[]{:S(2)}, u32[]{:S(2)}) collective-permute-start(f32[3,4,128,128]{3,2,1,0:T(8,128)} %get-tuple-element.124), channel_id=1, source_target_pairs={{0,2},{1,17},{2,4},{3,19},{4,6},{5,21},{6,8},{7,23},{8,10},{9,25},... | collective-permute-start | bytes 2359304 | tf_op jit(solution)/shard_map/ppermute | solution.py:232
  41.6 11.8 %collective-permute-start.13 = (f32[4,128,128]{2,1,0:T(8,128)S(1)}, f32[4,128,128]{2,1,0:T(8,128)S(1)}, u32[]{:S(2)}, u32[]{:S(2)}) collective-permute-start(f32[4,128,128]{2,1,0:T(8,128)S(1)} %collective-permute-done.5.rest_5_), channel_id=1, source_target_pairs={{0,2},{2,4},{4,6},{6,8},{8,10},{10,12},{12,14},{14,0},{1,3},{3,5},... | collective-permute-start | bytes 786440 | tf_op jit(solution)/shard_map/ppermute | solution.py:220
  41.7 11.7 %collective-permute-start.14 = (f32[4,128,128]{2,1,0:T(8,128)}, f32[4,128,128]{2,1,0:T(8,128)S(1)}, u32[]{:S(2)}, u32[]{:S(2)}) collective-permute-start(f32[4,128,128]{2,1,0:T(8,128)} %collective-permute-done.6.rest_6_), channel_id=1, source_target_pairs={{0,14},{2,0},{4,2},{6,4},{8,6},{10,8},{12,10},{14,12},{1,15},{3,1}... | collective-permute-start | bytes 786440 | tf_op jit(solution)/shard_map/ppermute | solution.py:220
  53.4 7.5 %collective-permute-start.15 = (f32[4,128,128]{2,1,0:T(8,128)S(1)}, f32[4,128,128]{2,1,0:T(8,128)S(1)}, u32[]{:S(2)}, u32[]{:S(2)}) collective-permute-start(f32[4,128,128]{2,1,0:T(8,128)S(1)} %broadcast_select_fusion), channel_id=1, source_target_pairs={{0,2},{1,15},{2,4},{3,1},{4,6},{5,3},{6,8},{7,5},{8,10},{9,7},{10,... | collective-permute-start | bytes 786440 | tf_op jit(solution)/shard_map/ppermute | solution.py:242
  54.2 18.7 %collective-permute-start.20 = (f32[2,2,12,32,128]{4,3,2,1,0:T(8,128)S(1)}, f32[2,2,12,32,128]{4,3,2,1,0:T(8,128)S(1)}, u32[]{:S(2)}, u32[]{:S(2)}) collective-permute-start(f32[2,2,12,32,128]{4,3,2,1,0:T(8,128)S(1)} %get-tuple-element.85), channel_id=1, source_target_pairs={{0,64},{1,193},{64,0},{65,129},{128,192},{129,65},{192,128},{193,1... | collective-permute-start | bytes 2359304 | tf_op jit(solution)/shard_map/ppermute | solution.py:255
  61.2 18.5 %collective-permute-start.19 = (f32[3,4,128,128]{3,2,1,0:T(8,128)S(1)}, f32[3,4,128,128]{3,2,1,0:T(8,128)S(1)}, u32[]{:S(2)}, u32[]{:S(2)}) collective-permute-start(f32[3,4,128,128]{3,2,1,0:T(8,128)S(1)} %get-tuple-element.125), channel_id=1, source_target_pairs={{0,14},{1,49},{2,0},{3,51},{4,2},{5,53},{6,4},{7,55},{8,6},{9,57},... | collective-permute-start | bytes 2359304 | tf_op jit(solution)/shard_map/ppermute | solution.py:232
  63.5 16.2 %collective-permute-start.18 = (f32[3,4,128,128]{3,2,1,0:T(8,128)S(1)}, f32[3,4,128,128]{3,2,1,0:T(8,128)S(1)}, u32[]{:S(2)}, u32[]{:S(2)}) collective-permute-start(f32[3,4,128,128]{3,2,1,0:T(8,128)S(1)} %get-tuple-element.126), channel_id=1, source_target_pairs={{0,2},{1,17},{2,4},{3,19},{4,6},{5,21},{6,8},{7,23},{8,10},{9,25},... | collective-permute-start | bytes 2359304 | tf_op jit(solution)/shard_map/ppermute | solution.py:232
  63.5 13.0 %collective-permute-start.17 = (f32[4,128,128]{2,1,0:T(8,128)S(1)}, f32[4,128,128]{2,1,0:T(8,128)S(1)}, u32[]{:S(2)}, u32[]{:S(2)}) collective-permute-start(f32[4,128,128]{2,1,0:T(8,128)S(1)} %collective-permute-done.15.rest_2_), channel_id=1, source_target_pairs={{0,48},{16,0},{32,16},{48,32},{1,49},{17,1},{33,17},{49,33},{2,50}... | collective-permute-start | bytes 786440 | tf_op jit(solution)/shard_map/ppermute | solution.py:220
  66.2 13.5 %collective-permute-start.16 = (f32[4,128,128]{2,1,0:T(8,128)S(1)}, f32[4,128,128]{2,1,0:T(8,128)S(1)}, u32[]{:S(2)}, u32[]{:S(2)}) collective-permute-start(f32[4,128,128]{2,1,0:T(8,128)S(1)} %collective-permute-done.15.rest_2_), channel_id=1, source_target_pairs={{0,16},{16,32},{32,48},{48,0},{1,17},{17,33},{33,49},{49,1},{2,18}... | collective-permute-start | bytes 786440 | tf_op jit(solution)/shard_map/ppermute | solution.py:220
  79.7 11.2 %collective-permute-start.21 = (f32[2,12,32,128]{3,2,1,0:T(8,128)S(1)}, f32[2,12,32,128]{3,2,1,0:T(8,128)S(1)}, u32[]{:S(2)}, u32[]{:S(2)}) collective-permute-start(f32[2,12,32,128]{3,2,1,0:T(8,128)S(1)} %slice_bitcast_fusion), channel_id=1, source_target_pairs={{0,192},{1,65},{64,128},{65,1},{128,64},{129,193},{192,0},{193,129... | collective-permute-start | bytes 1179656 | tf_op jit(solution)/shard_map/ppermute | solution.py:259
  81.1 14.5 %collective-permute-start.25 = (f32[2,2,9,32,128]{4,3,2,1,0:T(8,128)S(1)}, f32[2,2,9,32,128]{4,3,2,1,0:T(8,128)S(1)}, u32[]{:S(2)}, u32[]{:S(2)}) collective-permute-start(f32[2,2,9,32,128]{4,3,2,1,0:T(8,128)S(1)} %get-tuple-element.93), channel_id=1, source_target_pairs={{0,64},{1,193},{64,0},{65,129},{128,192},{129,65},{192,128},{193,1... | collective-permute-start | bytes 1769480 | tf_op jit(solution)/shard_map/ppermute | solution.py:255
  83.0 12.6 %collective-permute-start.24 = (f32[4,128,128]{2,1,0:T(8,128)S(1)}, f32[4,128,128]{2,1,0:T(8,128)S(1)}, u32[]{:S(2)}, u32[]{:S(2)}) collective-permute-start(f32[4,128,128]{2,1,0:T(8,128)S(1)} %slice_bitcast_fusion.3), channel_id=1, source_target_pairs={{0,14},{1,49},{2,0},{3,51},{4,2},{5,53},{6,4},{7,55},{8,6},{9,57},... | collective-permute-start | bytes 786440 | tf_op jit(solution)/shard_map/ppermute | solution.py:232
  83.4 12.3 %collective-permute-start.23 = (f32[4,128,128]{2,1,0:T(8,128)S(1)}, f32[4,128,128]{2,1,0:T(8,128)S(1)}, u32[]{:S(2)}, u32[]{:S(2)}) collective-permute-start(f32[4,128,128]{2,1,0:T(8,128)S(1)} %slice_bitcast_fusion.4), channel_id=1, source_target_pairs={{0,2},{1,17},{2,4},{3,19},{4,6},{5,21},{6,8},{7,23},{8,10},{9,25},... | collective-permute-start | bytes 786440 | tf_op jit(solution)/shard_map/ppermute | solution.py:232
  84.6 11.1 %collective-permute-start.22 = (f32[4,128,128]{2,1,0:T(8,128)S(1)}, f32[4,128,128]{2,1,0:T(8,128)S(1)}, u32[]{:S(2)}, u32[]{:S(2)}) collective-permute-start(f32[4,128,128]{2,1,0:T(8,128)S(1)} %collective-permute-done.16.rest_2_), channel_id=1, source_target_pairs={{0,16},{16,32},{32,48},{48,0},{1,17},{17,33},{33,49},{49,1},{2,18}... | collective-permute-start | bytes 786440 | tf_op jit(solution)/shard_map/ppermute | solution.py:220
  95.7 6.0 %collective-permute-start.27 = (f32[2,9,32,128]{3,2,1,0:T(8,128)S(1)}, f32[2,9,32,128]{3,2,1,0:T(8,128)S(1)}, u32[]{:S(2)}, u32[]{:S(2)}) collective-permute-start(f32[2,9,32,128]{3,2,1,0:T(8,128)S(1)} %slice_bitcast_fusion.1), channel_id=1, source_target_pairs={{0,192},{1,65},{64,128},{65,1},{128,64},{129,193},{192,0},{193,129... | collective-permute-start | bytes 884744 | tf_op jit(solution)/shard_map/ppermute | solution.py:259
  95.9 12.7 %collective-permute-start.26 = (f32[2,2,8,32,128]{4,3,2,1,0:T(8,128)S(1)}, f32[2,2,8,32,128]{4,3,2,1,0:T(8,128)S(1)}, u32[]{:S(2)}, u32[]{:S(2)}) collective-permute-start(f32[2,2,8,32,128]{4,3,2,1,0:T(8,128)S(1)} %get-tuple-element.98), channel_id=1, source_target_pairs={{0,64},{1,193},{64,0},{65,129},{128,192},{129,65},{192,128},{193,1... | collective-permute-start | bytes 1572872 | tf_op jit(solution)/shard_map/ppermute | solution.py:255
  108.7 6.0 %collective-permute-start.29 = (f32[2,3,32,128]{3,2,1,0:T(8,128)S(1)}, f32[2,3,32,128]{3,2,1,0:T(8,128)S(1)}, u32[]{:S(2)}, u32[]{:S(2)}) collective-permute-start(f32[2,3,32,128]{3,2,1,0:T(8,128)S(1)} %get-tuple-element.128), channel_id=1, source_target_pairs={{0,64},{1,193},{64,0},{65,129},{128,192},{129,65},{192,128},{193,1... | collective-permute-start | bytes 294920 | tf_op jit(solution)/shard_map/ppermute | solution.py:265
  110.5 4.6 %collective-permute-start.31 = (f32[2,3,32,128]{3,2,1,0:T(8,128)S(1)}, f32[2,3,32,128]{3,2,1,0:T(8,128)S(1)}, u32[]{:S(2)}, u32[]{:S(2)}) collective-permute-start(f32[2,3,32,128]{3,2,1,0:T(8,128)S(1)} %slice_bitcast_fusion.14), channel_id=1, source_target_pairs={{0,192},{1,65},{64,128},{65,1},{128,64},{129,193},{192,0},{193,129... | collective-permute-start | bytes 294920 | tf_op jit(solution)/shard_map/ppermute | solution.py:267
  110.6 6.5 %collective-permute-start.30 = (f32[2,3,32,128]{3,2,1,0:T(8,128)S(1)}, f32[2,3,32,128]{3,2,1,0:T(8,128)S(1)}, u32[]{:S(2)}, u32[]{:S(2)}) collective-permute-start(f32[2,3,32,128]{3,2,1,0:T(8,128)S(1)} %get-tuple-element.127), channel_id=1, source_target_pairs={{0,128},{1,129},{64,192},{65,193},{128,0},{129,1},{192,64},{193,65... | collective-permute-start | bytes 294920 | tf_op jit(solution)/shard_map/ppermute | solution.py:266
  112.8 6.4 %collective-permute-start.28 = (f32[2,8,32,128]{3,2,1,0:T(8,128)S(1)}, f32[2,8,32,128]{3,2,1,0:T(8,128)S(1)}, u32[]{:S(2)}, u32[]{:S(2)}) collective-permute-start(f32[2,8,32,128]{3,2,1,0:T(8,128)S(1)} %slice_bitcast_fusion.2), channel_id=1, source_target_pairs={{0,192},{1,65},{64,128},{65,1},{128,64},{129,193},{192,0},{193,129... | collective-permute-start | bytes 786440 | tf_op jit(solution)/shard_map/ppermute | solution.py:259
  (10 other events, 120.9 us)

commit v5 on v4

--- a/solution.py
+++ b/solution.py
@@ -66,7 +66,7 @@
     return lax.dot_general(a, b, (((1,), (1,)), ((), ())), preferred_element_type=jnp.float32)
 
 
-def work_kernel(names, pos, inverse, side_own, side_sib, blocks, blocks_sib, *rest):
+def work_kernel(names, pos, inverse, inverse_sib, side_own, side_sib, blocks, blocks_sib, *rest):
     arrays, rest = dict(zip(names, rest)), rest[len(names):]
     send, keep, table, sectors, right, wave, lefts, total, sem_r, sem_a, sem_b, sem_t = rest
     slots = slots_of(names)
@@ -92,26 +92,21 @@
         return pltpu.make_async_copy(blocks.at[inverse[sectors[i]]], wave.at[i, 0], sem_a.at[i])
 
     def sib_copy(i):
-        place = table[1, NM, sectors[i]].astype(jnp.int32)
-        return pltpu.make_async_copy(blocks_sib.at[place], wave.at[i, 1], sem_b.at[i])
-
-    def start_own(i, carry):
+        return pltpu.make_async_copy(blocks_sib.at[inverse_sib[sectors[i]]], wave.at[i, 1], sem_b.at[i])
+
+    def start(i, carry):
         own_copy(i).start()
-        return carry
-
-    def start_sib(i, carry):
         sib_copy(i).start()
         return carry
 
-    lax.fori_loop(0, n, start_own, 0)
-    tables[1].wait()
-    lax.fori_loop(0, n, start_sib, 0)
+    lax.fori_loop(0, n, start, 0)
     for side, ref in enumerate((side_own, side_sib)):
         for w in range(NM):
             high, low = split(ref[w * N:(w + 1) * N])
             lefts[side, w * N:(w + 1) * N, :N] = high
             lefts[side, w * N:(w + 1) * N, N:] = low
     tables[0].wait()
+    tables[1].wait()
 
     m = pos[0]
     zero = jnp.zeros((N, N), jnp.bfloat16)
@@ -177,7 +172,7 @@
     return pltpu.with_memory_space_constraint(array, pltpu.HBM)
 
 
-def work(limit, names, pos, inverse, side_own, side_sib, blocks, blocks_sib, got):
+def work(limit, names, pos, inverse, inverse_sib, side_own, side_sib, blocks, blocks_sib, got):
     n = sum(width(name) for name in names)
     arrays = [in_hbm(got[name]) if name in EARLY else got[name] for name in names]
     blocks, blocks_sib = in_hbm(blocks), in_hbm(blocks_sib)
@@ -185,7 +180,7 @@
     return pl.pallas_call(
         functools.partial(work_kernel, names),
         out_shape=(piece,) * 2,
-        in_specs=[SMEM] * 2 + [VMEM] * 2 + [ANY] * (2 + len(arrays)),
+        in_specs=[SMEM] * 3 + [VMEM] * 2 + [ANY] * (2 + len(arrays)),
         out_specs=(VMEM,) * 2,
         scratch_shapes=[
             pltpu.SMEM((2, 8, N), jnp.float32),
@@ -201,7 +196,7 @@
         ],
         compiler_params=pltpu.CompilerParams(vmem_limit_bytes=limit * 2**20),
         name="work",
-    )(pos, inverse, side_own, side_sib, blocks, blocks_sib, *arrays)
+    )(pos, inverse, inverse_sib, side_own, side_sib, blocks, blocks_sib, *arrays)
 
 
 def finish(batches, pos, inverse, pieces):
@@ -301,7 +296,10 @@
     side = jnp.concatenate([left, table], axis=0)
 
     def run(batch):
-        return work(LIMITS[batch], BATCHES[batch], pos, inverse, side, got["side_sib"], wavefunction, got["blocks_sib"], got)
+        inverse_sib = got["side_sib"][NM * N + NM, :NC * HALF].astype(jnp.int32)
+        return work(
+            LIMITS[batch], BATCHES[batch], pos, inverse, inverse_sib, side, got["side_sib"],
+            wavefunction, got["blocks_sib"], got)
 
     arrive(zf1=shift(own, "z", 1), zb1=shift(own, "z", -1))
     arrive(xf1=shift(own, "x", 1), xb1=shift(own, "x", -1))
@@ -323,7 +321,7 @@
         k2f=by_core(pick(jnp.stack([k1f[0], k1f[1], x2]), jnp.stack([zf2, zb2, k1f[0]])), 1),
         k2b=by_core(pick(jnp.stack([k1b[0], k1b[1], x2]), jnp.stack([zf2, zb2, k1b[1]])), -1),
     )
-    got["a"] = run(0)
+    a = got["a"] = run(0)
     tie("zf3", "zb3", "a")
     zf3, zb3 = got["zf3"], got["zb3"]
     arrive(z4=by_core_far(pick(zf3, zb3), "z"))
@@ -335,25 +333,21 @@
         k3f=by_core(pick(k2f, jnp.stack([zb3, k2f[0], zf3])), 1),
         k3b=by_core(pick(k2b, jnp.stack([zf3, k2b[1], zb3])), -1),
     )
-    a = halve(got["a"])
-    b = run(1)
-    got["done"] = a, b
-    tie("df1", "db1", "k3f", "k3b", "done")
+    a = halve(a)
+    b = got["b"] = run(1)
+    tie("df1", "db1", "k3f", "k3b", "b")
 
     k3f, k3b = got["k3f"], got["k3b"]
-    a, b = got["done"]
     arrive(d2=shift(got["df1"], "x", 1))
     arrive(k4f=by_core(k3f[2], 1), k4b=by_core(k3b[2], -1))
-    d = run(2)
+    d = got["d"] = run(2)
     b = halve(b)
-    got["done"] = b, d
-    tie("d2", "k4f", "k4b", "done")
-
-    b, d = got["done"]
+    a = quarter(a)
+    tie("d2", "k4f", "k4b", "d")
+
     e = run(3)
-    d = halve(d)
-    a = quarter(a)
-    a, d, e = fence((a, d, e))
+    d = halve(got["d"])
+    b, d, e = fence((b, d, e))
 
     e = direct(e)
     b = quarter(b)

time: 124 us -> 121 us (0.976)
  waiting for transfers between devices: 40.6 us -> 37.7 us
  Pallas kernels: 27.4 us -> 25.5 us
  starting transfers between devices: 46.1 us -> 48 us
    ppermute x3, waiting for transfers between devices: 11.5 us -> 3.31 us  [halve(): return keep + lax.ppermute(send, ('m', 'c'), hops(1, 3))]
    ppermute x15, waiting for transfers between devices: 18.6 us -> 22.7 us  [shift(): lax.ppermute(array, axis, [(i, (i + step) % size) for i in range(size)])]
    ppermute x3, waiting for transfers between devices: 2.38 us -> 5.8 us  [quarter(): got = lax.ppermute(sums[1], ('m', 'c'), hops(3, 1))]
    ppermute x1, waiting for transfers between devices: 1.98 us -> 0.01 us  [direct(): one = lax.ppermute(send[0], ('m', 'c'), hops(1, 3))]
    pallas_call x4, Pallas kernels: 25.6 us -> 23.7 us  [work(): pl.pallas_call(functools.partial(work_kernel, names), out_shape=(piece,)...]
    ppermute x3, starting transfers between devices: 1.48 us -> 2.85 us  [quarter(): got = lax.ppermute(sums[1], ('m', 'c'), hops(3, 1))]
    ppermute x1, starting transfers between devices: 1.72 us -> 2.98 us  [direct(): one = lax.ppermute(send[0], ('m', 'c'), hops(1, 3))]
  transfers between devices with their start and end apart: 33 -> 33, of which waited for: 15 -> 14; matrix products, arithmetic and copies ran while one was open for 5% -> 6% of each run, Pallas kernels for 21% -> 20%
where the time goes in v5:
time: 121 us
  starting transfers between devices  48 us (40%)
  waiting for transfers between devices  37.7 us (31%)
  Pallas kernels  25.5 us (21%)
  other arithmetic  7.84 us (6%)
    pallas_call x4, Pallas kernels, work(): pl.pallas_call(functools.partial(work_kernel, names), out_shape=(piece,)...  23.7 us
    ppermute x15, starting transfers between devices, shift(): lax.ppermute(array, axis, [(i, (i + step) % size) for i in range(size)])  22.9 us
    ppermute x15, waiting for transfers between devices, shift(): lax.ppermute(array, axis, [(i, (i + step) % size) for i in range(size)])  22.7 us
    ppermute x8, starting transfers between devices, by_core(): return lax.ppermute(array, TENSOR, pairs)  10.5 us
    ppermute x3, starting transfers between devices, halve(): return keep + lax.ppermute(send, ('m', 'c'), hops(1, 3))  7.45 us
    ppermute x3, waiting for transfers between devices, quarter(): got = lax.ppermute(sums[1], ('m', 'c'), hops(3, 1))  5.8 us
    ppermute x3, waiting for transfers between devices, halve(): return keep + lax.ppermute(send, ('m', 'c'), hops(1, 3))  3.31 us
    ppermute x1, starting transfers between devices, direct(): one = lax.ppermute(send[0], ('m', 'c'), hops(1, 3))  2.98 us
  transfers between devices with their start and end apart: 33, of which 14 were waited for; matrix products, arithmetic and copies ran while one was open for 6% of the time, Pallas kernels for 20%

profile of v5, /device:TPU:1, one launch (start us, length us, event | category | flops | bytes accessed | tf_op | source)
XLA Modules:
  0.0 120.6 jit_solution(4096815411964862532)
XLA Ops:
  0.0 3.2 %collective-permute-start.4 = (f32[64,128,128]{2,1,0:T(8,128)}, f32[64,128,128]{2,1,0:T(8,128)}, u32[]{:S(2)}, u32[]{:S(2)}) collective-permute-start(f32[64,128,128]{2,1,0:T(8,128)} %blocks.7), channel_id=1, source_target_pairs={{0,1},{1,0},{2,3},{3,2},{4,5},{5,4},{6,7},{7,6},{8,9},{9,8},{10,11... | collective-permute-start | bytes 12582920 | tf_op jit(solution)/shard_map/ppermute | solution.py:215
  6.5 4.9 %collective-permute-start.1 = (f32[4,128,128]{2,1,0:T(8,128)S(1)}, f32[4,128,128]{2,1,0:T(8,128)S(1)}, u32[]{:S(2)}, u32[]{:S(2)}) collective-permute-start(f32[4,128,128]{2,1,0:T(8,128)S(1)} %bitcast_select_fusion.1.rest_0_), channel_id=1, source_target_pairs={{0,14},{2,0},{4,2},{6,4},{8,6},{10,8},{12,10},{14,12},{1,15},{3,1}... | collective-permute-start | bytes 786440 | tf_op jit(solution)/shard_map/ppermute | solution.py:215
  16.8 3.2 %collective-permute-done.rest_1_ = f32[4,128,128]{2,1,0:T(8,128)} collective-permute-done((f32[4,128,128]{2,1,0:T(8,128)S(1)}, f32[4,128,128]{2,1,0:T(8,128)}, u32[]{:S(2)}, u32[]{:S(2)}) %collective-permute-start) | collective-permute-done | bytes 262176 | tf_op jit(solution)/shard_map/ppermute | solution.py:215
  21.4 1.8 %maximum_select_fusion.2 = f32[2,4,128,128]{3,2,1,0:T(8,128)} fusion(f32[1,4,128,128]{3,2,1,0:T(8,128)S(1)} %bitcast.87, f32[1,4,128,128]{3,2,1,0:T(8,128)S(1)} %bitcast.88, f32[1,4,128,128]{3,2,1,0:T(8,128)S(1)} %bitcast.89, f32[1,4,128,128]{3,2,1,0:T(8,128)} %bitcast.13, pred[]{:T(512)S(6)} %eq.46), kind=kLoop, calls=%fused_computation.7 | loop fusion | flops 393216 | bytes 1572865 | tf_op jit(solution)/shard_map/jit(_where)/select_n | solution.py:274
  23.2 2.7 %collective-permute-start.10 = (f32[2,4,128,128]{3,2,1,0:T(8,128)}, f32[2,4,128,128]{3,2,1,0:T(8,128)S(1)}, u32[]{:S(2)}, u32[]{:S(2)}) collective-permute-start(f32[2,4,128,128]{3,2,1,0:T(8,128)} %maximum_select_fusion.2), channel_id=1, source_target_pairs={{0,14},{1,49},{2,0},{3,51},{4,2},{5,53},{6,4},{7,55},{8,6},{9,57},... | collective-permute-start | bytes 1572872 | tf_op jit(solution)/shard_map/ppermute | solution.py:227
  25.9 2.7 %collective-permute-start.7 = (f32[4,128,128]{2,1,0:T(8,128)S(1)}, f32[4,128,128]{2,1,0:T(8,128)S(1)}, u32[]{:S(2)}, u32[]{:S(2)}) collective-permute-start(f32[4,128,128]{2,1,0:T(8,128)S(1)} %collective-permute-done.1.rest_2_), channel_id=1, source_target_pairs={{0,14},{2,0},{4,2},{6,4},{8,6},{10,8},{12,10},{14,12},{1,15},{3,1}... | collective-permute-start | bytes 786440 | tf_op jit(solution)/shard_map/ppermute | solution.py:215
  28.6 2.7 %collective-permute-start.8 = (f32[4,128,128]{2,1,0:T(8,128)S(1)}, f32[4,128,128]{2,1,0:T(8,128)S(1)}, u32[]{:S(2)}, u32[]{:S(2)}) collective-permute-start(f32[4,128,128]{2,1,0:T(8,128)S(1)} %collective-permute-done.3.rest_4_), channel_id=1, source_target_pairs={{0,48},{16,0},{32,16},{48,32},{1,49},{17,1},{33,17},{49,33},{2,50}... | collective-permute-start | bytes 786440 | tf_op jit(solution)/shard_map/ppermute | solution.py:215
  31.3 4.5 %collective-permute-done.6.rest_5_ = f32[4,128,128]{2,1,0:T(8,128)S(1)} collective-permute-done((f32[4,128,128]{2,1,0:T(8,128)}, f32[4,128,128]{2,1,0:T(8,128)S(1)}, u32[]{:S(2)}, u32[]{:S(2)}) %collective-permute-start.6) | collective-permute-done | bytes 262176 | tf_op jit(solution)/shard_map/ppermute | solution.py:215
  35.8 2.1 %collective-permute-done.8.rest_7_ = f32[4,128,128]{2,1,0:T(8,128)S(1)} collective-permute-done((f32[4,128,128]{2,1,0:T(8,128)S(1)}, f32[4,128,128]{2,1,0:T(8,128)S(1)}, u32[]{:S(2)}, u32[]{:S(2)}) %collective-permute-start.8) | collective-permute-done | bytes 262176 | tf_op jit(solution)/shard_map/ppermute | solution.py:215
  38.0 2.7 %collective-permute-start.14 = (f32[4,128,128]{2,1,0:T(8,128)S(1)}, f32[4,128,128]{2,1,0:T(8,128)S(1)}, u32[]{:S(2)}, u32[]{:S(2)}) collective-permute-start(f32[4,128,128]{2,1,0:T(8,128)S(1)} %collective-permute-done.7.rest_6_), channel_id=1, source_target_pairs={{0,14},{2,0},{4,2},{6,4},{8,6},{10,8},{12,10},{14,12},{1,15},{3,1}... | collective-permute-start | bytes 786440 | tf_op jit(solution)/shard_map/ppermute | solution.py:215
  40.8 3.5 %collective-permute-start.16 = (f32[3,4,128,128]{3,2,1,0:T(8,128)S(1)}, f32[3,4,128,128]{3,2,1,0:T(8,128)S(1)}, u32[]{:S(2)}, u32[]{:S(2)}) collective-permute-start(f32[3,4,128,128]{3,2,1,0:T(8,128)S(1)} %get-tuple-element.107), channel_id=1, source_target_pairs={{0,14},{1,49},{2,0},{3,51},{4,2},{5,53},{6,4},{7,55},{8,6},{9,57},... | collective-permute-start | bytes 2359304 | tf_op jit(solution)/shard_map/ppermute | solution.py:227
  44.5 8.6 %work.4 = (f32[2,2,12,32,128]{4,3,2,1,0:T(8,128)S(1)}, f32[2,2,12,32,128]{4,3,2,1,0:T(8,128)S(1)}) custom-call(s32[4]{0:T(128)S(1)} %pad_add_fusion.pos, s32[64]{0:T(128)S(1)} %select_reduce_fusion.2.inverse, s32[64]{0:T(128)S(1)} %convert_bitcast_fusion.inverse_sib, f32[520,128]{1,0:T(8,128)S(1)} %pad_maximum_fusion.4.side_own, ...), custom_call_target="tpu_custom_call" | custom-call | tf_op jit(solution)/shard_map/work/pallas_call | solution.py:180
  53.2 2.8 %collective-permute-start.11 = (f32[2,2,12,32,128]{4,3,2,1,0:T(8,128)S(1)}, f32[2,2,12,32,128]{4,3,2,1,0:T(8,128)S(1)}, u32[]{:S(2)}, u32[]{:S(2)}) collective-permute-start(f32[2,2,12,32,128]{4,3,2,1,0:T(8,128)S(1)} %get-tuple-element.70), channel_id=1, source_target_pairs={{0,64},{1,193},{64,0},{65,129},{128,192},{129,65},{192,128},{193,1... | collective-permute-start | bytes 2359304 | tf_op jit(solution)/shard_map/ppermute | solution.py:250
  56.0 2.7 %collective-permute-done.17.rest_2_ = f32[4,128,128]{2,1,0:T(8,128)S(1)} collective-permute-done((f32[4,128,128]{2,1,0:T(8,128)S(1)}, f32[4,128,128]{2,1,0:T(8,128)S(1)}, u32[]{:S(2)}, u32[]{:S(2)}) %collective-permute-start.17) | collective-permute-done | bytes 262176 | tf_op jit(solution)/shard_map/ppermute | solution.py:237
  58.9 2.8 %collective-permute-start.22 = (f32[3,4,128,128]{3,2,1,0:T(8,128)S(1)}, f32[3,4,128,128]{3,2,1,0:T(8,128)S(1)}, u32[]{:S(2)}, u32[]{:S(2)}) collective-permute-start(f32[3,4,128,128]{3,2,1,0:T(8,128)S(1)} %get-tuple-element.109), channel_id=1, source_target_pairs={{0,14},{1,49},{2,0},{3,51},{4,2},{5,53},{6,4},{7,55},{8,6},{9,57},... | collective-permute-start | bytes 2359304 | tf_op jit(solution)/shard_map/ppermute | solution.py:227
  61.8 2.7 %collective-permute-start.20 = (f32[4,128,128]{2,1,0:T(8,128)S(1)}, f32[4,128,128]{2,1,0:T(8,128)S(1)}, u32[]{:S(2)}, u32[]{:S(2)}) collective-permute-start(f32[4,128,128]{2,1,0:T(8,128)S(1)} %collective-permute-done.17.rest_2_), channel_id=1, source_target_pairs={{0,48},{16,0},{32,16},{48,32},{1,49},{17,1},{33,17},{49,33},{2,50}... | collective-permute-start | bytes 786440 | tf_op jit(solution)/shard_map/ppermute | solution.py:215
  64.4 6.3 %work.5 = (f32[2,2,9,32,128]{4,3,2,1,0:T(8,128)S(1)}, f32[2,2,9,32,128]{4,3,2,1,0:T(8,128)S(1)}) custom-call(s32[4]{0:T(128)S(1)} %pad_add_fusion.pos, s32[64]{0:T(128)S(1)} %select_reduce_fusion.2.inverse, s32[64]{0:T(128)S(1)} %convert_bitcast_fusion.inverse_sib, f32[520,128]{1,0:T(8,128)S(1)} %pad_maximum_fusion.4.side_own, ...), custom_call_target="tpu_custom_call" | custom-call | tf_op jit(solution)/shard_map/work/pallas_call | solution.py:180
  70.9 5.4 %collective-permute-done.20.rest_3_ = f32[4,128,128]{2,1,0:T(8,128)S(1)} collective-permute-done((f32[4,128,128]{2,1,0:T(8,128)S(1)}, f32[4,128,128]{2,1,0:T(8,128)S(1)}, u32[]{:S(2)}, u32[]{:S(2)}) %collective-permute-start.20) | collective-permute-done | bytes 262176 | tf_op jit(solution)/shard_map/ppermute | solution.py:215
  76.3 3.1 %collective-permute-done.19.rest_2_ = f32[4,128,128]{2,1,0:T(8,128)S(1)} collective-permute-done((f32[4,128,128]{2,1,0:T(8,128)S(1)}, f32[4,128,128]{2,1,0:T(8,128)S(1)}, u32[]{:S(2)}, u32[]{:S(2)}) %collective-permute-start.19) | collective-permute-done | bytes 262176 | tf_op jit(solution)/shard_map/ppermute | solution.py:215
  79.6 1.5 %collective-permute-start.24 = (f32[4,128,128]{2,1,0:T(8,128)S(1)}, f32[4,128,128]{2,1,0:T(8,128)S(1)}, u32[]{:S(2)}, u32[]{:S(2)}) collective-permute-start(f32[4,128,128]{2,1,0:T(8,128)S(1)} %slice_bitcast_fusion.4), channel_id=1, source_target_pairs={{0,2},{1,17},{2,4},{3,19},{4,6},{5,21},{6,8},{7,23},{8,10},{9,25},... | collective-permute-start | bytes 786440 | tf_op jit(solution)/shard_map/ppermute | solution.py:227
  82.5 1.9 %collective-permute-start.18 = (f32[2,2,9,32,128]{4,3,2,1,0:T(8,128)S(1)}, f32[2,2,9,32,128]{4,3,2,1,0:T(8,128)S(1)}, u32[]{:S(2)}, u32[]{:S(2)}) collective-permute-start(f32[2,2,9,32,128]{4,3,2,1,0:T(8,128)S(1)} %get-tuple-element.77), channel_id=1, source_target_pairs={{0,64},{1,193},{64,0},{65,129},{128,192},{129,65},{192,128},{193,1... | collective-permute-start | bytes 1769480 | tf_op jit(solution)/shard_map/ppermute | solution.py:250
  84.4 5.8 %work.6 = (f32[2,2,8,32,128]{4,3,2,1,0:T(8,128)S(1)}, f32[2,2,8,32,128]{4,3,2,1,0:T(8,128)S(1)}) custom-call(s32[4]{0:T(128)S(1)} %pad_add_fusion.pos, s32[64]{0:T(128)S(1)} %select_reduce_fusion.2.inverse, s32[64]{0:T(128)S(1)} %convert_bitcast_fusion.inverse_sib, f32[520,128]{1,0:T(8,128)S(1)} %pad_maximum_fusion.4.side_own, ...), custom_call_target="tpu_custom_call" | custom-call | tf_op jit(solution)/shard_map/work/pallas_call | solution.py:180
  90.2 1.5 %collective-permute-done.23.rest_2_ = f32[4,128,128]{2,1,0:T(8,128)S(1)} collective-permute-done((f32[4,128,128]{2,1,0:T(8,128)S(1)}, f32[4,128,128]{2,1,0:T(8,128)S(1)}, u32[]{:S(2)}, u32[]{:S(2)}) %collective-permute-start.23) | collective-permute-done | bytes 262176 | tf_op jit(solution)/shard_map/ppermute | solution.py:215
  91.7 2.7 %collective-permute-start.26 = (f32[2,2,8,32,128]{4,3,2,1,0:T(8,128)S(1)}, f32[2,2,8,32,128]{4,3,2,1,0:T(8,128)S(1)}, u32[]{:S(2)}, u32[]{:S(2)}) collective-permute-start(f32[2,2,8,32,128]{4,3,2,1,0:T(8,128)S(1)} %get-tuple-element.85), channel_id=1, source_target_pairs={{0,64},{1,193},{64,0},{65,129},{128,192},{129,65},{192,128},{193,1... | collective-permute-start | bytes 1572872 | tf_op jit(solution)/shard_map/ppermute | solution.py:250
  94.6 3.1 %work.7 = (f32[2,2,3,32,128]{4,3,2,1,0:T(8,128)S(1)}, f32[2,2,3,32,128]{4,3,2,1,0:T(8,128)S(1)}) custom-call(s32[4]{0:T(128)S(1)} %pad_add_fusion.pos, s32[64]{0:T(128)S(1)} %select_reduce_fusion.2.inverse, s32[64]{0:T(128)S(1)} %convert_bitcast_fusion.inverse_sib, f32[520,128]{1,0:T(8,128)S(1)} %pad_maximum_fusion.4.side_own, ...), custom_call_target="tpu_custom_call" | custom-call | tf_op jit(solution)/shard_map/work/pallas_call | solution.py:180
  97.7 3.3 %collective-permute-done.26 = f32[2,2,8,32,128]{4,3,2,1,0:T(8,128)S(1)} collective-permute-done((f32[2,2,8,32,128]{4,3,2,1,0:T(8,128)S(1)}, f32[2,2,8,32,128]{4,3,2,1,0:T(8,128)S(1)}, u32[]{:S(2)}, u32[]{:S(2)}) %collective-permute-start.26) | collective-permute-done | bytes 524320 | tf_op jit(solution)/shard_map/ppermute | solution.py:250
  101.2 3.0 %collective-permute-start.29 = (f32[2,3,32,128]{3,2,1,0:T(8,128)S(1)}, f32[2,3,32,128]{3,2,1,0:T(8,128)S(1)}, u32[]{:S(2)}, u32[]{:S(2)}) collective-permute-start(f32[2,3,32,128]{3,2,1,0:T(8,128)S(1)} %get-tuple-element.112), channel_id=1, source_target_pairs={{0,64},{1,193},{64,0},{65,129},{128,192},{129,65},{192,128},{193,1... | collective-permute-start | bytes 294920 | tf_op jit(solution)/shard_map/ppermute | solution.py:260
  108.0 2.2 %collective-permute-done.30 = f32[2,3,32,128]{3,2,1,0:T(8,128)S(1)} collective-permute-done((f32[2,3,32,128]{3,2,1,0:T(8,128)S(1)}, f32[2,3,32,128]{3,2,1,0:T(8,128)S(1)}, u32[]{:S(2)}, u32[]{:S(2)}) %collective-permute-start.30) | collective-permute-done | bytes 98336 | tf_op jit(solution)/shard_map/ppermute | solution.py:261
  110.3 2.7 %collective-permute-done.28 = f32[2,8,32,128]{3,2,1,0:T(8,128)S(1)} collective-permute-done((f32[2,8,32,128]{3,2,1,0:T(8,128)S(1)}, f32[2,8,32,128]{3,2,1,0:T(8,128)S(1)}, u32[]{:S(2)}, u32[]{:S(2)}) %collective-permute-start.28) | collective-permute-done | bytes 262176 | tf_op jit(solution)/shard_map/ppermute | solution.py:254
  113.0 3.1 %collective-permute-done.27 = f32[2,9,32,128]{3,2,1,0:T(8,128)S(1)} collective-permute-done((f32[2,9,32,128]{3,2,1,0:T(8,128)S(1)}, f32[2,9,32,128]{3,2,1,0:T(8,128)S(1)}, u32[]{:S(2)}, u32[]{:S(2)}) %collective-permute-start.27) | collective-permute-done | bytes 294944 | tf_op jit(solution)/shard_map/ppermute | solution.py:254
  117.2 1.5 %collective-permute-done.32.rest_8_ = f32[32,32,128]{2,1,0:T(8,128)S(1)} collective-permute-done((f32[32,32,128]{2,1,0:T(8,128)S(1)}, f32[32,32,128]{2,1,0:T(8,128)S(1)}, u32[]{:S(2)}, u32[]{:S(2)}) %collective-permute-start.32) | collective-permute-done | bytes 524320 | tf_op jit(solution)/shard_map/ppermute | solution.py:215
  118.8 1.8 %finish.1 = f32[64,32,128]{2,1,0:T(8,128)} custom-call(s32[4]{0:T(128)S(1)} %pad_add_fusion.pos, s32[64]{0:T(128)S(1)} %select_reduce_fusion.2.inverse, f32[12,32,128]{2,1,0:T(8,128)S(1)} %slice_bitcast_fusion.8.rest_0_, f32[12,32,128]{2,1,0:T(8,128)S(1)} %slice_bitcast_fusion.7.rest_1_, f32[9,32,128]{2,1,0:T(8,128)S(1)} %slice_bitcast_fusion.11.rest_2_, ...), custom_call_target="tpu_custom_call" | custom-call | tf_op jit(solution)/shard_map/finish/pallas_call | solution.py:203
  (103 shorter events, 17.2 us)
Async XLA Ops:
  0.0 20.0 %collective-permute-start.4 = (f32[64,128,128]{2,1,0:T(8,128)}, f32[64,128,128]{2,1,0:T(8,128)}, u32[]{:S(2)}, u32[]{:S(2)}) collective-permute-start(f32[64,128,128]{2,1,0:T(8,128)} %blocks.7), channel_id=1, source_target_pairs={{0,1},{1,0},{2,3},{3,2},{4,5},{5,4},{6,7},{7,6},{8,9},{9,8},{10,11... | collective-permute-start | bytes 12582920 | tf_op jit(solution)/shard_map/ppermute | solution.py:215
  5.0 10.5 %collective-permute-start.3 = (f32[4,128,128]{2,1,0:T(8,128)S(1)}, f32[4,128,128]{2,1,0:T(8,128)S(1)}, u32[]{:S(2)}, u32[]{:S(2)}) collective-permute-start(f32[4,128,128]{2,1,0:T(8,128)S(1)} %bitcast_select_fusion.1.rest_0_), channel_id=1, source_target_pairs={{0,48},{16,0},{32,16},{48,32},{1,49},{17,1},{33,17},{49,33},{2,50}... | collective-permute-start | bytes 786440 | tf_op jit(solution)/shard_map/ppermute | solution.py:215
  5.8 9.7 %collective-permute-start.2 = (f32[4,128,128]{2,1,0:T(8,128)S(1)}, f32[4,128,128]{2,1,0:T(8,128)S(1)}, u32[]{:S(2)}, u32[]{:S(2)}) collective-permute-start(f32[4,128,128]{2,1,0:T(8,128)S(1)} %bitcast_select_fusion.1.rest_0_), channel_id=1, source_target_pairs={{0,16},{16,32},{32,48},{48,0},{1,17},{17,33},{33,49},{49,1},{2,18}... | collective-permute-start | bytes 786440 | tf_op jit(solution)/shard_map/ppermute | solution.py:215
  6.5 10.3 %collective-permute-start.1 = (f32[4,128,128]{2,1,0:T(8,128)S(1)}, f32[4,128,128]{2,1,0:T(8,128)S(1)}, u32[]{:S(2)}, u32[]{:S(2)}) collective-permute-start(f32[4,128,128]{2,1,0:T(8,128)S(1)} %bitcast_select_fusion.1.rest_0_), channel_id=1, source_target_pairs={{0,14},{2,0},{4,2},{6,4},{8,6},{10,8},{12,10},{14,12},{1,15},{3,1}... | collective-permute-start | bytes 786440 | tf_op jit(solution)/shard_map/ppermute | solution.py:215
  11.4 8.6 %collective-permute-start = (f32[4,128,128]{2,1,0:T(8,128)S(1)}, f32[4,128,128]{2,1,0:T(8,128)}, u32[]{:S(2)}, u32[]{:S(2)}) collective-permute-start(f32[4,128,128]{2,1,0:T(8,128)S(1)} %bitcast_select_fusion.1.rest_0_), channel_id=1, source_target_pairs={{0,2},{2,4},{4,6},{6,8},{8,10},{10,12},{12,14},{14,0},{1,3},{3,5},... | collective-permute-start | bytes 786440 | tf_op jit(solution)/shard_map/ppermute | solution.py:215
  20.0 8.6 %collective-permute-start.5 = (f32[520,128]{1,0:T(8,128)S(1)}, f32[520,128]{1,0:T(8,128)S(1)}, u32[]{:S(2)}, u32[]{:S(2)}) collective-permute-start(f32[520,128]{1,0:T(8,128)S(1)} %pad_maximum_fusion.4.side_own), channel_id=1, source_target_pairs={{0,1},{1,0},{2,3},{3,2},{4,5},{5,4},{6,7},{7,6},{8,9},{9,8},{10,11... | collective-permute-start | bytes 798728 | tf_op jit(solution)/shard_map/ppermute | solution.py:215
  23.2 12.5 %collective-permute-start.10 = (f32[2,4,128,128]{3,2,1,0:T(8,128)}, f32[2,4,128,128]{3,2,1,0:T(8,128)S(1)}, u32[]{:S(2)}, u32[]{:S(2)}) collective-permute-start(f32[2,4,128,128]{3,2,1,0:T(8,128)} %maximum_select_fusion.2), channel_id=1, source_target_pairs={{0,14},{1,49},{2,0},{3,51},{4,2},{5,53},{6,4},{7,55},{8,6},{9,57},... | collective-permute-start | bytes 1572872 | tf_op jit(solution)/shard_map/ppermute | solution.py:227
  25.9 9.8 %collective-permute-start.9 = (f32[2,4,128,128]{3,2,1,0:T(8,128)}, f32[2,4,128,128]{3,2,1,0:T(8,128)S(1)}, u32[]{:S(2)}, u32[]{:S(2)}) collective-permute-start(f32[2,4,128,128]{3,2,1,0:T(8,128)} %maximum_select_fusion.2), channel_id=1, source_target_pairs={{0,2},{1,17},{2,4},{3,19},{4,6},{5,21},{6,8},{7,23},{8,10},{9,25},... | collective-permute-start | bytes 1572872 | tf_op jit(solution)/shard_map/ppermute | solution.py:227
  25.9 9.8 %collective-permute-start.6 = (f32[4,128,128]{2,1,0:T(8,128)}, f32[4,128,128]{2,1,0:T(8,128)S(1)}, u32[]{:S(2)}, u32[]{:S(2)}) collective-permute-start(f32[4,128,128]{2,1,0:T(8,128)} %collective-permute-done.rest_1_), channel_id=1, source_target_pairs={{0,2},{2,4},{4,6},{6,8},{8,10},{10,12},{12,14},{14,0},{1,3},{3,5},... | collective-permute-start | bytes 786440 | tf_op jit(solution)/shard_map/ppermute | solution.py:215
  25.9 9.8 %collective-permute-start.7 = (f32[4,128,128]{2,1,0:T(8,128)S(1)}, f32[4,128,128]{2,1,0:T(8,128)S(1)}, u32[]{:S(2)}, u32[]{:S(2)}) collective-permute-start(f32[4,128,128]{2,1,0:T(8,128)S(1)} %collective-permute-done.1.rest_2_), channel_id=1, source_target_pairs={{0,14},{2,0},{4,2},{6,4},{8,6},{10,8},{12,10},{14,12},{1,15},{3,1}... | collective-permute-start | bytes 786440 | tf_op jit(solution)/shard_map/ppermute | solution.py:215
  28.6 9.3 %collective-permute-start.8 = (f32[4,128,128]{2,1,0:T(8,128)S(1)}, f32[4,128,128]{2,1,0:T(8,128)S(1)}, u32[]{:S(2)}, u32[]{:S(2)}) collective-permute-start(f32[4,128,128]{2,1,0:T(8,128)S(1)} %collective-permute-done.3.rest_4_), channel_id=1, source_target_pairs={{0,48},{16,0},{32,16},{48,32},{1,49},{17,1},{33,17},{49,33},{2,50}... | collective-permute-start | bytes 786440 | tf_op jit(solution)/shard_map/ppermute | solution.py:215
  37.9 15.1 %collective-permute-start.13 = (f32[4,128,128]{2,1,0:T(8,128)S(1)}, f32[4,128,128]{2,1,0:T(8,128)S(1)}, u32[]{:S(2)}, u32[]{:S(2)}) collective-permute-start(f32[4,128,128]{2,1,0:T(8,128)S(1)} %collective-permute-done.6.rest_5_), channel_id=1, source_target_pairs={{0,2},{2,4},{4,6},{6,8},{8,10},{10,12},{12,14},{14,0},{1,3},{3,5},... | collective-permute-start | bytes 786440 | tf_op jit(solution)/shard_map/ppermute | solution.py:215
  38.0 15.0 %collective-permute-start.14 = (f32[4,128,128]{2,1,0:T(8,128)S(1)}, f32[4,128,128]{2,1,0:T(8,128)S(1)}, u32[]{:S(2)}, u32[]{:S(2)}) collective-permute-start(f32[4,128,128]{2,1,0:T(8,128)S(1)} %collective-permute-done.7.rest_6_), channel_id=1, source_target_pairs={{0,14},{2,0},{4,2},{6,4},{8,6},{10,8},{12,10},{14,12},{1,15},{3,1}... | collective-permute-start | bytes 786440 | tf_op jit(solution)/shard_map/ppermute | solution.py:215
  40.8 17.9 %collective-permute-start.16 = (f32[3,4,128,128]{3,2,1,0:T(8,128)S(1)}, f32[3,4,128,128]{3,2,1,0:T(8,128)S(1)}, u32[]{:S(2)}, u32[]{:S(2)}) collective-permute-start(f32[3,4,128,128]{3,2,1,0:T(8,128)S(1)} %get-tuple-element.107), channel_id=1, source_target_pairs={{0,14},{1,49},{2,0},{3,51},{4,2},{5,53},{6,4},{7,55},{8,6},{9,57},... | collective-permute-start | bytes 2359304 | tf_op jit(solution)/shard_map/ppermute | solution.py:227
  44.3 14.4 %collective-permute-start.15 = (f32[3,4,128,128]{3,2,1,0:T(8,128)S(1)}, f32[3,4,128,128]{3,2,1,0:T(8,128)S(1)}, u32[]{:S(2)}, u32[]{:S(2)}) collective-permute-start(f32[3,4,128,128]{3,2,1,0:T(8,128)S(1)} %get-tuple-element.108), channel_id=1, source_target_pairs={{0,2},{1,17},{2,4},{3,19},{4,6},{5,21},{6,8},{7,23},{8,10},{9,25},... | collective-permute-start | bytes 2359304 | tf_op jit(solution)/shard_map/ppermute | solution.py:227
  53.1 5.6 %collective-permute-start.17 = (f32[4,128,128]{2,1,0:T(8,128)S(1)}, f32[4,128,128]{2,1,0:T(8,128)S(1)}, u32[]{:S(2)}, u32[]{:S(2)}) collective-permute-start(f32[4,128,128]{2,1,0:T(8,128)S(1)} %broadcast_select_fusion), channel_id=1, source_target_pairs={{0,2},{1,15},{2,4},{3,1},{4,6},{5,3},{6,8},{7,5},{8,10},{9,7},{10,... | collective-permute-start | bytes 786440 | tf_op jit(solution)/shard_map/ppermute | solution.py:237
  53.2 17.5 %collective-permute-start.11 = (f32[2,2,12,32,128]{4,3,2,1,0:T(8,128)S(1)}, f32[2,2,12,32,128]{4,3,2,1,0:T(8,128)S(1)}, u32[]{:S(2)}, u32[]{:S(2)}) collective-permute-start(f32[2,2,12,32,128]{4,3,2,1,0:T(8,128)S(1)} %get-tuple-element.70), channel_id=1, source_target_pairs={{0,64},{1,193},{64,0},{65,129},{128,192},{129,65},{192,128},{193,1... | collective-permute-start | bytes 2359304 | tf_op jit(solution)/shard_map/ppermute | solution.py:250
  58.9 20.5 %collective-permute-start.22 = (f32[3,4,128,128]{3,2,1,0:T(8,128)S(1)}, f32[3,4,128,128]{3,2,1,0:T(8,128)S(1)}, u32[]{:S(2)}, u32[]{:S(2)}) collective-permute-start(f32[3,4,128,128]{3,2,1,0:T(8,128)S(1)} %get-tuple-element.109), channel_id=1, source_target_pairs={{0,14},{1,49},{2,0},{3,51},{4,2},{5,53},{6,4},{7,55},{8,6},{9,57},... | collective-permute-start | bytes 2359304 | tf_op jit(solution)/shard_map/ppermute | solution.py:227
  61.8 17.7 %collective-permute-start.21 = (f32[3,4,128,128]{3,2,1,0:T(8,128)S(1)}, f32[3,4,128,128]{3,2,1,0:T(8,128)S(1)}, u32[]{:S(2)}, u32[]{:S(2)}) collective-permute-start(f32[3,4,128,128]{3,2,1,0:T(8,128)S(1)} %get-tuple-element.110), channel_id=1, source_target_pairs={{0,2},{1,17},{2,4},{3,19},{4,6},{5,21},{6,8},{7,23},{8,10},{9,25},... | collective-permute-start | bytes 2359304 | tf_op jit(solution)/shard_map/ppermute | solution.py:227
  61.8 14.5 %collective-permute-start.20 = (f32[4,128,128]{2,1,0:T(8,128)S(1)}, f32[4,128,128]{2,1,0:T(8,128)S(1)}, u32[]{:S(2)}, u32[]{:S(2)}) collective-permute-start(f32[4,128,128]{2,1,0:T(8,128)S(1)} %collective-permute-done.17.rest_2_), channel_id=1, source_target_pairs={{0,48},{16,0},{32,16},{48,32},{1,49},{17,1},{33,17},{49,33},{2,50}... | collective-permute-start | bytes 786440 | tf_op jit(solution)/shard_map/ppermute | solution.py:215
  64.4 15.0 %collective-permute-start.19 = (f32[4,128,128]{2,1,0:T(8,128)S(1)}, f32[4,128,128]{2,1,0:T(8,128)S(1)}, u32[]{:S(2)}, u32[]{:S(2)}) collective-permute-start(f32[4,128,128]{2,1,0:T(8,128)S(1)} %collective-permute-done.17.rest_2_), channel_id=1, source_target_pairs={{0,16},{16,32},{32,48},{48,0},{1,17},{17,33},{33,49},{49,1},{2,18}... | collective-permute-start | bytes 786440 | tf_op jit(solution)/shard_map/ppermute | solution.py:215
  79.5 10.7 %collective-permute-start.25 = (f32[4,128,128]{2,1,0:T(8,128)S(1)}, f32[4,128,128]{2,1,0:T(8,128)S(1)}, u32[]{:S(2)}, u32[]{:S(2)}) collective-permute-start(f32[4,128,128]{2,1,0:T(8,128)S(1)} %slice_bitcast_fusion.3), channel_id=1, source_target_pairs={{0,14},{1,49},{2,0},{3,51},{4,2},{5,53},{6,4},{7,55},{8,6},{9,57},... | collective-permute-start | bytes 786440 | tf_op jit(solution)/shard_map/ppermute | solution.py:227
  79.6 10.6 %collective-permute-start.24 = (f32[4,128,128]{2,1,0:T(8,128)S(1)}, f32[4,128,128]{2,1,0:T(8,128)S(1)}, u32[]{:S(2)}, u32[]{:S(2)}) collective-permute-start(f32[4,128,128]{2,1,0:T(8,128)S(1)} %slice_bitcast_fusion.4), channel_id=1, source_target_pairs={{0,2},{1,17},{2,4},{3,19},{4,6},{5,21},{6,8},{7,23},{8,10},{9,25},... | collective-permute-start | bytes 786440 | tf_op jit(solution)/shard_map/ppermute | solution.py:227
  81.0 10.7 %collective-permute-start.23 = (f32[4,128,128]{2,1,0:T(8,128)S(1)}, f32[4,128,128]{2,1,0:T(8,128)S(1)}, u32[]{:S(2)}, u32[]{:S(2)}) collective-permute-start(f32[4,128,128]{2,1,0:T(8,128)S(1)} %collective-permute-done.19.rest_2_), channel_id=1, source_target_pairs={{0,16},{16,32},{32,48},{48,0},{1,17},{17,33},{33,49},{49,1},{2,18}... | collective-permute-start | bytes 786440 | tf_op jit(solution)/shard_map/ppermute | solution.py:215
  81.1 13.4 %collective-permute-start.12 = (f32[2,12,32,128]{3,2,1,0:T(8,128)S(1)}, f32[2,12,32,128]{3,2,1,0:T(8,128)S(1)}, u32[]{:S(2)}, u32[]{:S(2)}) collective-permute-start(f32[2,12,32,128]{3,2,1,0:T(8,128)S(1)} %slice_bitcast_fusion), channel_id=1, source_target_pairs={{0,192},{1,65},{64,128},{65,1},{128,64},{129,193},{192,0},{193,129... | collective-permute-start | bytes 1179656 | tf_op jit(solution)/shard_map/ppermute | solution.py:254
  82.5 12.1 %collective-permute-start.18 = (f32[2,2,9,32,128]{4,3,2,1,0:T(8,128)S(1)}, f32[2,2,9,32,128]{4,3,2,1,0:T(8,128)S(1)}, u32[]{:S(2)}, u32[]{:S(2)}) collective-permute-start(f32[2,2,9,32,128]{4,3,2,1,0:T(8,128)S(1)} %get-tuple-element.77), channel_id=1, source_target_pairs={{0,64},{1,193},{64,0},{65,129},{128,192},{129,65},{192,128},{193,1... | collective-permute-start | bytes 1769480 | tf_op jit(solution)/shard_map/ppermute | solution.py:250
  91.7 9.3 %collective-permute-start.26 = (f32[2,2,8,32,128]{4,3,2,1,0:T(8,128)S(1)}, f32[2,2,8,32,128]{4,3,2,1,0:T(8,128)S(1)}, u32[]{:S(2)}, u32[]{:S(2)}) collective-permute-start(f32[2,2,8,32,128]{4,3,2,1,0:T(8,128)S(1)} %get-tuple-element.85), channel_id=1, source_target_pairs={{0,64},{1,193},{64,0},{65,129},{128,192},{129,65},{192,128},{193,1... | collective-permute-start | bytes 1572872 | tf_op jit(solution)/shard_map/ppermute | solution.py:250
  101.2 5.8 %collective-permute-start.29 = (f32[2,3,32,128]{3,2,1,0:T(8,128)S(1)}, f32[2,3,32,128]{3,2,1,0:T(8,128)S(1)}, u32[]{:S(2)}, u32[]{:S(2)}) collective-permute-start(f32[2,3,32,128]{3,2,1,0:T(8,128)S(1)} %get-tuple-element.112), channel_id=1, source_target_pairs={{0,64},{1,193},{64,0},{65,129},{128,192},{129,65},{192,128},{193,1... | collective-permute-start | bytes 294920 | tf_op jit(solution)/shard_map/ppermute | solution.py:260
  104.2 3.8 %collective-permute-start.31 = (f32[2,3,32,128]{3,2,1,0:T(8,128)S(1)}, f32[2,3,32,128]{3,2,1,0:T(8,128)S(1)}, u32[]{:S(2)}, u32[]{:S(2)}) collective-permute-start(f32[2,3,32,128]{3,2,1,0:T(8,128)S(1)} %slice_bitcast_fusion.15), channel_id=1, source_target_pairs={{0,192},{1,65},{64,128},{65,1},{128,64},{129,193},{192,0},{193,129... | collective-permute-start | bytes 294920 | tf_op jit(solution)/shard_map/ppermute | solution.py:262
  104.3 5.9 %collective-permute-start.30 = (f32[2,3,32,128]{3,2,1,0:T(8,128)S(1)}, f32[2,3,32,128]{3,2,1,0:T(8,128)S(1)}, u32[]{:S(2)}, u32[]{:S(2)}) collective-permute-start(f32[2,3,32,128]{3,2,1,0:T(8,128)S(1)} %get-tuple-element.111), channel_id=1, source_target_pairs={{0,128},{1,129},{64,192},{65,193},{128,0},{129,1},{192,64},{193,65... | collective-permute-start | bytes 294920 | tf_op jit(solution)/shard_map/ppermute | solution.py:261
  105.5 7.5 %collective-permute-start.28 = (f32[2,8,32,128]{3,2,1,0:T(8,128)S(1)}, f32[2,8,32,128]{3,2,1,0:T(8,128)S(1)}, u32[]{:S(2)}, u32[]{:S(2)}) collective-permute-start(f32[2,8,32,128]{3,2,1,0:T(8,128)S(1)} %slice_bitcast_fusion.2), channel_id=1, source_target_pairs={{0,192},{1,65},{64,128},{65,1},{128,64},{129,193},{192,0},{193,129... | collective-permute-start | bytes 786440 | tf_op jit(solution)/shard_map/ppermute | solution.py:254
  105.7 10.4 %collective-permute-start.27 = (f32[2,9,32,128]{3,2,1,0:T(8,128)S(1)}, f32[2,9,32,128]{3,2,1,0:T(8,128)S(1)}, u32[]{:S(2)}, u32[]{:S(2)}) collective-permute-start(f32[2,9,32,128]{3,2,1,0:T(8,128)S(1)} %slice_bitcast_fusion.1), channel_id=1, source_target_pairs={{0,192},{1,65},{64,128},{65,1},{128,64},{129,193},{192,0},{193,129... | collective-permute-start | bytes 884744 | tf_op jit(solution)/shard_map/ppermute | solution.py:254
  (10 other events, 168.9 us)

commit v6 on v5

--- a/solution.py
+++ b/solution.py
@@ -35,7 +35,6 @@
 )
 
 EARLY = ("own", "zf1", "zb1", "xf1", "xb1", "x2", "zf2", "zb2", "k1f", "k1b")
-LIMITS = (12, 12, 12, 12)
 
 
 def slots_of(names):
@@ -66,9 +65,14 @@
     return lax.dot_general(a, b, (((1,), (1,)), ((), ())), preferred_element_type=jnp.float32)
 
 
-def work_kernel(names, pos, inverse, inverse_sib, side_own, side_sib, blocks, blocks_sib, *rest):
+def work_kernel(first, names, pos, inverse, inverse_sib, side_own, side_sib, blocks, blocks_sib, *rest):
+    if not first:
+        lefts, rest = rest[0], rest[1:]
     arrays, rest = dict(zip(names, rest)), rest[len(names):]
-    send, keep, table, sectors, right, wave, lefts, total, sem_r, sem_a, sem_b, sem_t = rest
+    send, keep, *rest = rest
+    if first:
+        lefts, rest = rest[0], rest[1:]
+    table, sectors, right, wave, total, sem_r, sem_a, sem_b, sem_t = rest
     slots = slots_of(names)
     n = len(slots)
 
@@ -100,11 +104,12 @@
         return carry
 
     lax.fori_loop(0, n, start, 0)
-    for side, ref in enumerate((side_own, side_sib)):
-        for w in range(NM):
-            high, low = split(ref[w * N:(w + 1) * N])
-            lefts[side, w * N:(w + 1) * N, :N] = high
-            lefts[side, w * N:(w + 1) * N, N:] = low
+    if first:
+        for side, ref in enumerate((side_own, side_sib)):
+            for w in range(NM):
+                high, low = split(ref[w * N:(w + 1) * N])
+                lefts[side, w * N:(w + 1) * N, :N] = high
+                lefts[side, w * N:(w + 1) * N, N:] = low
     tables[0].wait()
     tables[1].wait()
 
@@ -172,31 +177,32 @@
     return pltpu.with_memory_space_constraint(array, pltpu.HBM)
 
 
-def work(limit, names, pos, inverse, inverse_sib, side_own, side_sib, blocks, blocks_sib, got):
+def work(names, pos, inverse, inverse_sib, side_own, side_sib, blocks, blocks_sib, got, lefts):
+    first = lefts is None
+    given = [] if first else [lefts]
     n = sum(width(name) for name in names)
     arrays = [in_hbm(got[name]) if name in EARLY else got[name] for name in names]
     blocks, blocks_sib = in_hbm(blocks), in_hbm(blocks_sib)
     piece = jax.ShapeDtypeStruct((2, 2, n, N // NM, N), jnp.float32)
     return pl.pallas_call(
-        functools.partial(work_kernel, names),
-        out_shape=(piece,) * 2,
-        in_specs=[SMEM] * 3 + [VMEM] * 2 + [ANY] * (2 + len(arrays)),
-        out_specs=(VMEM,) * 2,
+        functools.partial(work_kernel, first, names),
+        out_shape=(piece,) * 2 + (jax.ShapeDtypeStruct((2, NM * N, 2 * N), jnp.bfloat16),) * first,
+        in_specs=[SMEM] * 3 + [VMEM if first else ANY] * 2 + [ANY] * 2 + [VMEM] * (not first) + [ANY] * len(arrays),
+        out_specs=(VMEM,) * (2 + first),
         scratch_shapes=[
             pltpu.SMEM((2, 8, N), jnp.float32),
             pltpu.SMEM((n,), jnp.int32),
             pltpu.VMEM((n, NM, N, N), jnp.float32),
             pltpu.VMEM((n, 2, N, N), jnp.float32),
-            pltpu.VMEM((2, NM * N, 2 * N), jnp.bfloat16),
             pltpu.VMEM((2 * N, N), jnp.float32),
             pltpu.SemaphoreType.DMA((n,)),
             pltpu.SemaphoreType.DMA((n,)),
             pltpu.SemaphoreType.DMA((n,)),
             pltpu.SemaphoreType.DMA((2,)),
         ],
-        compiler_params=pltpu.CompilerParams(vmem_limit_bytes=limit * 2**20),
+        compiler_params=pltpu.CompilerParams(vmem_limit_bytes=12 * 2**20),
         name="work",
-    )(pos, inverse, inverse_sib, side_own, side_sib, blocks, blocks_sib, *arrays)
+    )(pos, inverse, inverse_sib, side_own, side_sib, blocks, blocks_sib, *given, *arrays)
 
 
 def finish(batches, pos, inverse, pieces):
@@ -295,11 +301,11 @@
     left = jnp.where(live[:, None] & live[None, :], left_env[:, 0], 0.0).reshape(NM * N, N)
     side = jnp.concatenate([left, table], axis=0)
 
-    def run(batch):
+    def run(batch, lefts=None):
         inverse_sib = got["side_sib"][NM * N + NM, :NC * HALF].astype(jnp.int32)
         return work(
-            LIMITS[batch], BATCHES[batch], pos, inverse, inverse_sib, side, got["side_sib"],
-            wavefunction, got["blocks_sib"], got)
+            BATCHES[batch], pos, inverse, inverse_sib, side, got["side_sib"],
+            wavefunction, got["blocks_sib"], got, lefts)
 
     arrive(zf1=shift(own, "z", 1), zb1=shift(own, "z", -1))
     arrive(xf1=shift(own, "x", 1), xb1=shift(own, "x", -1))
@@ -321,7 +327,8 @@
         k2f=by_core(pick(jnp.stack([k1f[0], k1f[1], x2]), jnp.stack([zf2, zb2, k1f[0]])), 1),
         k2b=by_core(pick(jnp.stack([k1b[0], k1b[1], x2]), jnp.stack([zf2, zb2, k1b[1]])), -1),
     )
-    a = got["a"] = run(0)
+    *a, lefts = run(0)
+    got["a"] = a
     tie("zf3", "zb3", "a")
     zf3, zb3 = got["zf3"], got["zb3"]
     arrive(z4=by_core_far(pick(zf3, zb3), "z"))
@@ -334,18 +341,18 @@
         k3b=by_core(pick(k2b, jnp.stack([zf3, k2b[1], zb3])), -1),
     )
     a = halve(a)
-    b = got["b"] = run(1)
+    b = got["b"] = run(1, lefts)
     tie("df1", "db1", "k3f", "k3b", "b")
 
     k3f, k3b = got["k3f"], got["k3b"]
     arrive(d2=shift(got["df1"], "x", 1))
     arrive(k4f=by_core(k3f[2], 1), k4b=by_core(k3b[2], -1))
-    d = got["d"] = run(2)
+    d = got["d"] = run(2, lefts)
     b = halve(b)
     a = quarter(a)
     tie("d2", "k4f", "k4b", "d")
 
-    e = run(3)
+    e = run(3, lefts)
     d = halve(got["d"])
     b, d, e = fence((b, d, e))
 

time: 121 us -> 121 us (level)
  transfers between devices with their start and end apart: 33 -> 33, of which waited for: 14 -> 15; matrix products, arithmetic and copies ran while one was open for 6% -> 6% of each run, Pallas kernels for 20% -> 20%
where the time goes in v6:
time: 121 us
  starting transfers between devices  48 us (40%)
  waiting for transfers between devices  37.6 us (31%)
  Pallas kernels  25.8 us (21%)
  other arithmetic  7.83 us (6%)
    pallas_call x4, Pallas kernels, work(): pl.pallas_call(functools.partial(work_kernel, first, names), out_shape=(p...  24 us
    ppermute x15, starting transfers between devices, shift(): lax.ppermute(array, axis, [(i, (i + step) % size) for i in range(size)])  22.9 us
    ppermute x15, waiting for transfers between devices, shift(): lax.ppermute(array, axis, [(i, (i + step) % size) for i in range(size)])  22.5 us
    ppermute x8, starting transfers between devices, by_core(): return lax.ppermute(array, TENSOR, pairs)  10.4 us
    ppermute x3, starting transfers between devices, halve(): return keep + lax.ppermute(send, ('m', 'c'), hops(1, 3))  7.45 us
    ppermute x3, waiting for transfers between devices, quarter(): got = lax.ppermute(sums[1], ('m', 'c'), hops(3, 1))  5.89 us
    ppermute x3, waiting for transfers between devices, halve(): return keep + lax.ppermute(send, ('m', 'c'), hops(1, 3))  3.29 us
    ppermute x1, starting transfers between devices, direct(): one = lax.ppermute(send[0], ('m', 'c'), hops(1, 3))  2.98 us
  transfers between devices with their start and end apart: 33, of which 15 were waited for; matrix products, arithmetic and copies ran while one was open for 6% of the time, Pallas kernels for 20%

profile of v6, /device:TPU:1, one launch (start us, length us, event | category | flops | bytes accessed | tf_op | source)
XLA Modules:
  0.0 120.6 jit_solution(1637861387050898426)
XLA Ops:
  0.0 3.2 %collective-permute-start.4 = (f32[64,128,128]{2,1,0:T(8,128)}, f32[64,128,128]{2,1,0:T(8,128)}, u32[]{:S(2)}, u32[]{:S(2)}) collective-permute-start(f32[64,128,128]{2,1,0:T(8,128)} %blocks.7), channel_id=1, source_target_pairs={{0,1},{1,0},{2,3},{3,2},{4,5},{5,4},{6,7},{7,6},{8,9},{9,8},{10,11... | collective-permute-start | bytes 12582920 | tf_op jit(solution)/shard_map/ppermute | solution.py:221
  6.5 4.9 %collective-permute-start.1 = (f32[4,128,128]{2,1,0:T(8,128)S(1)}, f32[4,128,128]{2,1,0:T(8,128)S(1)}, u32[]{:S(2)}, u32[]{:S(2)}) collective-permute-start(f32[4,128,128]{2,1,0:T(8,128)S(1)} %bitcast_select_fusion.1.rest_0_), channel_id=1, source_target_pairs={{0,14},{2,0},{4,2},{6,4},{8,6},{10,8},{12,10},{14,12},{1,15},{3,1}... | collective-permute-start | bytes 786440 | tf_op jit(solution)/shard_map/ppermute | solution.py:221
  16.8 3.2 %collective-permute-done.rest_1_ = f32[4,128,128]{2,1,0:T(8,128)} collective-permute-done((f32[4,128,128]{2,1,0:T(8,128)S(1)}, f32[4,128,128]{2,1,0:T(8,128)}, u32[]{:S(2)}, u32[]{:S(2)}) %collective-permute-start) | collective-permute-done | bytes 262176 | tf_op jit(solution)/shard_map/ppermute | solution.py:221
  21.4 1.8 %maximum_select_fusion.2 = f32[2,4,128,128]{3,2,1,0:T(8,128)} fusion(f32[1,4,128,128]{3,2,1,0:T(8,128)S(1)} %bitcast.87, f32[1,4,128,128]{3,2,1,0:T(8,128)S(1)} %bitcast.88, f32[1,4,128,128]{3,2,1,0:T(8,128)S(1)} %bitcast.89, f32[1,4,128,128]{3,2,1,0:T(8,128)} %bitcast.13, pred[]{:T(512)S(6)} %eq.46), kind=kLoop, calls=%fused_computation.7 | loop fusion | flops 393216 | bytes 1572865 | tf_op jit(solution)/shard_map/jit(_where)/select_n | solution.py:280
  23.2 2.7 %collective-permute-start.10 = (f32[2,4,128,128]{3,2,1,0:T(8,128)}, f32[2,4,128,128]{3,2,1,0:T(8,128)S(1)}, u32[]{:S(2)}, u32[]{:S(2)}) collective-permute-start(f32[2,4,128,128]{3,2,1,0:T(8,128)} %maximum_select_fusion.2), channel_id=1, source_target_pairs={{0,14},{1,49},{2,0},{3,51},{4,2},{5,53},{6,4},{7,55},{8,6},{9,57},... | collective-permute-start | bytes 1572872 | tf_op jit(solution)/shard_map/ppermute | solution.py:233
  25.9 2.7 %collective-permute-start.7 = (f32[4,128,128]{2,1,0:T(8,128)S(1)}, f32[4,128,128]{2,1,0:T(8,128)S(1)}, u32[]{:S(2)}, u32[]{:S(2)}) collective-permute-start(f32[4,128,128]{2,1,0:T(8,128)S(1)} %collective-permute-done.1.rest_2_), channel_id=1, source_target_pairs={{0,14},{2,0},{4,2},{6,4},{8,6},{10,8},{12,10},{14,12},{1,15},{3,1}... | collective-permute-start | bytes 786440 | tf_op jit(solution)/shard_map/ppermute | solution.py:221
  28.6 2.7 %collective-permute-start.8 = (f32[4,128,128]{2,1,0:T(8,128)S(1)}, f32[4,128,128]{2,1,0:T(8,128)S(1)}, u32[]{:S(2)}, u32[]{:S(2)}) collective-permute-start(f32[4,128,128]{2,1,0:T(8,128)S(1)} %collective-permute-done.3.rest_4_), channel_id=1, source_target_pairs={{0,48},{16,0},{32,16},{48,32},{1,49},{17,1},{33,17},{49,33},{2,50}... | collective-permute-start | bytes 786440 | tf_op jit(solution)/shard_map/ppermute | solution.py:221
  31.3 4.5 %collective-permute-done.6.rest_5_ = f32[4,128,128]{2,1,0:T(8,128)S(1)} collective-permute-done((f32[4,128,128]{2,1,0:T(8,128)}, f32[4,128,128]{2,1,0:T(8,128)S(1)}, u32[]{:S(2)}, u32[]{:S(2)}) %collective-permute-start.6) | collective-permute-done | bytes 262176 | tf_op jit(solution)/shard_map/ppermute | solution.py:221
  35.8 2.1 %collective-permute-done.8.rest_7_ = f32[4,128,128]{2,1,0:T(8,128)S(1)} collective-permute-done((f32[4,128,128]{2,1,0:T(8,128)S(1)}, f32[4,128,128]{2,1,0:T(8,128)S(1)}, u32[]{:S(2)}, u32[]{:S(2)}) %collective-permute-start.8) | collective-permute-done | bytes 262176 | tf_op jit(solution)/shard_map/ppermute | solution.py:221
  38.0 2.7 %collective-permute-start.14 = (f32[4,128,128]{2,1,0:T(8,128)S(1)}, f32[4,128,128]{2,1,0:T(8,128)S(1)}, u32[]{:S(2)}, u32[]{:S(2)}) collective-permute-start(f32[4,128,128]{2,1,0:T(8,128)S(1)} %collective-permute-done.7.rest_6_), channel_id=1, source_target_pairs={{0,14},{2,0},{4,2},{6,4},{8,6},{10,8},{12,10},{14,12},{1,15},{3,1}... | collective-permute-start | bytes 786440 | tf_op jit(solution)/shard_map/ppermute | solution.py:221
  40.8 3.5 %collective-permute-start.16 = (f32[3,4,128,128]{3,2,1,0:T(8,128)S(1)}, f32[3,4,128,128]{3,2,1,0:T(8,128)S(1)}, u32[]{:S(2)}, u32[]{:S(2)}) collective-permute-start(f32[3,4,128,128]{3,2,1,0:T(8,128)S(1)} %get-tuple-element.109), channel_id=1, source_target_pairs={{0,14},{1,49},{2,0},{3,51},{4,2},{5,53},{6,4},{7,55},{8,6},{9,57},... | collective-permute-start | bytes 2359304 | tf_op jit(solution)/shard_map/ppermute | solution.py:233
  44.5 8.7 %work.4 = (f32[2,2,12,32,128]{4,3,2,1,0:T(8,128)S(1)}, f32[2,2,12,32,128]{4,3,2,1,0:T(8,128)S(1)}, bf16[2,512,256]{2,1,0:T(8,128)(2,1)S(1)}) custom-call(s32[4]{0:T(128)S(1)} %pad_add_fusion.pos, s32[64]{0:T(128)S(1)} %select_reduce_fusion.2.inverse, s32[64]{0:T(128)S(1)} %convert_bitcast_fusion.inverse_sib, f32[520,128]{1,0:T(8,128)S(1)} %pad_maximum_fusion.4.side_own, ...), custom_call_target="tpu_custom_call" | custom-call | tf_op jit(solution)/shard_map/work/pallas_call | solution.py:187
  53.3 2.8 %collective-permute-start.11 = (f32[2,2,12,32,128]{4,3,2,1,0:T(8,128)S(1)}, f32[2,2,12,32,128]{4,3,2,1,0:T(8,128)S(1)}, u32[]{:S(2)}, u32[]{:S(2)}) collective-permute-start(f32[2,2,12,32,128]{4,3,2,1,0:T(8,128)S(1)} %get-tuple-element.71), channel_id=1, source_target_pairs={{0,64},{1,193},{64,0},{65,129},{128,192},{129,65},{192,128},{193,1... | collective-permute-start | bytes 2359304 | tf_op jit(solution)/shard_map/ppermute | solution.py:256
  56.1 2.7 %collective-permute-done.17.rest_3_ = f32[4,128,128]{2,1,0:T(8,128)S(1)} collective-permute-done((f32[4,128,128]{2,1,0:T(8,128)S(1)}, f32[4,128,128]{2,1,0:T(8,128)S(1)}, u32[]{:S(2)}, u32[]{:S(2)}) %collective-permute-start.17) | collective-permute-done | bytes 262176 | tf_op jit(solution)/shard_map/ppermute | solution.py:243
  59.0 2.8 %collective-permute-start.22 = (f32[3,4,128,128]{3,2,1,0:T(8,128)S(1)}, f32[3,4,128,128]{3,2,1,0:T(8,128)S(1)}, u32[]{:S(2)}, u32[]{:S(2)}) collective-permute-start(f32[3,4,128,128]{3,2,1,0:T(8,128)S(1)} %get-tuple-element.111), channel_id=1, source_target_pairs={{0,14},{1,49},{2,0},{3,51},{4,2},{5,53},{6,4},{7,55},{8,6},{9,57},... | collective-permute-start | bytes 2359304 | tf_op jit(solution)/shard_map/ppermute | solution.py:233
  61.8 2.7 %collective-permute-start.20 = (f32[4,128,128]{2,1,0:T(8,128)S(1)}, f32[4,128,128]{2,1,0:T(8,128)S(1)}, u32[]{:S(2)}, u32[]{:S(2)}) collective-permute-start(f32[4,128,128]{2,1,0:T(8,128)S(1)} %collective-permute-done.17.rest_3_), channel_id=1, source_target_pairs={{0,48},{16,0},{32,16},{48,32},{1,49},{17,1},{33,17},{49,33},{2,50}... | collective-permute-start | bytes 786440 | tf_op jit(solution)/shard_map/ppermute | solution.py:221
  64.5 6.4 %work.5 = (f32[2,2,9,32,128]{4,3,2,1,0:T(8,128)S(1)}, f32[2,2,9,32,128]{4,3,2,1,0:T(8,128)S(1)}) custom-call(s32[4]{0:T(128)S(1)} %pad_add_fusion.pos, s32[64]{0:T(128)S(1)} %select_reduce_fusion.2.inverse, s32[64]{0:T(128)S(1)} %convert_bitcast_fusion.inverse_sib, f32[520,128]{1,0:T(8,128)S(1)} %pad_maximum_fusion.4.side_own, ...), custom_call_target="tpu_custom_call" | custom-call | tf_op jit(solution)/shard_map/work/pallas_call | solution.py:187
  71.0 5.3 %collective-permute-done.20.rest_4_ = f32[4,128,128]{2,1,0:T(8,128)S(1)} collective-permute-done((f32[4,128,128]{2,1,0:T(8,128)S(1)}, f32[4,128,128]{2,1,0:T(8,128)S(1)}, u32[]{:S(2)}, u32[]{:S(2)}) %collective-permute-start.20) | collective-permute-done | bytes 262176 | tf_op jit(solution)/shard_map/ppermute | solution.py:221
  76.3 3.1 %collective-permute-done.19.rest_3_ = f32[4,128,128]{2,1,0:T(8,128)S(1)} collective-permute-done((f32[4,128,128]{2,1,0:T(8,128)S(1)}, f32[4,128,128]{2,1,0:T(8,128)S(1)}, u32[]{:S(2)}, u32[]{:S(2)}) %collective-permute-start.19) | collective-permute-done | bytes 262176 | tf_op jit(solution)/shard_map/ppermute | solution.py:221
  79.6 1.5 %collective-permute-start.24 = (f32[4,128,128]{2,1,0:T(8,128)S(1)}, f32[4,128,128]{2,1,0:T(8,128)S(1)}, u32[]{:S(2)}, u32[]{:S(2)}) collective-permute-start(f32[4,128,128]{2,1,0:T(8,128)S(1)} %slice_bitcast_fusion.4), channel_id=1, source_target_pairs={{0,2},{1,17},{2,4},{3,19},{4,6},{5,21},{6,8},{7,23},{8,10},{9,25},... | collective-permute-start | bytes 786440 | tf_op jit(solution)/shard_map/ppermute | solution.py:233
  82.5 1.9 %collective-permute-start.18 = (f32[2,2,9,32,128]{4,3,2,1,0:T(8,128)S(1)}, f32[2,2,9,32,128]{4,3,2,1,0:T(8,128)S(1)}, u32[]{:S(2)}, u32[]{:S(2)}) collective-permute-start(f32[2,2,9,32,128]{4,3,2,1,0:T(8,128)S(1)} %get-tuple-element.79), channel_id=1, source_target_pairs={{0,64},{1,193},{64,0},{65,129},{128,192},{129,65},{192,128},{193,1... | collective-permute-start | bytes 1769480 | tf_op jit(solution)/shard_map/ppermute | solution.py:256
  84.4 5.8 %work.6 = (f32[2,2,8,32,128]{4,3,2,1,0:T(8,128)S(1)}, f32[2,2,8,32,128]{4,3,2,1,0:T(8,128)S(1)}) custom-call(s32[4]{0:T(128)S(1)} %pad_add_fusion.pos, s32[64]{0:T(128)S(1)} %select_reduce_fusion.2.inverse, s32[64]{0:T(128)S(1)} %convert_bitcast_fusion.inverse_sib, f32[520,128]{1,0:T(8,128)S(1)} %pad_maximum_fusion.4.side_own, ...), custom_call_target="tpu_custom_call" | custom-call | tf_op jit(solution)/shard_map/work/pallas_call | solution.py:187
  90.3 1.5 %collective-permute-done.23.rest_3_ = f32[4,128,128]{2,1,0:T(8,128)S(1)} collective-permute-done((f32[4,128,128]{2,1,0:T(8,128)S(1)}, f32[4,128,128]{2,1,0:T(8,128)S(1)}, u32[]{:S(2)}, u32[]{:S(2)}) %collective-permute-start.23) | collective-permute-done | bytes 262176 | tf_op jit(solution)/shard_map/ppermute | solution.py:221
  91.7 2.7 %collective-permute-start.26 = (f32[2,2,8,32,128]{4,3,2,1,0:T(8,128)S(1)}, f32[2,2,8,32,128]{4,3,2,1,0:T(8,128)S(1)}, u32[]{:S(2)}, u32[]{:S(2)}) collective-permute-start(f32[2,2,8,32,128]{4,3,2,1,0:T(8,128)S(1)} %get-tuple-element.87), channel_id=1, source_target_pairs={{0,64},{1,193},{64,0},{65,129},{128,192},{129,65},{192,128},{193,1... | collective-permute-start | bytes 1572872 | tf_op jit(solution)/shard_map/ppermute | solution.py:256
  94.7 3.1 %work.7 = (f32[2,2,3,32,128]{4,3,2,1,0:T(8,128)S(1)}, f32[2,2,3,32,128]{4,3,2,1,0:T(8,128)S(1)}) custom-call(s32[4]{0:T(128)S(1)} %pad_add_fusion.pos, s32[64]{0:T(128)S(1)} %select_reduce_fusion.2.inverse, s32[64]{0:T(128)S(1)} %convert_bitcast_fusion.inverse_sib, f32[520,128]{1,0:T(8,128)S(1)} %pad_maximum_fusion.4.side_own, ...), custom_call_target="tpu_custom_call" | custom-call | tf_op jit(solution)/shard_map/work/pallas_call | solution.py:187
  97.8 3.2 %collective-permute-done.26 = f32[2,2,8,32,128]{4,3,2,1,0:T(8,128)S(1)} collective-permute-done((f32[2,2,8,32,128]{4,3,2,1,0:T(8,128)S(1)}, f32[2,2,8,32,128]{4,3,2,1,0:T(8,128)S(1)}, u32[]{:S(2)}, u32[]{:S(2)}) %collective-permute-start.26) | collective-permute-done | bytes 524320 | tf_op jit(solution)/shard_map/ppermute | solution.py:256
  101.2 3.0 %collective-permute-start.29 = (f32[2,3,32,128]{3,2,1,0:T(8,128)S(1)}, f32[2,3,32,128]{3,2,1,0:T(8,128)S(1)}, u32[]{:S(2)}, u32[]{:S(2)}) collective-permute-start(f32[2,3,32,128]{3,2,1,0:T(8,128)S(1)} %get-tuple-element.114), channel_id=1, source_target_pairs={{0,64},{1,193},{64,0},{65,129},{128,192},{129,65},{192,128},{193,1... | collective-permute-start | bytes 294920 | tf_op jit(solution)/shard_map/ppermute | solution.py:266
  108.1 2.1 %collective-permute-done.30 = f32[2,3,32,128]{3,2,1,0:T(8,128)S(1)} collective-permute-done((f32[2,3,32,128]{3,2,1,0:T(8,128)S(1)}, f32[2,3,32,128]{3,2,1,0:T(8,128)S(1)}, u32[]{:S(2)}, u32[]{:S(2)}) %collective-permute-start.30) | collective-permute-done | bytes 98336 | tf_op jit(solution)/shard_map/ppermute | solution.py:267
  110.2 2.8 %collective-permute-done.28 = f32[2,8,32,128]{3,2,1,0:T(8,128)S(1)} collective-permute-done((f32[2,8,32,128]{3,2,1,0:T(8,128)S(1)}, f32[2,8,32,128]{3,2,1,0:T(8,128)S(1)}, u32[]{:S(2)}, u32[]{:S(2)}) %collective-permute-start.28) | collective-permute-done | bytes 262176 | tf_op jit(solution)/shard_map/ppermute | solution.py:260
  113.0 3.1 %collective-permute-done.27 = f32[2,9,32,128]{3,2,1,0:T(8,128)S(1)} collective-permute-done((f32[2,9,32,128]{3,2,1,0:T(8,128)S(1)}, f32[2,9,32,128]{3,2,1,0:T(8,128)S(1)}, u32[]{:S(2)}, u32[]{:S(2)}) %collective-permute-start.27) | collective-permute-done | bytes 294944 | tf_op jit(solution)/shard_map/ppermute | solution.py:260
  117.3 1.5 %collective-permute-done.32.rest_8_ = f32[32,32,128]{2,1,0:T(8,128)S(1)} collective-permute-done((f32[32,32,128]{2,1,0:T(8,128)S(1)}, f32[32,32,128]{2,1,0:T(8,128)S(1)}, u32[]{:S(2)}, u32[]{:S(2)}) %collective-permute-start.32) | collective-permute-done | bytes 524320 | tf_op jit(solution)/shard_map/ppermute | solution.py:221
  118.8 1.8 %finish.1 = f32[64,32,128]{2,1,0:T(8,128)} custom-call(s32[4]{0:T(128)S(1)} %pad_add_fusion.pos, s32[64]{0:T(128)S(1)} %select_reduce_fusion.2.inverse, f32[12,32,128]{2,1,0:T(8,128)S(1)} %slice_bitcast_fusion.8.rest_0_, f32[12,32,128]{2,1,0:T(8,128)S(1)} %slice_bitcast_fusion.7.rest_1_, f32[9,32,128]{2,1,0:T(8,128)S(1)} %slice_bitcast_fusion.11.rest_2_, ...), custom_call_target="tpu_custom_call" | custom-call | tf_op jit(solution)/shard_map/finish/pallas_call | solution.py:209
  (103 shorter events, 17.2 us)
Async XLA Ops:
  0.0 20.0 %collective-permute-start.4 = (f32[64,128,128]{2,1,0:T(8,128)}, f32[64,128,128]{2,1,0:T(8,128)}, u32[]{:S(2)}, u32[]{:S(2)}) collective-permute-start(f32[64,128,128]{2,1,0:T(8,128)} %blocks.7), channel_id=1, source_target_pairs={{0,1},{1,0},{2,3},{3,2},{4,5},{5,4},{6,7},{7,6},{8,9},{9,8},{10,11... | collective-permute-start | bytes 12582920 | tf_op jit(solution)/shard_map/ppermute | solution.py:221
  5.0 10.5 %collective-permute-start.3 = (f32[4,128,128]{2,1,0:T(8,128)S(1)}, f32[4,128,128]{2,1,0:T(8,128)S(1)}, u32[]{:S(2)}, u32[]{:S(2)}) collective-permute-start(f32[4,128,128]{2,1,0:T(8,128)S(1)} %bitcast_select_fusion.1.rest_0_), channel_id=1, source_target_pairs={{0,48},{16,0},{32,16},{48,32},{1,49},{17,1},{33,17},{49,33},{2,50}... | collective-permute-start | bytes 786440 | tf_op jit(solution)/shard_map/ppermute | solution.py:221
  5.8 9.7 %collective-permute-start.2 = (f32[4,128,128]{2,1,0:T(8,128)S(1)}, f32[4,128,128]{2,1,0:T(8,128)S(1)}, u32[]{:S(2)}, u32[]{:S(2)}) collective-permute-start(f32[4,128,128]{2,1,0:T(8,128)S(1)} %bitcast_select_fusion.1.rest_0_), channel_id=1, source_target_pairs={{0,16},{16,32},{32,48},{48,0},{1,17},{17,33},{33,49},{49,1},{2,18}... | collective-permute-start | bytes 786440 | tf_op jit(solution)/shard_map/ppermute | solution.py:221
  6.5 10.3 %collective-permute-start.1 = (f32[4,128,128]{2,1,0:T(8,128)S(1)}, f32[4,128,128]{2,1,0:T(8,128)S(1)}, u32[]{:S(2)}, u32[]{:S(2)}) collective-permute-start(f32[4,128,128]{2,1,0:T(8,128)S(1)} %bitcast_select_fusion.1.rest_0_), channel_id=1, source_target_pairs={{0,14},{2,0},{4,2},{6,4},{8,6},{10,8},{12,10},{14,12},{1,15},{3,1}... | collective-permute-start | bytes 786440 | tf_op jit(solution)/shard_map/ppermute | solution.py:221
  11.4 8.6 %collective-permute-start = (f32[4,128,128]{2,1,0:T(8,128)S(1)}, f32[4,128,128]{2,1,0:T(8,128)}, u32[]{:S(2)}, u32[]{:S(2)}) collective-permute-start(f32[4,128,128]{2,1,0:T(8,128)S(1)} %bitcast_select_fusion.1.rest_0_), channel_id=1, source_target_pairs={{0,2},{2,4},{4,6},{6,8},{8,10},{10,12},{12,14},{14,0},{1,3},{3,5},... | collective-permute-start | bytes 786440 | tf_op jit(solution)/shard_map/ppermute | solution.py:221
  20.0 8.6 %collective-permute-start.5 = (f32[520,128]{1,0:T(8,128)S(1)}, f32[520,128]{1,0:T(8,128)S(1)}, u32[]{:S(2)}, u32[]{:S(2)}) collective-permute-start(f32[520,128]{1,0:T(8,128)S(1)} %pad_maximum_fusion.4.side_own), channel_id=1, source_target_pairs={{0,1},{1,0},{2,3},{3,2},{4,5},{5,4},{6,7},{7,6},{8,9},{9,8},{10,11... | collective-permute-start | bytes 798728 | tf_op jit(solution)/shard_map/ppermute | solution.py:221
  23.2 12.5 %collective-permute-start.10 = (f32[2,4,128,128]{3,2,1,0:T(8,128)}, f32[2,4,128,128]{3,2,1,0:T(8,128)S(1)}, u32[]{:S(2)}, u32[]{:S(2)}) collective-permute-start(f32[2,4,128,128]{3,2,1,0:T(8,128)} %maximum_select_fusion.2), channel_id=1, source_target_pairs={{0,14},{1,49},{2,0},{3,51},{4,2},{5,53},{6,4},{7,55},{8,6},{9,57},... | collective-permute-start | bytes 1572872 | tf_op jit(solution)/shard_map/ppermute | solution.py:233
  25.9 9.8 %collective-permute-start.9 = (f32[2,4,128,128]{3,2,1,0:T(8,128)}, f32[2,4,128,128]{3,2,1,0:T(8,128)S(1)}, u32[]{:S(2)}, u32[]{:S(2)}) collective-permute-start(f32[2,4,128,128]{3,2,1,0:T(8,128)} %maximum_select_fusion.2), channel_id=1, source_target_pairs={{0,2},{1,17},{2,4},{3,19},{4,6},{5,21},{6,8},{7,23},{8,10},{9,25},... | collective-permute-start | bytes 1572872 | tf_op jit(solution)/shard_map/ppermute | solution.py:233
  25.9 9.8 %collective-permute-start.6 = (f32[4,128,128]{2,1,0:T(8,128)}, f32[4,128,128]{2,1,0:T(8,128)S(1)}, u32[]{:S(2)}, u32[]{:S(2)}) collective-permute-start(f32[4,128,128]{2,1,0:T(8,128)} %collective-permute-done.rest_1_), channel_id=1, source_target_pairs={{0,2},{2,4},{4,6},{6,8},{8,10},{10,12},{12,14},{14,0},{1,3},{3,5},... | collective-permute-start | bytes 786440 | tf_op jit(solution)/shard_map/ppermute | solution.py:221
  25.9 9.8 %collective-permute-start.7 = (f32[4,128,128]{2,1,0:T(8,128)S(1)}, f32[4,128,128]{2,1,0:T(8,128)S(1)}, u32[]{:S(2)}, u32[]{:S(2)}) collective-permute-start(f32[4,128,128]{2,1,0:T(8,128)S(1)} %collective-permute-done.1.rest_2_), channel_id=1, source_target_pairs={{0,14},{2,0},{4,2},{6,4},{8,6},{10,8},{12,10},{14,12},{1,15},{3,1}... | collective-permute-start | bytes 786440 | tf_op jit(solution)/shard_map/ppermute | solution.py:221
  28.6 9.3 %collective-permute-start.8 = (f32[4,128,128]{2,1,0:T(8,128)S(1)}, f32[4,128,128]{2,1,0:T(8,128)S(1)}, u32[]{:S(2)}, u32[]{:S(2)}) collective-permute-start(f32[4,128,128]{2,1,0:T(8,128)S(1)} %collective-permute-done.3.rest_4_), channel_id=1, source_target_pairs={{0,48},{16,0},{32,16},{48,32},{1,49},{17,1},{33,17},{49,33},{2,50}... | collective-permute-start | bytes 786440 | tf_op jit(solution)/shard_map/ppermute | solution.py:221
  37.9 15.2 %collective-permute-start.13 = (f32[4,128,128]{2,1,0:T(8,128)S(1)}, f32[4,128,128]{2,1,0:T(8,128)S(1)}, u32[]{:S(2)}, u32[]{:S(2)}) collective-permute-start(f32[4,128,128]{2,1,0:T(8,128)S(1)} %collective-permute-done.6.rest_5_), channel_id=1, source_target_pairs={{0,2},{2,4},{4,6},{6,8},{8,10},{10,12},{12,14},{14,0},{1,3},{3,5},... | collective-permute-start | bytes 786440 | tf_op jit(solution)/shard_map/ppermute | solution.py:221
  38.0 15.1 %collective-permute-start.14 = (f32[4,128,128]{2,1,0:T(8,128)S(1)}, f32[4,128,128]{2,1,0:T(8,128)S(1)}, u32[]{:S(2)}, u32[]{:S(2)}) collective-permute-start(f32[4,128,128]{2,1,0:T(8,128)S(1)} %collective-permute-done.7.rest_6_), channel_id=1, source_target_pairs={{0,14},{2,0},{4,2},{6,4},{8,6},{10,8},{12,10},{14,12},{1,15},{3,1}... | collective-permute-start | bytes 786440 | tf_op jit(solution)/shard_map/ppermute | solution.py:221
  40.8 18.0 %collective-permute-start.16 = (f32[3,4,128,128]{3,2,1,0:T(8,128)S(1)}, f32[3,4,128,128]{3,2,1,0:T(8,128)S(1)}, u32[]{:S(2)}, u32[]{:S(2)}) collective-permute-start(f32[3,4,128,128]{3,2,1,0:T(8,128)S(1)} %get-tuple-element.109), channel_id=1, source_target_pairs={{0,14},{1,49},{2,0},{3,51},{4,2},{5,53},{6,4},{7,55},{8,6},{9,57},... | collective-permute-start | bytes 2359304 | tf_op jit(solution)/shard_map/ppermute | solution.py:233
  44.3 14.5 %collective-permute-start.15 = (f32[3,4,128,128]{3,2,1,0:T(8,128)S(1)}, f32[3,4,128,128]{3,2,1,0:T(8,128)S(1)}, u32[]{:S(2)}, u32[]{:S(2)}) collective-permute-start(f32[3,4,128,128]{3,2,1,0:T(8,128)S(1)} %get-tuple-element.110), channel_id=1, source_target_pairs={{0,2},{1,17},{2,4},{3,19},{4,6},{5,21},{6,8},{7,23},{8,10},{9,25},... | collective-permute-start | bytes 2359304 | tf_op jit(solution)/shard_map/ppermute | solution.py:233
  53.2 5.6 %collective-permute-start.17 = (f32[4,128,128]{2,1,0:T(8,128)S(1)}, f32[4,128,128]{2,1,0:T(8,128)S(1)}, u32[]{:S(2)}, u32[]{:S(2)}) collective-permute-start(f32[4,128,128]{2,1,0:T(8,128)S(1)} %broadcast_select_fusion), channel_id=1, source_target_pairs={{0,2},{1,15},{2,4},{3,1},{4,6},{5,3},{6,8},{7,5},{8,10},{9,7},{10,... | collective-permute-start | bytes 786440 | tf_op jit(solution)/shard_map/ppermute | solution.py:243
  53.3 17.6 %collective-permute-start.11 = (f32[2,2,12,32,128]{4,3,2,1,0:T(8,128)S(1)}, f32[2,2,12,32,128]{4,3,2,1,0:T(8,128)S(1)}, u32[]{:S(2)}, u32[]{:S(2)}) collective-permute-start(f32[2,2,12,32,128]{4,3,2,1,0:T(8,128)S(1)} %get-tuple-element.71), channel_id=1, source_target_pairs={{0,64},{1,193},{64,0},{65,129},{128,192},{129,65},{192,128},{193,1... | collective-permute-start | bytes 2359304 | tf_op jit(solution)/shard_map/ppermute | solution.py:256
  59.0 20.4 %collective-permute-start.22 = (f32[3,4,128,128]{3,2,1,0:T(8,128)S(1)}, f32[3,4,128,128]{3,2,1,0:T(8,128)S(1)}, u32[]{:S(2)}, u32[]{:S(2)}) collective-permute-start(f32[3,4,128,128]{3,2,1,0:T(8,128)S(1)} %get-tuple-element.111), channel_id=1, source_target_pairs={{0,14},{1,49},{2,0},{3,51},{4,2},{5,53},{6,4},{7,55},{8,6},{9,57},... | collective-permute-start | bytes 2359304 | tf_op jit(solution)/shard_map/ppermute | solution.py:233
  61.8 17.7 %collective-permute-start.21 = (f32[3,4,128,128]{3,2,1,0:T(8,128)S(1)}, f32[3,4,128,128]{3,2,1,0:T(8,128)S(1)}, u32[]{:S(2)}, u32[]{:S(2)}) collective-permute-start(f32[3,4,128,128]{3,2,1,0:T(8,128)S(1)} %get-tuple-element.112), channel_id=1, source_target_pairs={{0,2},{1,17},{2,4},{3,19},{4,6},{5,21},{6,8},{7,23},{8,10},{9,25},... | collective-permute-start | bytes 2359304 | tf_op jit(solution)/shard_map/ppermute | solution.py:233
  61.8 14.5 %collective-permute-start.20 = (f32[4,128,128]{2,1,0:T(8,128)S(1)}, f32[4,128,128]{2,1,0:T(8,128)S(1)}, u32[]{:S(2)}, u32[]{:S(2)}) collective-permute-start(f32[4,128,128]{2,1,0:T(8,128)S(1)} %collective-permute-done.17.rest_3_), channel_id=1, source_target_pairs={{0,48},{16,0},{32,16},{48,32},{1,49},{17,1},{33,17},{49,33},{2,50}... | collective-permute-start | bytes 786440 | tf_op jit(solution)/shard_map/ppermute | solution.py:221
  64.5 15.0 %collective-permute-start.19 = (f32[4,128,128]{2,1,0:T(8,128)S(1)}, f32[4,128,128]{2,1,0:T(8,128)S(1)}, u32[]{:S(2)}, u32[]{:S(2)}) collective-permute-start(f32[4,128,128]{2,1,0:T(8,128)S(1)} %collective-permute-done.17.rest_3_), channel_id=1, source_target_pairs={{0,16},{16,32},{32,48},{48,0},{1,17},{17,33},{33,49},{49,1},{2,18}... | collective-permute-start | bytes 786440 | tf_op jit(solution)/shard_map/ppermute | solution.py:221
  79.5 10.7 %collective-permute-start.25 = (f32[4,128,128]{2,1,0:T(8,128)S(1)}, f32[4,128,128]{2,1,0:T(8,128)S(1)}, u32[]{:S(2)}, u32[]{:S(2)}) collective-permute-start(f32[4,128,128]{2,1,0:T(8,128)S(1)} %slice_bitcast_fusion.3), channel_id=1, source_target_pairs={{0,14},{1,49},{2,0},{3,51},{4,2},{5,53},{6,4},{7,55},{8,6},{9,57},... | collective-permute-start | bytes 786440 | tf_op jit(solution)/shard_map/ppermute | solution.py:233
  79.6 10.6 %collective-permute-start.24 = (f32[4,128,128]{2,1,0:T(8,128)S(1)}, f32[4,128,128]{2,1,0:T(8,128)S(1)}, u32[]{:S(2)}, u32[]{:S(2)}) collective-permute-start(f32[4,128,128]{2,1,0:T(8,128)S(1)} %slice_bitcast_fusion.4), channel_id=1, source_target_pairs={{0,2},{1,17},{2,4},{3,19},{4,6},{5,21},{6,8},{7,23},{8,10},{9,25},... | collective-permute-start | bytes 786440 | tf_op jit(solution)/shard_map/ppermute | solution.py:233
  81.1 10.7 %collective-permute-start.23 = (f32[4,128,128]{2,1,0:T(8,128)S(1)}, f32[4,128,128]{2,1,0:T(8,128)S(1)}, u32[]{:S(2)}, u32[]{:S(2)}) collective-permute-start(f32[4,128,128]{2,1,0:T(8,128)S(1)} %collective-permute-done.19.rest_3_), channel_id=1, source_target_pairs={{0,16},{16,32},{32,48},{48,0},{1,17},{17,33},{33,49},{49,1},{2,18}... | collective-permute-start | bytes 786440 | tf_op jit(solution)/shard_map/ppermute | solution.py:221
  81.1 13.4 %collective-permute-start.12 = (f32[2,12,32,128]{3,2,1,0:T(8,128)S(1)}, f32[2,12,32,128]{3,2,1,0:T(8,128)S(1)}, u32[]{:S(2)}, u32[]{:S(2)}) collective-permute-start(f32[2,12,32,128]{3,2,1,0:T(8,128)S(1)} %slice_bitcast_fusion), channel_id=1, source_target_pairs={{0,192},{1,65},{64,128},{65,1},{128,64},{129,193},{192,0},{193,129... | collective-permute-start | bytes 1179656 | tf_op jit(solution)/shard_map/ppermute | solution.py:260
  82.5 12.1 %collective-permute-start.18 = (f32[2,2,9,32,128]{4,3,2,1,0:T(8,128)S(1)}, f32[2,2,9,32,128]{4,3,2,1,0:T(8,128)S(1)}, u32[]{:S(2)}, u32[]{:S(2)}) collective-permute-start(f32[2,2,9,32,128]{4,3,2,1,0:T(8,128)S(1)} %get-tuple-element.79), channel_id=1, source_target_pairs={{0,64},{1,193},{64,0},{65,129},{128,192},{129,65},{192,128},{193,1... | collective-permute-start | bytes 1769480 | tf_op jit(solution)/shard_map/ppermute | solution.py:256
  91.7 9.3 %collective-permute-start.26 = (f32[2,2,8,32,128]{4,3,2,1,0:T(8,128)S(1)}, f32[2,2,8,32,128]{4,3,2,1,0:T(8,128)S(1)}, u32[]{:S(2)}, u32[]{:S(2)}) collective-permute-start(f32[2,2,8,32,128]{4,3,2,1,0:T(8,128)S(1)} %get-tuple-element.87), channel_id=1, source_target_pairs={{0,64},{1,193},{64,0},{65,129},{128,192},{129,65},{192,128},{193,1... | collective-permute-start | bytes 1572872 | tf_op jit(solution)/shard_map/ppermute | solution.py:256
  101.2 5.8 %collective-permute-start.29 = (f32[2,3,32,128]{3,2,1,0:T(8,128)S(1)}, f32[2,3,32,128]{3,2,1,0:T(8,128)S(1)}, u32[]{:S(2)}, u32[]{:S(2)}) collective-permute-start(f32[2,3,32,128]{3,2,1,0:T(8,128)S(1)} %get-tuple-element.114), channel_id=1, source_target_pairs={{0,64},{1,193},{64,0},{65,129},{128,192},{129,65},{192,128},{193,1... | collective-permute-start | bytes 294920 | tf_op jit(solution)/shard_map/ppermute | solution.py:266
  104.2 3.8 %collective-permute-start.31 = (f32[2,3,32,128]{3,2,1,0:T(8,128)S(1)}, f32[2,3,32,128]{3,2,1,0:T(8,128)S(1)}, u32[]{:S(2)}, u32[]{:S(2)}) collective-permute-start(f32[2,3,32,128]{3,2,1,0:T(8,128)S(1)} %slice_bitcast_fusion.15), channel_id=1, source_target_pairs={{0,192},{1,65},{64,128},{65,1},{128,64},{129,193},{192,0},{193,129... | collective-permute-start | bytes 294920 | tf_op jit(solution)/shard_map/ppermute | solution.py:268
  104.3 5.9 %collective-permute-start.30 = (f32[2,3,32,128]{3,2,1,0:T(8,128)S(1)}, f32[2,3,32,128]{3,2,1,0:T(8,128)S(1)}, u32[]{:S(2)}, u32[]{:S(2)}) collective-permute-start(f32[2,3,32,128]{3,2,1,0:T(8,128)S(1)} %get-tuple-element.113), channel_id=1, source_target_pairs={{0,128},{1,129},{64,192},{65,193},{128,0},{129,1},{192,64},{193,65... | collective-permute-start | bytes 294920 | tf_op jit(solution)/shard_map/ppermute | solution.py:267
  105.5 7.5 %collective-permute-start.28 = (f32[2,8,32,128]{3,2,1,0:T(8,128)S(1)}, f32[2,8,32,128]{3,2,1,0:T(8,128)S(1)}, u32[]{:S(2)}, u32[]{:S(2)}) collective-permute-start(f32[2,8,32,128]{3,2,1,0:T(8,128)S(1)} %slice_bitcast_fusion.2), channel_id=1, source_target_pairs={{0,192},{1,65},{64,128},{65,1},{128,64},{129,193},{192,0},{193,129... | collective-permute-start | bytes 786440 | tf_op jit(solution)/shard_map/ppermute | solution.py:260
  105.8 10.4 %collective-permute-start.27 = (f32[2,9,32,128]{3,2,1,0:T(8,128)S(1)}, f32[2,9,32,128]{3,2,1,0:T(8,128)S(1)}, u32[]{:S(2)}, u32[]{:S(2)}) collective-permute-start(f32[2,9,32,128]{3,2,1,0:T(8,128)S(1)} %slice_bitcast_fusion.1), channel_id=1, source_target_pairs={{0,192},{1,65},{64,128},{65,1},{128,64},{129,193},{192,0},{193,129... | collective-permute-start | bytes 884744 | tf_op jit(solution)/shard_map/ppermute | solution.py:260
  (10 other events, 168.9 us)
